TPU v7x, 32 devices: a whole 2x2x4 slice. The times are simulated.
32 devices in a mesh: member: 4 (over z), domain: 8 (over y, x, core).
Axes of the slice: x: 2, y: 2, z: 4, core: 2. Of those that a mesh axis runs over, the one named last changes fastest.
Arguments:
- perturbations: bfloat16 [100, 16, 2048], P('member', None, 'domain'), may hold values from -0.59765625 to 0.59765625
- innovations: float32 [16, 2048], P(None, 'domain'), may hold values from -6 to 6
- precision_field: float32 [16, 2048], P(None, 'domain'), may hold values from 0.2 to 4
- obs_counts: int32 [2048], P('domain'), may hold values from 1 to 8
- vertical_map: float32 [16, 16], replicated, may hold values from -1.5 to 1.5
- diffusivity: float32 [16], replicated, may hold values from 0.05 to 0.24
Outputs:
- control: float32 [100, 16, 2048], P('member', None, 'domain')
- increment: float32 [16, 2048], P(None, 'domain')
All inputs are finite; a program needn't handle non-finite values.
Results may differ from a plain program's by a relative error of at most 0.0003.
Values sent between devices are 32-bit elements; how exact they have to be, the bound alone decides.
No kernel may reach another device: no remote copies, remote signals or barrier semaphores. Data moves between devices by JAX's collectives and lax.ppermute only.
A program may use at most 64 MiB of HBM per device.

v0:
```python
import jax
import jax.numpy as jnp
from jax import lax
from jax.sharding import PartitionSpec as P

DIFF = 2
ITERS = 2


def extended(value, sides, width):
    for axis, dim in sides:
        size, length = (lax.axis_size(axis), value.shape[dim])
        up = [(i, (i + 1) % size) for i in range(size)]
        down = [(j, i) for i, j in up]
        last = lax.slice_in_dim(value, length - width, length, axis=dim)
        first = lax.slice_in_dim(value, 0, width, axis=dim)
        before = lax.ppermute(last, axis, up)
        after = lax.ppermute(first, axis, down)
        value = jnp.concatenate([before, value, after], axis=dim)
    return value


def diffuse(field, diffusivity):
    coef = diffusivity[None, :, None]
    for step in range(DIFF):
        padded = extended(field, (("domain", 2),), 1)
        field = field + coef * (padded[..., 2:] - 2.0 * field + padded[..., :-2])
    return field


def forward(field, vertical_map, diffusivity):
    mixed = jnp.einsum("lk,mkh->mlh", vertical_map, field, precision=lax.Precision.HIGHEST)
    return diffuse(mixed, diffusivity)


def adjoint(field, vertical_map, diffusivity):
    smooth = diffuse(field, diffusivity)
    return jnp.einsum("kl,mkh->mlh", vertical_map, smooth, precision=lax.Precision.HIGHEST)


def total_sum(value):
    return lax.psum(value, ("member", "domain"))


def local(perturbations, innovations, precision_field, obs_counts, vertical_map, diffusivity):
    members = perturbations.astype(jnp.float32)
    weight = obs_counts.astype(jnp.float32)[None, :] * precision_field

    def local_part(field):
        return jnp.sum(members * forward(field, vertical_map, diffusivity), axis=0)

    rhs = adjoint(members * (weight * innovations)[None], vertical_map, diffusivity)
    control = jnp.zeros_like(rhs)
    residual = rhs
    direction = rhs
    norm_now = total_sum(jnp.sum(residual * residual))
    for step in range(ITERS):
        partial_sum = local_part(direction)
        weighted = weight * lax.psum(partial_sum, "member")
        image = direction + adjoint(members * weighted[None], vertical_map, diffusivity)
        alpha = norm_now / lax.psum(jnp.sum(direction * image), ("member", "domain"))
        control = control + alpha * direction
        residual = residual - alpha * image
        norm_next = total_sum(jnp.sum(residual * residual))
        direction = residual + norm_next / norm_now * direction
        norm_now = norm_next
    increment = lax.psum(local_part(control), "member")
    return (control, increment)


def solution(mesh):
    in_specs = (
        P("member", None, "domain"),
        P(None, "domain"),
        P(None, "domain"),
        P("domain"),
        P(),
        P(),
    )
    out_specs = (P("member", None, "domain"), P(None, "domain"))
    return jax.shard_map(local, mesh=mesh, in_specs=in_specs, out_specs=out_specs, check_vma=False)
```

profile of v0, /device:TPU:0, one launch (start us, length us, event | category | flops | bytes accessed | tf_op | source)
XLA Modules:
  0.0 281.7 jit_solution(6978943742259423165)
XLA Ops:
  0.6 0.7 convert_element_type.7
  1.3 0.7 multiply_multiply_fusion.2
  2.1 1.0 convert_multiply_fusion.5
  3.2 3.4 %collective-permute-start = (f32[25,16,1]{2,1,0:T(8,128)S(1)}, f32[25,16,1]{2,1,0:T(8,128)S(1)}, u32[]{:S(2)}, u32[]{:S(2)}) collective-permute-start(f32[25,16,1]{2,1,0:T(8,128)S(1)} %get-tuple-element.28), channel_id=1, source_target_pairs={{1,0},{2,1},{3,2},{4,3},{5,4},{6,5},{7,6},{0,7},{9,8},{10,9},{11,1... | collective-permute-start | bytes 4808 | tf_op jit(solution)/shard_map/ppermute | solution.py:18
  6.6 4.6 %collective-permute-done = f32[25,16,1]{2,1,0:T(8,128)S(1)} collective-permute-done((f32[25,16,1]{2,1,0:T(8,128)S(1)}, f32[25,16,1]{2,1,0:T(8,128)S(1)}, u32[]{:S(2)}, u32[]{:S(2)}) %collective-permute-start) | collective-permute-done | bytes 1632 | tf_op jit(solution)/shard_map/ppermute | solution.py:18
  11.1 1.9 collective-permute-done.1
  13.5 0.9 collective-permute-start.2
  14.5 4.4 %collective-permute-done.2 = f32[25,16,1]{2,1,0:T(8,128)S(1)} collective-permute-done((f32[25,16,1]{2,1,0:T(8,128)S(1)}, f32[25,16,1]{2,1,0:T(8,128)S(1)}, u32[]{:S(2)}, u32[]{:S(2)}) %collective-permute-start.2) | collective-permute-done | bytes 1632 | tf_op jit(solution)/shard_map/ppermute | solution.py:18
  18.9 2.0 collective-permute-done.3
  20.9 0.8 convolution_bitcast_fusion.5
  22.3 0.8 collective-permute-start.4
  23.1 4.5 %collective-permute-done.4 = f32[25,16,1]{2,1,0:T(8,128)S(1)} collective-permute-done((f32[25,16,1]{2,1,0:T(8,128)S(1)}, f32[25,16,1]{2,1,0:T(8,128)S(1)}, u32[]{:S(2)}, u32[]{:S(2)}) %collective-permute-start.4) | collective-permute-done | bytes 1632 | tf_op jit(solution)/shard_map/ppermute | solution.py:18
  27.6 1.6 collective-permute-done.5
  29.7 1.3 collective-permute-start.6
  31.0 4.0 %collective-permute-done.6 = f32[25,16,1]{2,1,0:T(8,128)S(1)} collective-permute-done((f32[25,16,1]{2,1,0:T(8,128)S(1)}, f32[25,16,1]{2,1,0:T(8,128)S(1)}, u32[]{:S(2)}, u32[]{:S(2)}) %collective-permute-start.6) | collective-permute-done | bytes 1632 | tf_op jit(solution)/shard_map/ppermute | solution.py:18
  35.0 2.0 collective-permute-done.7
  37.4 19.0 %psum.50 = f32[16,256]{1,0:T(8,128)S(1)} all-reduce(f32[16,256]{1,0:T(8,128)S(1)} %fusion.4), channel_id=1, replica_groups=mesh['member'=4,'domain'=8] {'member'}, use_global_device_ids=true, to_apply=%region_3.0 | all-reduce | flops 4096 | bytes 32768 | tf_op jit(solution)/shard_map/psum | solution.py:59
  56.7 0.5 collective-permute-start.9
  57.1 4.8 %collective-permute-done.8 = f32[25,16,1]{2,1,0:T(8,128)S(1)} collective-permute-done((f32[25,16,1]{2,1,0:T(8,128)S(1)}, f32[25,16,1]{2,1,0:T(8,128)S(1)}, u32[]{:S(2)}, u32[]{:S(2)}) %collective-permute-start.8) | collective-permute-done | bytes 1632 | tf_op jit(solution)/shard_map/ppermute | solution.py:18
  61.9 1.3 collective-permute-done.9
  63.7 1.5 collective-permute-start.10
  65.3 4.4 %collective-permute-done.10 = f32[25,16,1]{2,1,0:T(8,128)S(1)} collective-permute-done((f32[25,16,1]{2,1,0:T(8,128)S(1)}, f32[25,16,1]{2,1,0:T(8,128)S(1)}, u32[]{:S(2)}, u32[]{:S(2)}) %collective-permute-start.10) | collective-permute-done | bytes 1632 | tf_op jit(solution)/shard_map/ppermute | solution.py:18
  69.7 1.6 collective-permute-done.11
  71.3 1.4 multiply_reduce_fusion.1
  72.8 37.1 %all-reduce = (f32[]{:T(128)}, f32[]{:T(128)}) all-reduce(f32[]{:T(128)} %get-tuple-element.3, f32[]{:T(128)} %get-tuple-element.2), channel_id=1, replica_groups=mesh['member'=4,'domain'=8] {'member','domain'}, use_global_device_ids=true, to_apply=%region_1.0 | all-reduce | flops 2 | bytes 16 | tf_op jit(solution)/shard_map/psum | solution.py:42
  111.2 0.7 multiply_reduce_fusion
  112.0 42.3 %psum.52 = f32[]{:T(128)} all-reduce(f32[]{:T(128)} %multiply_reduce_fusion), channel_id=1, replica_groups=mesh['member'=4,'domain'=8] {'member','domain'}, use_global_device_ids=true, to_apply=%region_7.0 | all-reduce | flops 1 | bytes 8 | tf_op jit(solution)/shard_map/psum | solution.py:42
  155.6 0.5 convolution_bitcast_fusion.2
  156.3 1.1 collective-permute-start.12
  157.5 4.8 %collective-permute-done.12 = f32[25,16,1]{2,1,0:T(8,128)S(1)} collective-permute-done((f32[25,16,1]{2,1,0:T(8,128)S(1)}, f32[25,16,1]{2,1,0:T(8,128)S(1)}, u32[]{:S(2)}, u32[]{:S(2)}) %collective-permute-start.12) | collective-permute-done | bytes 1632 | tf_op jit(solution)/shard_map/ppermute | solution.py:18
  162.3 2.8 collective-permute-done.13
  166.1 4.8 %collective-permute-done.14 = f32[25,16,1]{2,1,0:T(8,128)S(1)} collective-permute-done((f32[25,16,1]{2,1,0:T(8,128)S(1)}, f32[25,16,1]{2,1,0:T(8,128)S(1)}, u32[]{:S(2)}, u32[]{:S(2)}) %collective-permute-start.14) | collective-permute-done | bytes 1632 | tf_op jit(solution)/shard_map/ppermute | solution.py:18
  170.9 1.8 collective-permute-done.15
  173.0 16.9 %psum.53 = f32[16,256]{1,0:T(8,128)S(1)} all-reduce(f32[16,256]{1,0:T(8,128)S(1)} %fusion.5), channel_id=1, replica_groups=mesh['member'=4,'domain'=8] {'member'}, use_global_device_ids=true, to_apply=%region_9.0 | all-reduce | flops 4096 | bytes 32768 | tf_op jit(solution)/shard_map/psum | solution.py:59
  190.2 0.5 collective-permute-start.17
  190.7 5.0 %collective-permute-done.16 = f32[25,16,1]{2,1,0:T(8,128)S(1)} collective-permute-done((f32[25,16,1]{2,1,0:T(8,128)S(1)}, f32[25,16,1]{2,1,0:T(8,128)S(1)}, u32[]{:S(2)}, u32[]{:S(2)}) %collective-permute-start.16) | collective-permute-done | bytes 1632 | tf_op jit(solution)/shard_map/ppermute | solution.py:18
  195.7 1.5 collective-permute-done.17
  197.6 1.4 collective-permute-start.18
  199.0 4.6 %collective-permute-done.18 = f32[25,16,1]{2,1,0:T(8,128)S(1)} collective-permute-done((f32[25,16,1]{2,1,0:T(8,128)S(1)}, f32[25,16,1]{2,1,0:T(8,128)S(1)}, u32[]{:S(2)}, u32[]{:S(2)}) %collective-permute-start.18) | collective-permute-done | bytes 1632 | tf_op jit(solution)/shard_map/ppermute | solution.py:18
  203.6 1.5 collective-permute-done.19
  205.1 1.4 fusion.3
  206.5 37.3 %psum.54 = f32[]{:T(128)} all-reduce(f32[]{:T(128)} %fusion.3), channel_id=1, replica_groups=mesh['member'=4,'domain'=8] {'member','domain'}, use_global_device_ids=true, to_apply=%region_11.0 | all-reduce | flops 1 | bytes 8 | tf_op jit(solution)/shard_map/psum | solution.py:61
  246.1 1.1 collective-permute-start.20
  247.2 4.8 %collective-permute-done.20 = f32[25,16,1]{2,1,0:T(8,128)S(1)} collective-permute-done((f32[25,16,1]{2,1,0:T(8,128)S(1)}, f32[25,16,1]{2,1,0:T(8,128)S(1)}, u32[]{:S(2)}, u32[]{:S(2)}) %collective-permute-start.20) | collective-permute-done | bytes 1632 | tf_op jit(solution)/shard_map/ppermute | solution.py:18
  252.1 2.8 %collective-permute-done.21 = f32[25,16,1]{2,1,0:T(8,128)S(1)} collective-permute-done((f32[25,16,1]{2,1,0:T(8,128)S(1)}, f32[25,16,1]{2,1,0:T(8,128)S(1)}, u32[]{:S(2)}, u32[]{:S(2)}) %collective-permute-start.21) | collective-permute-done | bytes 1632 | tf_op jit(solution)/shard_map/ppermute | solution.py:17
  255.9 4.8 %collective-permute-done.22 = f32[25,16,1]{2,1,0:T(8,128)S(1)} collective-permute-done((f32[25,16,1]{2,1,0:T(8,128)S(1)}, f32[25,16,1]{2,1,0:T(8,128)S(1)}, u32[]{:S(2)}, u32[]{:S(2)}) %collective-permute-start.22) | collective-permute-done | bytes 1632 | tf_op jit(solution)/shard_map/ppermute | solution.py:18
  260.7 1.8 collective-permute-done.23
  262.9 18.8 %psum.55 = f32[16,256]{1,0:T(8,128)} all-reduce(f32[16,256]{1,0:T(8,128)S(1)} %fusion.6), channel_id=1, replica_groups=mesh['member'=4,'domain'=8] {'member'}, use_global_device_ids=true, to_apply=%region_13.0 | all-reduce | flops 4096 | bytes 32768 | tf_op jit(solution)/shard_map/psum | solution.py:67
  (52 shorter events, 7.1 us)
Async XLA Ops:
  0.6 20.3 %copy-start = (f32[16,16]{1,0:T(8,128)S(1)}, f32[16,16]{1,0:T(8,128)}, u32[]{:S(2)}) copy-start(f32[16,16]{1,0:T(8,128)} %param.10) | copy-start | bytes 3076
  3.2 9.9 %copy-start.4 = (f32[16]{0:T(128)S(1)}, f32[16]{0:T(128)}, u32[]{:S(2)}) copy-start(f32[16]{0:T(128)} %param.11) | copy-start | bytes 196
  3.2 8.0 %collective-permute-start = (f32[25,16,1]{2,1,0:T(8,128)S(1)}, f32[25,16,1]{2,1,0:T(8,128)S(1)}, u32[]{:S(2)}, u32[]{:S(2)}) collective-permute-start(f32[25,16,1]{2,1,0:T(8,128)S(1)} %get-tuple-element.28), channel_id=1, source_target_pairs={{1,0},{2,1},{3,2},{4,3},{5,4},{6,5},{7,6},{0,7},{9,8},{10,9},{11,1... | collective-permute-start | bytes 4808 | tf_op jit(solution)/shard_map/ppermute | solution.py:18
  6.6 6.5 %collective-permute-start.1 = (f32[25,16,1]{2,1,0:T(8,128)S(1)}, f32[25,16,1]{2,1,0:T(8,128)S(1)}, u32[]{:S(2)}, u32[]{:S(2)}) collective-permute-start(f32[25,16,1]{2,1,0:T(8,128)S(1)} %get-tuple-element.29), channel_id=1, source_target_pairs={{0,1},{1,2},{2,3},{3,4},{4,5},{5,6},{6,7},{7,0},{8,9},{9,10},{10,1... | collective-permute-start | bytes 4808 | tf_op jit(solution)/shard_map/ppermute | solution.py:17
  13.5 5.3 %collective-permute-start.2 = (f32[25,16,1]{2,1,0:T(8,128)S(1)}, f32[25,16,1]{2,1,0:T(8,128)S(1)}, u32[]{:S(2)}, u32[]{:S(2)}) collective-permute-start(f32[25,16,1]{2,1,0:T(8,128)S(1)} %get-tuple-element.26), channel_id=1, source_target_pairs={{1,0},{2,1},{3,2},{4,3},{5,4},{6,5},{7,6},{0,7},{9,8},{10,9},{11,1... | collective-permute-start | bytes 4808 | tf_op jit(solution)/shard_map/ppermute | solution.py:18
  14.5 6.5 %collective-permute-start.3 = (f32[25,16,1]{2,1,0:T(8,128)S(1)}, f32[25,16,1]{2,1,0:T(8,128)S(1)}, u32[]{:S(2)}, u32[]{:S(2)}) collective-permute-start(f32[25,16,1]{2,1,0:T(8,128)S(1)} %get-tuple-element.27), channel_id=1, source_target_pairs={{0,1},{1,2},{2,3},{3,4},{4,5},{5,6},{6,7},{7,0},{8,9},{9,10},{10,1... | collective-permute-start | bytes 4808 | tf_op jit(solution)/shard_map/ppermute | solution.py:17
  22.3 5.3 %collective-permute-start.4 = (f32[25,16,1]{2,1,0:T(8,128)S(1)}, f32[25,16,1]{2,1,0:T(8,128)S(1)}, u32[]{:S(2)}, u32[]{:S(2)}) collective-permute-start(f32[25,16,1]{2,1,0:T(8,128)S(1)} %get-tuple-element.24), channel_id=1, source_target_pairs={{1,0},{2,1},{3,2},{4,3},{5,4},{6,5},{7,6},{0,7},{9,8},{10,9},{11,1... | collective-permute-start | bytes 4808 | tf_op jit(solution)/shard_map/ppermute | solution.py:18
  23.1 6.1 %collective-permute-start.5 = (f32[25,16,1]{2,1,0:T(8,128)S(1)}, f32[25,16,1]{2,1,0:T(8,128)S(1)}, u32[]{:S(2)}, u32[]{:S(2)}) collective-permute-start(f32[25,16,1]{2,1,0:T(8,128)S(1)} %get-tuple-element.25), channel_id=1, source_target_pairs={{0,1},{1,2},{2,3},{3,4},{4,5},{5,6},{6,7},{7,0},{8,9},{9,10},{10,1... | collective-permute-start | bytes 4808 | tf_op jit(solution)/shard_map/ppermute | solution.py:17
  29.5 7.5 %copy-start.1 = (bf16[25,16,256]{2,1,0:T(8,128)(2,1)S(1)}, bf16[25,16,256]{2,1,0:T(8,128)(2,1)}, u32[]{:S(2)}) copy-start(bf16[25,16,256]{2,1,0:T(8,128)(2,1)} %param.6) | copy-start | bytes 614404
  29.7 5.3 %collective-permute-start.6 = (f32[25,16,1]{2,1,0:T(8,128)S(1)}, f32[25,16,1]{2,1,0:T(8,128)S(1)}, u32[]{:S(2)}, u32[]{:S(2)}) collective-permute-start(f32[25,16,1]{2,1,0:T(8,128)S(1)} %get-tuple-element.22), channel_id=1, source_target_pairs={{1,0},{2,1},{3,2},{4,3},{5,4},{6,5},{7,6},{0,7},{9,8},{10,9},{11,1... | collective-permute-start | bytes 4808 | tf_op jit(solution)/shard_map/ppermute | solution.py:18
  31.0 6.1 %collective-permute-start.7 = (f32[25,16,1]{2,1,0:T(8,128)S(1)}, f32[25,16,1]{2,1,0:T(8,128)S(1)}, u32[]{:S(2)}, u32[]{:S(2)}) collective-permute-start(f32[25,16,1]{2,1,0:T(8,128)S(1)} %get-tuple-element.23), channel_id=1, source_target_pairs={{0,1},{1,2},{2,3},{3,4},{4,5},{5,6},{6,7},{7,0},{8,9},{9,10},{10,1... | collective-permute-start | bytes 4808 | tf_op jit(solution)/shard_map/ppermute | solution.py:17
  37.4 19.0 %copy-start.3 = (f32[16,256]{1,0:T(8,128)S(1)}, f32[16,256]{1,0:T(8,128)}, u32[]{:S(2)}) copy-start(f32[16,256]{1,0:T(8,128)} %param.8) | copy-start | bytes 49156
  56.6 5.3 %collective-permute-start.8 = (f32[25,16,1]{2,1,0:T(8,128)S(1)}, f32[25,16,1]{2,1,0:T(8,128)S(1)}, u32[]{:S(2)}, u32[]{:S(2)}) collective-permute-start(f32[25,16,1]{2,1,0:T(8,128)S(1)} %get-tuple-element.20), channel_id=1, source_target_pairs={{1,0},{2,1},{3,2},{4,3},{5,4},{6,5},{7,6},{0,7},{9,8},{10,9},{11,1... | collective-permute-start | bytes 4808 | tf_op jit(solution)/shard_map/ppermute | solution.py:18
  56.7 6.6 %collective-permute-start.9 = (f32[25,16,1]{2,1,0:T(8,128)S(1)}, f32[25,16,1]{2,1,0:T(8,128)S(1)}, u32[]{:S(2)}, u32[]{:S(2)}) collective-permute-start(f32[25,16,1]{2,1,0:T(8,128)S(1)} %get-tuple-element.21), channel_id=1, source_target_pairs={{0,1},{1,2},{2,3},{3,4},{4,5},{5,6},{6,7},{7,0},{8,9},{9,10},{10,1... | collective-permute-start | bytes 4808 | tf_op jit(solution)/shard_map/ppermute | solution.py:17
  63.7 6.0 %collective-permute-start.10 = (f32[25,16,1]{2,1,0:T(8,128)S(1)}, f32[25,16,1]{2,1,0:T(8,128)S(1)}, u32[]{:S(2)}, u32[]{:S(2)}) collective-permute-start(f32[25,16,1]{2,1,0:T(8,128)S(1)} %get-tuple-element.18), channel_id=1, source_target_pairs={{1,0},{2,1},{3,2},{4,3},{5,4},{6,5},{7,6},{0,7},{9,8},{10,9},{11,1... | collective-permute-start | bytes 4808 | tf_op jit(solution)/shard_map/ppermute | solution.py:18
  65.3 6.1 %collective-permute-start.11 = (f32[25,16,1]{2,1,0:T(8,128)S(1)}, f32[25,16,1]{2,1,0:T(8,128)S(1)}, u32[]{:S(2)}, u32[]{:S(2)}) collective-permute-start(f32[25,16,1]{2,1,0:T(8,128)S(1)} %get-tuple-element.19), channel_id=1, source_target_pairs={{0,1},{1,2},{2,3},{3,4},{4,5},{5,6},{6,7},{7,0},{8,9},{9,10},{10,1... | collective-permute-start | bytes 4808 | tf_op jit(solution)/shard_map/ppermute | solution.py:17
  156.3 6.0 %collective-permute-start.12 = (f32[25,16,1]{2,1,0:T(8,128)S(1)}, f32[25,16,1]{2,1,0:T(8,128)S(1)}, u32[]{:S(2)}, u32[]{:S(2)}) collective-permute-start(f32[25,16,1]{2,1,0:T(8,128)S(1)} %get-tuple-element.16), channel_id=1, source_target_pairs={{1,0},{2,1},{3,2},{4,3},{5,4},{6,5},{7,6},{0,7},{9,8},{10,9},{11,1... | collective-permute-start | bytes 4808 | tf_op jit(solution)/shard_map/ppermute | solution.py:18
  157.4 7.6 %collective-permute-start.13 = (f32[25,16,1]{2,1,0:T(8,128)S(1)}, f32[25,16,1]{2,1,0:T(8,128)S(1)}, u32[]{:S(2)}, u32[]{:S(2)}) collective-permute-start(f32[25,16,1]{2,1,0:T(8,128)S(1)} %get-tuple-element.17), channel_id=1, source_target_pairs={{0,1},{1,2},{2,3},{3,4},{4,5},{5,6},{6,7},{7,0},{8,9},{9,10},{10,1... | collective-permute-start | bytes 4808 | tf_op jit(solution)/shard_map/ppermute | solution.py:17
  165.5 5.3 %collective-permute-start.14 = (f32[25,16,1]{2,1,0:T(8,128)S(1)}, f32[25,16,1]{2,1,0:T(8,128)S(1)}, u32[]{:S(2)}, u32[]{:S(2)}) collective-permute-start(f32[25,16,1]{2,1,0:T(8,128)S(1)} %get-tuple-element.14), channel_id=1, source_target_pairs={{1,0},{2,1},{3,2},{4,3},{5,4},{6,5},{7,6},{0,7},{9,8},{10,9},{11,1... | collective-permute-start | bytes 4808 | tf_op jit(solution)/shard_map/ppermute | solution.py:18
  165.6 7.0 %collective-permute-start.15 = (f32[25,16,1]{2,1,0:T(8,128)S(1)}, f32[25,16,1]{2,1,0:T(8,128)S(1)}, u32[]{:S(2)}, u32[]{:S(2)}) collective-permute-start(f32[25,16,1]{2,1,0:T(8,128)S(1)} %get-tuple-element.15), channel_id=1, source_target_pairs={{0,1},{1,2},{2,3},{3,4},{4,5},{5,6},{6,7},{7,0},{8,9},{9,10},{10,1... | collective-permute-start | bytes 4808 | tf_op jit(solution)/shard_map/ppermute | solution.py:17
  190.1 5.5 %collective-permute-start.16 = (f32[25,16,1]{2,1,0:T(8,128)S(1)}, f32[25,16,1]{2,1,0:T(8,128)S(1)}, u32[]{:S(2)}, u32[]{:S(2)}) collective-permute-start(f32[25,16,1]{2,1,0:T(8,128)S(1)} %get-tuple-element.12), channel_id=1, source_target_pairs={{1,0},{2,1},{3,2},{4,3},{5,4},{6,5},{7,6},{0,7},{9,8},{10,9},{11,1... | collective-permute-start | bytes 4808 | tf_op jit(solution)/shard_map/ppermute | solution.py:18
  190.2 6.9 %collective-permute-start.17 = (f32[25,16,1]{2,1,0:T(8,128)S(1)}, f32[25,16,1]{2,1,0:T(8,128)S(1)}, u32[]{:S(2)}, u32[]{:S(2)}) collective-permute-start(f32[25,16,1]{2,1,0:T(8,128)S(1)} %get-tuple-element.13), channel_id=1, source_target_pairs={{0,1},{1,2},{2,3},{3,4},{4,5},{5,6},{6,7},{7,0},{8,9},{9,10},{10,1... | collective-permute-start | bytes 4808 | tf_op jit(solution)/shard_map/ppermute | solution.py:17
  197.6 6.0 %collective-permute-start.18 = (f32[25,16,1]{2,1,0:T(8,128)S(1)}, f32[25,16,1]{2,1,0:T(8,128)S(1)}, u32[]{:S(2)}, u32[]{:S(2)}) collective-permute-start(f32[25,16,1]{2,1,0:T(8,128)S(1)} %get-tuple-element.10), channel_id=1, source_target_pairs={{1,0},{2,1},{3,2},{4,3},{5,4},{6,5},{7,6},{0,7},{9,8},{10,9},{11,1... | collective-permute-start | bytes 4808 | tf_op jit(solution)/shard_map/ppermute | solution.py:18
  199.0 6.1 %collective-permute-start.19 = (f32[25,16,1]{2,1,0:T(8,128)S(1)}, f32[25,16,1]{2,1,0:T(8,128)S(1)}, u32[]{:S(2)}, u32[]{:S(2)}) collective-permute-start(f32[25,16,1]{2,1,0:T(8,128)S(1)} %get-tuple-element.11), channel_id=1, source_target_pairs={{0,1},{1,2},{2,3},{3,4},{4,5},{5,6},{6,7},{7,0},{8,9},{9,10},{10,1... | collective-permute-start | bytes 4808 | tf_op jit(solution)/shard_map/ppermute | solution.py:17
  245.2 0.8 copy-start.2
  246.1 6.0 %collective-permute-start.20 = (f32[25,16,1]{2,1,0:T(8,128)S(1)}, f32[25,16,1]{2,1,0:T(8,128)S(1)}, u32[]{:S(2)}, u32[]{:S(2)}) collective-permute-start(f32[25,16,1]{2,1,0:T(8,128)S(1)} %get-tuple-element.8), channel_id=1, source_target_pairs={{1,0},{2,1},{3,2},{4,3},{5,4},{6,5},{7,6},{0,7},{9,8},{10,9},{11,1... | collective-permute-start | bytes 4808 | tf_op jit(solution)/shard_map/ppermute | solution.py:18
  247.2 7.7 %collective-permute-start.21 = (f32[25,16,1]{2,1,0:T(8,128)S(1)}, f32[25,16,1]{2,1,0:T(8,128)S(1)}, u32[]{:S(2)}, u32[]{:S(2)}) collective-permute-start(f32[25,16,1]{2,1,0:T(8,128)S(1)} %get-tuple-element.9), channel_id=1, source_target_pairs={{0,1},{1,2},{2,3},{3,4},{4,5},{5,6},{6,7},{7,0},{8,9},{9,10},{10,1... | collective-permute-start | bytes 4808 | tf_op jit(solution)/shard_map/ppermute | solution.py:17
  255.3 5.3 %collective-permute-start.22 = (f32[25,16,1]{2,1,0:T(8,128)S(1)}, f32[25,16,1]{2,1,0:T(8,128)S(1)}, u32[]{:S(2)}, u32[]{:S(2)}) collective-permute-start(f32[25,16,1]{2,1,0:T(8,128)S(1)} %get-tuple-element.6), channel_id=1, source_target_pairs={{1,0},{2,1},{3,2},{4,3},{5,4},{6,5},{7,6},{0,7},{9,8},{10,9},{11,1... | collective-permute-start | bytes 4808 | tf_op jit(solution)/shard_map/ppermute | solution.py:18
  255.4 7.1 %collective-permute-start.23 = (f32[25,16,1]{2,1,0:T(8,128)S(1)}, f32[25,16,1]{2,1,0:T(8,128)S(1)}, u32[]{:S(2)}, u32[]{:S(2)}) collective-permute-start(f32[25,16,1]{2,1,0:T(8,128)S(1)} %get-tuple-element.7), channel_id=1, source_target_pairs={{0,1},{1,2},{2,3},{3,4},{4,5},{5,6},{6,7},{7,0},{8,9},{9,10},{10,1... | collective-permute-start | bytes 4808 | tf_op jit(solution)/shard_map/ppermute | solution.py:17
where the time goes:
time: 283 us; the launch traced here: 282 us
  blocking collectives  171 us (60%)
  waiting for transfers between devices  78.3 us (28%)
  starting transfers between devices  13.9 us (5%)
  other arithmetic  6.39 us (2%)
  matrix products  5.07 us (2%)
  between operations  4.89 us (2%)
    psum x2, blocking collectives, total_sum(): return lax.psum(value, ('member', 'domain'))  79.5 us
    ppermute x12, waiting for transfers between devices, extended(): after = lax.ppermute(first, axis, down)  55.6 us
    psum x1, blocking collectives, local(): lax.psum(jnp.sum(direction * image), ('member', 'domain'))  37.3 us
    psum x2, blocking collectives, local(): weighted = weight * lax.psum(partial_sum, 'member')  35.9 us
    ppermute x12, waiting for transfers between devices, extended(): before = lax.ppermute(last, axis, up)  22.7 us
    psum x1, blocking collectives, local(): increment = lax.psum(local_part(control), 'member')  18.8 us
    ppermute x12, starting transfers between devices, extended(): after = lax.ppermute(first, axis, down)  11.9 us
  transfers between devices with their start and end apart: 24, of which 24 were waited for; matrix products, arithmetic and copies ran while one was open for 0% of the time, Pallas kernels for 0%

commit v1 on v0

v1 whole, which is shorter than its diff:
```python
import functools

import jax
import jax.numpy as jnp
from jax import lax
from jax.experimental import pallas as pl
from jax.experimental.pallas import tpu as pltpu
from jax.sharding import PartitionSpec as P

DIFF = 2
LANES = 128
HALO = 4 * DIFF
F32 = jnp.float32
HIGHEST = lax.Precision.HIGHEST
VMEM_LIMIT = 32 * 1024 * 1024


def lane_roll(value, shift):
    return pltpu.roll(value, shift % value.shape[-1], value.ndim - 1)


def lane_index(shape):
    return lax.broadcasted_iota(jnp.int32, shape, len(shape) - 1)


def level_column(diffusivity_ref, levels):
    row = lax.broadcasted_iota(jnp.int32, (levels, LANES), 0)
    column = jnp.zeros((levels, LANES), F32)
    for level in range(levels):
        column = jnp.where(row == level, diffusivity_ref[level], column)
    return column


def widen(column, like):
    copies = like.shape[-1] // LANES
    return column if copies == 1 else jnp.concatenate([column] * copies, axis=-1)


def smooth(field, coef):
    keep = 1.0 - 2.0 * coef
    for _ in range(DIFF):
        field = keep * field + coef * (lane_roll(field, 1) + lane_roll(field, -1))
    return field


def fill_columns(mix_ref, matrix):
    levels = matrix.shape[0]
    for k in range(levels):
        mix_ref[k] = jnp.broadcast_to(matrix[:, k : k + 1], (levels, LANES))


def mixed(mix_ref, field):
    levels = field.shape[0]
    out = None
    for k in range(levels):
        term = widen(mix_ref[k], field) * field[k : k + 1, :]
        out = term if out is None else out + term
    return out


def level_covariance(vertical_map):
    dims = (((1,), (1,)), ((), ()))
    return lax.dot_general(vertical_map, vertical_map, dims, precision=HIGHEST, preferred_element_type=F32)


def ensemble_square(members_ref, field, coef, mix_ref):
    coef = widen(coef, field)

    def one(m, total):
        p = members_ref[m].astype(F32)
        return total + p * smooth(mixed(mix_ref, smooth(p * field, coef)), coef)

    return lax.fori_loop(0, members_ref.shape[0], one, jnp.zeros(field.shape, F32), unroll=5)


def edge_from_own(field):
    lane = lane_index((field.shape[0], LANES))
    last = lane_roll(field[:, -LANES:], HALO)
    first = lane_roll(field[:, :LANES], LANES - HALO)
    return jnp.where(lane < HALO, last, jnp.where(lane >= LANES - HALO, first, 0.0))


def patch(main, edge, width):
    size = main.shape[-1]
    copies = size // LANES
    first = lane_roll(edge, HALO)
    last = lane_roll(edge, LANES - HALO)
    lane = lane_index(main.shape)
    out = jnp.where(lane < width, widen(first, main), main)
    return jnp.where(lane >= size - width, widen(last, main), out)


def weight_of(precision_ref, counts_ref):
    return counts_ref[...].astype(F32) * precision_ref[...]


def pack_kernel(members_ref, innovations_ref, precision_ref, counts_ref, first_ref, last_ref):
    count, levels, size = members_ref.shape
    lane = lane_index((levels, LANES))
    weight = weight_of(precision_ref, counts_ref)
    fields = (weight * innovations_ref[...], weight)

    def put(row, first, last):
        for ref, value, keep, shift in (
            (first_ref, first, lane < HALO, 0),
            (last_ref, last, lane >= LANES - HALO, HALO),
        ):
            value = jnp.where(keep, value, 0.0)
            value = pltpu.roll(value, shift, 1, stride=HALO, stride_axis=0)
            ref[row, :] = jnp.sum(value, axis=0)

    for m in range(count):
        put(m, members_ref[m, :, :LANES].astype(F32), members_ref[m, :, size - LANES :].astype(F32))
    for i, field in enumerate(fields):
        put(count + i, field[:, :LANES], field[:, size - LANES :])


def main_kernel(diffusivity_ref, members_ref, innovations_ref, precision_ref, counts_ref, map_ref, out_ref, mix_ref):
    levels = members_ref.shape[1]
    fill_columns(mix_ref, level_covariance(map_ref[...]))
    coef = level_column(diffusivity_ref, levels)
    source = weight_of(precision_ref, counts_ref) * innovations_ref[...]
    out_ref[...] = ensemble_square(members_ref, source, coef, mix_ref)


def edge_kernel(
    diffusivity_ref, members_ref, innovations_ref, precision_ref, counts_ref, map_ref, before_ref, after_ref, main_ref,
    edge_members_ref, edge_fields_ref, out_ref, mix_ref,
):
    count, levels, size = members_ref.shape
    fill_columns(mix_ref, level_covariance(map_ref[...]))
    coef = level_column(diffusivity_ref, levels)
    lane = lane_index((levels, LANES))
    weight = weight_of(precision_ref, counts_ref)
    fields = (weight * innovations_ref[...], weight)

    mine = lane // HALO == lax.broadcasted_iota(jnp.int32, (levels, LANES), 0)

    def repeated(value):
        value = jnp.where(mine, value, 0.0)
        shift = LANES // 2
        while shift >= HALO:
            value = value + lane_roll(value, shift)
            shift //= 2
        return value

    def unpacked(row, own):
        before, after = (
            repeated(jnp.broadcast_to(ref[row : row + 1, :], (levels, LANES))) for ref in (before_ref, after_ref)
        )
        value = jnp.where((lane >= HALO) & (lane < 2 * HALO), after, own)
        return jnp.where((lane >= LANES - 2 * HALO) & (lane < LANES - HALO), before, value)

    for m in range(count):
        ends = jnp.concatenate([members_ref[m, :, :LANES], members_ref[m, :, size - LANES :]], axis=-1).astype(F32)
        edge_members_ref[m] = unpacked(m, edge_from_own(ends)).astype(edge_members_ref.dtype)
    for i, field in enumerate(fields):
        edge_fields_ref[i] = unpacked(count + i, edge_from_own(field))
    edge = ensemble_square(edge_members_ref, edge_fields_ref[0], coef, mix_ref)
    out_ref[:, :size] = patch(main_ref[...], edge, HALO // 2)
    out_ref[:, size:] = edge


def tree_sum(own, others):
    a, b, c = (ref[...] for ref in others)
    return (own + a) + (b + c)


def second_kernel(
    diffusivity_ref, members_ref, precision_ref, counts_ref, map_ref, edge_members_ref, edge_fields_ref,
    own_ref, a_ref, b_ref, c_ref, first_ref, weighted_ref, out_ref, mix_ref,
):
    levels, size = precision_ref.shape
    fill_columns(mix_ref, level_covariance(map_ref[...]))
    coef = level_column(diffusivity_ref, levels)
    lane = lane_index((levels, LANES))
    total = tree_sum(own_ref[...], (a_ref, b_ref, c_ref))
    first, edge = total[:, :size], total[:, size:]
    own_lane = (lane < HALO) | (lane >= LANES - HALO)
    edge = jnp.where(own_lane, edge_from_own(first), edge)
    near = (lane < HALO + HALO // 2) | (lane >= LANES - HALO - HALO // 2)
    weighted = weight_of(precision_ref, counts_ref) * first
    edge_weighted = jnp.where(near, edge_fields_ref[1] * edge, 0.0)
    first_ref[...] = first
    weighted_ref[:, :size] = weighted
    weighted_ref[:, size:] = edge_weighted
    main = ensemble_square(members_ref, weighted, coef, mix_ref)
    edge = ensemble_square(edge_members_ref, edge_weighted, coef, mix_ref)
    out_ref[...] = patch(main, edge, HALO // 2)


def moments_kernel(
    innovations_ref, precision_ref, counts_ref, first_ref, weighted_ref, own_ref, a_ref, b_ref, c_ref,
    second_ref, moments_ref,
):
    levels, size = precision_ref.shape
    weight = weight_of(precision_ref, counts_ref)
    source = weight * innovations_ref[...]
    first, weighted = first_ref[...], weighted_ref[:, :size]
    second = tree_sum(own_ref[...], (a_ref, b_ref, c_ref))
    second_ref[...] = second
    lane = lane_index((1, LANES))
    width = LANES // 4
    out = jnp.zeros((1, LANES), F32)
    for i, product in enumerate((source * first, weighted * first, weighted * second, weight * second * second)):
        row = sum(product[:, at : at + LANES] for at in range(0, size, LANES))
        row = jnp.sum(row, axis=0, keepdims=True)
        row = row + lane_roll(row, LANES // 2)
        row = row + lane_roll(row, LANES // 4)
        out = jnp.where((lane >= i * width) & (lane < (i + 1) * width), row, out)
    moments_ref[...] = jnp.broadcast_to(out[None], moments_ref.shape)


def adjoint_kernel(diffusivity_ref, members_ref, edge_members_ref, map_ref, field_ref, edge_field_ref, out_ref, mix_ref):
    count, levels, size = members_ref.shape
    fill_columns(mix_ref, map_ref[...].T)
    coef = level_column(diffusivity_ref, levels)
    field, edge_field = field_ref[...], edge_field_ref[...]
    wide = widen(coef, field)

    def one(m, carry):
        main = smooth(members_ref[m].astype(F32) * field, wide)
        edge = smooth(edge_members_ref[m].astype(F32) * edge_field, coef)
        out_ref[m] = mixed(mix_ref, patch(main, edge, DIFF))
        return carry

    lax.fori_loop(0, count, one, 0, unroll=5)


def final_kernel(moments_ref, start_ref, image_ref, first_ref, second_ref, control_ref, increment_ref):
    lane = lane_index((1, LANES))
    width = LANES // 4
    row = jnp.sum(moments_ref[...], axis=0)
    sums = [
        jnp.sum(jnp.where((lane >= i * width) & (lane < (i + 1) * width), row, 0.0), axis=1, keepdims=True)
        for i in range(4)
    ]
    m1, m2, m3 = (value / sums[0] for value in sums[1:])
    alpha = 1.0 / (1.0 + m1)
    spread = jnp.maximum(m2 - m1 * m1, 0.0)
    bend = jnp.maximum(m3 - 2.0 * m1 * m2 + m1 * m1 * m1, 0.0)
    beta = alpha * alpha * spread
    below = spread + bend - alpha * spread * spread
    usable = (spread > 0.0) & (below > 0.0)
    later = jnp.where(usable, jnp.minimum(spread / jnp.where(usable, below, 1.0), 1.0), 0.0)
    on_start = alpha + later * (alpha * m1 + beta)
    on_image = -later * alpha
    increment_ref[...] = on_start * first_ref[...] + on_image * second_ref[...]
    for m in range(start_ref.shape[0]):
        control_ref[m] = on_start * start_ref[m] + on_image * image_ref[m]


def vmem():
    return pl.BlockSpec(memory_space=pltpu.VMEM)


def smem():
    return pl.BlockSpec(memory_space=pltpu.SMEM)


def call(kernel, name, out_shape, args, levels=None, scalars=False, flops=0):
    specs = [vmem()] * len(args)
    if scalars:
        specs[0] = smem()
    scratch = [] if levels is None else [pltpu.VMEM((levels, levels, LANES), F32)]
    multiple = isinstance(out_shape, (list, tuple))
    moved = sum(a.size * a.dtype.itemsize for a in (*args, *(out_shape if multiple else (out_shape,))))
    return pl.pallas_call(
        kernel,
        name=name,
        out_shape=out_shape,
        in_specs=specs,
        out_specs=[vmem()] * len(out_shape) if multiple else vmem(),
        scratch_shapes=scratch,
        cost_estimate=pl.CostEstimate(flops=flops, bytes_accessed=moved, transcendentals=0),
        compiler_params=pltpu.CompilerParams(vmem_limit_bytes=VMEM_LIMIT),
    )(*args)


def shape_of(*dims, dtype=F32):
    return jax.ShapeDtypeStruct(dims, dtype)


def from_partners(value, axis):
    size = lax.axis_size(axis)
    return [lax.ppermute(value, axis, [(i, i ^ step) for i in range(size)]) for step in range(1, size)]


def local(perturbations, innovations, precision_field, obs_counts, vertical_map, diffusivity):
    count, levels, size = perturbations.shape
    counts = obs_counts.reshape(1, size)
    rows = -(-(count + 2) // 8) * 8
    domains = lax.axis_size("domain")
    fields = (innovations, precision_field, counts)
    up = [(i, (i + 1) % domains) for i in range(domains)]
    down = [(j, i) for i, j in up]

    first_cells, last_cells = call(
        pack_kernel, "pack_edges", [shape_of(rows, LANES)] * 2, (perturbations, *fields), flops=count * levels * LANES
    )
    before = lax.ppermute(last_cells, "domain", up)
    after = lax.ppermute(first_cells, "domain", down)
    work = count * levels * size * 60
    main = call(
        main_kernel, "first_inner", shape_of(levels, size), (diffusivity, perturbations, *fields, vertical_map),
        levels, True, work,
    )
    edge_members, edge_fields, part = call(
        edge_kernel, "first_edges",
        [shape_of(count, levels, LANES, dtype=perturbations.dtype), shape_of(2, levels, LANES), shape_of(levels, size + LANES)],
        (diffusivity, perturbations, *fields, vertical_map, before, after, main), levels, True, work,
    )
    others = from_partners(part, "member")
    source = precision_field * counts.astype(F32) * innovations

    def adjoint(name, field, edge_field):
        return call(
            adjoint_kernel, name, shape_of(count, levels, size),
            (diffusivity, perturbations, edge_members, vertical_map, field, edge_field), levels, True, work,
        )

    start = adjoint("start_vector", source, edge_fields[0])
    first, weighted, part = call(
        second_kernel, "second_apply", [shape_of(levels, size), shape_of(levels, size + LANES), shape_of(levels, size)],
        (diffusivity, perturbations, precision_field, counts, vertical_map, edge_members, edge_fields, part, *others),
        levels, True, work,
    )
    others = from_partners(part, "member")
    image = adjoint("image_vector", weighted[:, :size], weighted[:, size:])
    second, moments = call(
        moments_kernel, "moments", [shape_of(levels, size), shape_of(domains, 1, LANES)],
        (*fields, first, weighted, part, *others),
    )
    moments = lax.all_to_all(moments, "domain", 0, 0)
    return tuple(
        call(
            final_kernel, "combine", [shape_of(count, levels, size), shape_of(levels, size)],
            (moments, start, image, first, second),
        )
    )


def solution(mesh):
    in_specs = (
        P("member", None, "domain"),
        P(None, "domain"),
        P(None, "domain"),
        P("domain"),
        P(),
        P(),
    )
    out_specs = (P("member", None, "domain"), P(None, "domain"))
    return jax.shard_map(local, mesh=mesh, in_specs=in_specs, out_specs=out_specs, check_vma=False)
```

time: 283 us -> 49.4 us (0.17)
  blocking collectives: 171 us -> 0 us
  waiting for transfers between devices: 78.3 us -> 5.97 us
  Pallas kernels: 0 us -> 23.1 us
  other arithmetic: 6.39 us -> 0.01 us
  matrix products: 5.07 us -> 0 us
  between operations: 4.89 us -> 0.76 us
    psum x6 -> x0, blocking collectives: 171 us -> none  [the longest x2 79.5 us: total_sum(): return lax.psum(value, ('member', 'domain'))]
    ppermute x24 -> x8, waiting for transfers between devices: 78.3 us -> 5.97 us  [the longest x6 5.96 us: from_partners(): lax.ppermute(value, axis, [(i, i ^ step) for i in range(size)])]
    pallas_call x0 -> x8, Pallas kernels: none -> 23.1 us  [call(): pl.pallas_call(kernel, name=name, out_shape=out_shape, in_specs=specs, ou...]
    dot_general x6 -> x0, matrix products: 5.07 us -> none  [the longest x3 3.59 us: adjoint(): jnp.einsum('kl,mkh->mlh', vertical_map, smooth, precision=lax.Precision.H...]
    all_to_all x0 -> x1, starting transfers between devices: none -> 3.31 us  [local(): moments = lax.all_to_all(moments, 'domain', 0, 0)]
    ppermute x24 -> x8, starting transfers between devices: 13.9 us -> 12.8 us  [the longest x6 9.35 us: from_partners(): lax.ppermute(value, axis, [(i, i ^ step) for i in range(size)])]
  transfers between devices with their start and end apart: 24 -> 9, of which waited for: 24 -> 5; matrix products, arithmetic and copies ran while one was open for 0% -> 0% of each run, Pallas kernels for 0% -> 17%
where the time goes in v1:
time: 49.4 us; the launch traced here: 49 us
  Pallas kernels  23.1 us (47%)
  starting transfers between devices  16.1 us (33%)
  waiting for transfers between devices  5.97 us (12%)
  local copies, waits for them, and re-layouts  3.06 us (6%)
  between operations  0.76 us (2%)
    pallas_call x8, Pallas kernels, call(): pl.pallas_call(kernel, name=name, out_shape=out_shape, in_specs=specs, ou...  23.1 us
    ppermute x6, starting transfers between devices, from_partners(): lax.ppermute(value, axis, [(i, i ^ step) for i in range(size)])  9.35 us
    ppermute x6, waiting for transfers between devices, from_partners(): lax.ppermute(value, axis, [(i, i ^ step) for i in range(size)])  5.96 us
    all_to_all x1, starting transfers between devices, local(): moments = lax.all_to_all(moments, 'domain', 0, 0)  3.31 us
    unnamed x16, local copies, waits for them, and re-layouts  3.06 us
    ppermute x1, starting transfers between devices, local(): after = lax.ppermute(first_cells, 'domain', down)  2.95 us
  transfers between devices with their start and end apart: 9, of which 5 were waited for; matrix products, arithmetic and copies ran while one was open for 0% of the time, Pallas kernels for 17%

profile of v1, /device:TPU:0, one launch (start us, length us, event | category | flops | bytes accessed | tf_op | source)
XLA Modules:
  0.0 49.0 jit_solution(13083136747637859855)
XLA Ops:
  0.6 0.0 copy-start.6
  0.6 0.7 %copy-done.6 = s32[256]{0:T(256)S(1)} copy-done((s32[256]{0:T(256)S(1)}, s32[256]{0:T(256)}, u32[]{:S(2)}) %copy-start.6) | copy-done | bytes 1048
  1.3 0.0 copy-start
  1.3 0.9 %copy-done = bf16[25,16,256]{2,1,0:T(8,128)(2,1)S(1)} copy-done((bf16[25,16,256]{2,1,0:T(8,128)(2,1)S(1)}, bf16[25,16,256]{2,1,0:T(8,128)(2,1)}, u32[]{:S(2)}) %copy-start) | copy-done | bytes 204824
  2.2 0.0 copy-start.2
  2.2 0.7 %copy-done.2 = f32[16,256]{1,0:T(8,128)S(1)} copy-done((f32[16,256]{1,0:T(8,128)S(1)}, f32[16,256]{1,0:T(8,128)}, u32[]{:S(2)}) %copy-start.2) | copy-done | bytes 16408
  3.0 0.0 copy-start.4
  3.0 0.7 %copy-done.4 = f32[16,256]{1,0:T(8,128)S(1)} copy-done((f32[16,256]{1,0:T(8,128)S(1)}, f32[16,256]{1,0:T(8,128)}, u32[]{:S(2)}) %copy-start.4) | copy-done | bytes 16408
  3.7 0.0 copy-start.5
  3.7 0.1 pack_edges.1
  3.8 0.0 copy-start.7
  3.8 0.5 %collective-permute-start = (f32[32,128]{1,0:T(8,128)S(1)}, f32[32,128]{1,0:T(8,128)S(1)}, u32[]{:S(2)}, u32[]{:S(2)}) collective-permute-start(f32[32,128]{1,0:T(8,128)S(1)} %get-tuple-element.12), channel_id=1, source_target_pairs={{0,1},{1,2},{2,3},{3,4},{4,5},{5,6},{6,7},{7,0},{8,9},{9,10},{10,1... | collective-permute-start | bytes 49160 | tf_op jit(solution)/shard_map/ppermute | solution.py:301
  4.3 2.9 %collective-permute-start.1 = (f32[32,128]{1,0:T(8,128)S(1)}, f32[32,128]{1,0:T(8,128)S(1)}, u32[]{:S(2)}, u32[]{:S(2)}) collective-permute-start(f32[32,128]{1,0:T(8,128)S(1)} %get-tuple-element.13), channel_id=1, source_target_pairs={{1,0},{2,1},{3,2},{4,3},{5,4},{6,5},{7,6},{0,7},{9,8},{10,9},{11,1... | collective-permute-start | bytes 49160 | tf_op jit(solution)/shard_map/ppermute | solution.py:302
  7.3 0.0 copy-done.5
  7.3 0.0 copy-done.7
  7.3 2.9 %first_inner.1.main_ref = f32[16,256]{1,0:T(8,128)S(1)} custom-call(f32[16]{0:T(128)S(1)} %copy-done.7, bf16[25,16,256]{2,1,0:T(8,128)(2,1)S(1)} %copy-done, f32[16,256]{1,0:T(8,128)S(1)} %copy-done.4, f32[16,256]{1,0:T(8,128)S(1)} %copy-done.2, s32[1,256]{1,0:T(1,128)S(1)} %bitcast.4, f32[16,16]{1,0:T(8,128)S(1)} %copy-done.5), custom_call_target="tpu_custom_call" | custom-call | flops 6144000 | bytes 256064 | tf_op jit(solution)/shard_map/first_inner/pallas_call | solution.py:268
  10.2 0.0 collective-permute-done.before_ref
  10.3 0.0 collective-permute-done.1.after_ref
  10.3 0.0 copy-start.3
  10.3 8.3 %first_edges.1 = (bf16[25,16,128]{2,1,0:T(8,128)(2,1)S(1)}, f32[2,16,128]{2,1,0:T(8,128)S(1)}, f32[16,384]{1,0:T(8,128)S(1)}) custom-call(f32[16]{0:T(128)S(1)} %copy-done.7, bf16[25,16,256]{2,1,0:T(8,128)(2,1)S(1)} %copy-done, f32[16,256]{1,0:T(8,128)S(1)} %copy-done.4, f32[16,256]{1,0:T(8,128)S(1)} %copy-done.2, s32[1,256]{1,0:T(1,128)S(1)} %bitcast.5, ...), custom_call_target="tpu_custom_call" | custom-call | flops 6144000 | bytes 432192 | tf_op jit(solution)/shard_map/first_edges/pallas_call | solution.py:268
  18.6 4.3 %collective-permute-start.4 = (f32[16,384]{1,0:T(8,128)S(1)}, f32[16,384]{1,0:T(8,128)S(1)}, u32[]{:S(2)}, u32[]{:S(2)}) collective-permute-start(f32[16,384]{1,0:T(8,128)S(1)} %get-tuple-element.16.own_ref), channel_id=1, source_target_pairs={{0,24},{8,16},{16,8},{24,0},{1,25},{9,17},{17,9},{25,1},{2,26},{10... | collective-permute-start | bytes 73736 | tf_op jit(solution)/shard_map/ppermute | solution.py:286
  22.9 0.0 collective-permute-start.3
  22.9 0.6 %collective-permute-start.2 = (f32[16,384]{1,0:T(8,128)S(1)}, f32[16,384]{1,0:T(8,128)S(1)}, u32[]{:S(2)}, u32[]{:S(2)}) collective-permute-start(f32[16,384]{1,0:T(8,128)S(1)} %get-tuple-element.16.own_ref), channel_id=1, source_target_pairs={{0,8},{8,0},{16,24},{24,16},{1,9},{9,1},{17,25},{25,17},{2,10},{10... | collective-permute-start | bytes 73736 | tf_op jit(solution)/shard_map/ppermute | solution.py:286
  23.6 1.3 %collective-permute-done.4.c_ref = f32[16,384]{1,0:T(8,128)S(1)} collective-permute-done((f32[16,384]{1,0:T(8,128)S(1)}, f32[16,384]{1,0:T(8,128)S(1)}, u32[]{:S(2)}, u32[]{:S(2)}) %collective-permute-start.4) | collective-permute-done | bytes 24608 | tf_op jit(solution)/shard_map/ppermute | solution.py:286
  24.9 2.8 %collective-permute-done.3.b_ref = f32[16,384]{1,0:T(8,128)S(1)} collective-permute-done((f32[16,384]{1,0:T(8,128)S(1)}, f32[16,384]{1,0:T(8,128)S(1)}, u32[]{:S(2)}, u32[]{:S(2)}) %collective-permute-start.3) | collective-permute-done | bytes 24608 | tf_op jit(solution)/shard_map/ppermute | solution.py:286
  27.6 0.0 collective-permute-done.2.a_ref
  27.6 0.0 copy-done.3
  27.6 4.8 %second_apply.1 = (f32[16,256]{1,0:T(8,128)S(1)}, f32[16,384]{1,0:T(8,128)S(1)}, f32[16,256]{1,0:T(8,128)S(1)}) custom-call(f32[16]{0:T(128)S(1)} %copy-done.7, bf16[25,16,256]{2,1,0:T(8,128)(2,1)S(1)} %copy-done, f32[16,256]{1,0:T(8,128)S(1)} %copy-done.3, s32[1,256]{1,0:T(1,128)S(1)} %bitcast.6, f32[16,16]{1,0:T(8,128)S(1)} %copy-done.5, ...), custom_call_target="tpu_custom_call" | custom-call | flops 6144000 | bytes 497728 | tf_op jit(solution)/shard_map/second_apply/pallas_call | solution.py:268
  32.5 0.0 copy-start.1
  32.5 1.5 %collective-permute-start.7 = (f32[16,256]{1,0:T(8,128)S(1)}, f32[16,256]{1,0:T(8,128)S(1)}, u32[]{:S(2)}, u32[]{:S(2)}) collective-permute-start(f32[16,256]{1,0:T(8,128)S(1)} %get-tuple-element.19.own_ref), channel_id=1, source_target_pairs={{0,24},{8,16},{16,8},{24,0},{1,25},{9,17},{17,9},{25,1},{2,26},{10... | collective-permute-start | bytes 49160 | tf_op jit(solution)/shard_map/ppermute | solution.py:286
  34.0 0.6 %collective-permute-start.6 = (f32[16,256]{1,0:T(8,128)S(1)}, f32[16,256]{1,0:T(8,128)S(1)}, u32[]{:S(2)}, u32[]{:S(2)}) collective-permute-start(f32[16,256]{1,0:T(8,128)S(1)} %get-tuple-element.19.own_ref), channel_id=1, source_target_pairs={{0,16},{8,24},{16,0},{24,8},{1,17},{9,25},{17,1},{25,9},{2,18},{10... | collective-permute-start | bytes 49160 | tf_op jit(solution)/shard_map/ppermute | solution.py:286
  34.6 2.3 %collective-permute-start.5 = (f32[16,256]{1,0:T(8,128)S(1)}, f32[16,256]{1,0:T(8,128)S(1)}, u32[]{:S(2)}, u32[]{:S(2)}) collective-permute-start(f32[16,256]{1,0:T(8,128)S(1)} %get-tuple-element.19.own_ref), channel_id=1, source_target_pairs={{0,8},{8,0},{16,24},{24,16},{1,9},{9,1},{17,25},{25,17},{2,10},{10... | collective-permute-start | bytes 49160 | tf_op jit(solution)/shard_map/ppermute | solution.py:286
  36.9 1.1 %collective-permute-done.7.c_ref = f32[16,256]{1,0:T(8,128)S(1)} collective-permute-done((f32[16,256]{1,0:T(8,128)S(1)}, f32[16,256]{1,0:T(8,128)S(1)}, u32[]{:S(2)}, u32[]{:S(2)}) %collective-permute-start.7) | collective-permute-done | bytes 16416 | tf_op jit(solution)/shard_map/ppermute | solution.py:286
  38.0 0.6 %collective-permute-done.6.b_ref = f32[16,256]{1,0:T(8,128)S(1)} collective-permute-done((f32[16,256]{1,0:T(8,128)S(1)}, f32[16,256]{1,0:T(8,128)S(1)}, u32[]{:S(2)}, u32[]{:S(2)}) %collective-permute-start.6) | collective-permute-done | bytes 16416 | tf_op jit(solution)/shard_map/ppermute | solution.py:286
  38.6 0.2 collective-permute-done.5.a_ref
  38.8 0.8 %moments.1 = (f32[16,256]{1,0:T(8,128)S(1)}, f32[8,1,128]{2,1,0:T(1,128)}) custom-call(f32[16,256]{1,0:T(8,128)S(1)} %copy-done.4, f32[16,256]{1,0:T(8,128)S(1)} %copy-done.3, s32[1,256]{1,0:T(1,128)S(1)} %bitcast.7, f32[16,256]{1,0:T(8,128)S(1)} %get-tuple-element.17.first_ref, f32[16,384]{1,0:T(8,128)S(1)} %get-tuple-element.18.weighted_ref, ...), custom_call_target="tpu_custom_call" | custom-call | bytes 160768 | tf_op jit(solution)/shard_map/moments/pallas_call | solution.py:268
  39.5 3.3 %all-to-all-start = ((f32[8,1,128]{2,1,0:T(1,128)}), f32[8,1,128]{2,1,0:T(1,128)S(1)}, u32[]{:S(2)}, u32[]{:S(2)}) async-start(f32[8,1,128]{2,1,0:T(1,128)} %get-tuple-element.20), calls=%async_computation | async-start | bytes 8192 | tf_op jit(solution)/shard_map/all_to_all | solution.py:334
  42.8 0.0 copy-done.1
  42.9 2.6 %start_vector.1.start_ref = f32[25,16,256]{2,1,0:T(8,128)S(1)} custom-call(f32[16]{0:T(128)S(1)} %copy-done.7, bf16[25,16,256]{2,1,0:T(8,128)(2,1)S(1)} %copy-done.1, bf16[25,16,128]{2,1,0:T(8,128)(2,1)S(1)} %get-tuple-element.14.edge_members_ref, f32[16,16]{1,0:T(8,128)S(1)} %copy-done.5, f32[16,256]{1,0:T(8,128)S(1)} %multiply_multiply_fusion.field_ref, ...), custom_call_target="tpu_custom_call" | custom-call | flops 6144000 | bytes 742464 | tf_op jit(solution)/shard_map/start_vector/pallas_call | solution.py:268
  45.5 2.6 %image_vector.1.image_ref = f32[25,16,256]{2,1,0:T(8,128)S(1)} custom-call(f32[16]{0:T(128)S(1)} %copy-done.7, bf16[25,16,256]{2,1,0:T(8,128)(2,1)S(1)} %copy-done.1, bf16[25,16,128]{2,1,0:T(8,128)(2,1)S(1)} %get-tuple-element.14.edge_members_ref, f32[16,16]{1,0:T(8,128)S(1)} %copy-done.5, f32[16,256]{1,0:T(8,128)S(1)} %slice.10.field_ref, ...), custom_call_target="tpu_custom_call" | custom-call | flops 6144000 | bytes 742464 | tf_op jit(solution)/shard_map/image_vector/pallas_call | solution.py:268
  48.1 0.0 all-to-all-done.moments_ref
  48.1 0.9 %combine.1 = (f32[25,16,256]{2,1,0:T(8,128)}, f32[16,256]{1,0:T(8,128)}) custom-call(f32[8,1,128]{2,1,0:T(1,128)S(1)} %all-to-all-done.moments_ref, f32[25,16,256]{2,1,0:T(8,128)S(1)} %start_vector.1.start_ref, f32[25,16,256]{2,1,0:T(8,128)S(1)} %image_vector.1.image_ref, f32[16,256]{1,0:T(8,128)S(1)} %get-tuple-element.17.first_ref, ...), custom_call_target="tpu_custom_call" | custom-call | bytes 1282048 | tf_op jit(solution)/shard_map/combine/pallas_call | solution.py:268
  (5 shorter events, 0.0 us)
Async XLA Ops:
  0.6 0.7 %copy-start.6 = (s32[256]{0:T(256)S(1)}, s32[256]{0:T(256)}, u32[]{:S(2)}) copy-start(s32[256]{0:T(256)} %param.9) | copy-start | bytes 3076
  1.3 0.9 %copy-start = (bf16[25,16,256]{2,1,0:T(8,128)(2,1)S(1)}, bf16[25,16,256]{2,1,0:T(8,128)(2,1)}, u32[]{:S(2)}) copy-start(bf16[25,16,256]{2,1,0:T(8,128)(2,1)} %members_ref.11) | copy-start | bytes 614404
  2.2 0.7 %copy-start.2 = (f32[16,256]{1,0:T(8,128)S(1)}, f32[16,256]{1,0:T(8,128)}, u32[]{:S(2)}) copy-start(f32[16,256]{1,0:T(8,128)} %precision_ref.9) | copy-start | bytes 49156
  3.0 0.7 %copy-start.4 = (f32[16,256]{1,0:T(8,128)S(1)}, f32[16,256]{1,0:T(8,128)}, u32[]{:S(2)}) copy-start(f32[16,256]{1,0:T(8,128)} %innovations_ref.7) | copy-start | bytes 49156
  3.7 3.6 %copy-start.5 = (f32[16,16]{1,0:T(8,128)S(1)}, f32[16,16]{1,0:T(8,128)}, u32[]{:S(2)}) copy-start(f32[16,16]{1,0:T(8,128)} %map_ref.9) | copy-start | bytes 3076
  3.8 3.5 %copy-start.7 = (f32[16]{0:T(128)S(1)}, f32[16]{0:T(128)}, u32[]{:S(2)}) copy-start(f32[16]{0:T(128)} %diffusivity_ref.9) | copy-start | bytes 196
  3.8 6.4 %collective-permute-start = (f32[32,128]{1,0:T(8,128)S(1)}, f32[32,128]{1,0:T(8,128)S(1)}, u32[]{:S(2)}, u32[]{:S(2)}) collective-permute-start(f32[32,128]{1,0:T(8,128)S(1)} %get-tuple-element.12), channel_id=1, source_target_pairs={{0,1},{1,2},{2,3},{3,4},{4,5},{5,6},{6,7},{7,0},{8,9},{9,10},{10,1... | collective-permute-start | bytes 49160 | tf_op jit(solution)/shard_map/ppermute | solution.py:301
  4.3 5.9 %collective-permute-start.1 = (f32[32,128]{1,0:T(8,128)S(1)}, f32[32,128]{1,0:T(8,128)S(1)}, u32[]{:S(2)}, u32[]{:S(2)}) collective-permute-start(f32[32,128]{1,0:T(8,128)S(1)} %get-tuple-element.13), channel_id=1, source_target_pairs={{1,0},{2,1},{3,2},{4,3},{5,4},{6,5},{7,6},{0,7},{9,8},{10,9},{11,1... | collective-permute-start | bytes 49160 | tf_op jit(solution)/shard_map/ppermute | solution.py:302
  10.3 17.4 %copy-start.3 = (f32[16,256]{1,0:T(8,128)S(1)}, f32[16,256]{1,0:T(8,128)}, u32[]{:S(2)}) copy-start(f32[16,256]{1,0:T(8,128)} %precision_ref.9) | copy-start | bytes 49156
  18.6 6.3 %collective-permute-start.4 = (f32[16,384]{1,0:T(8,128)S(1)}, f32[16,384]{1,0:T(8,128)S(1)}, u32[]{:S(2)}, u32[]{:S(2)}) collective-permute-start(f32[16,384]{1,0:T(8,128)S(1)} %get-tuple-element.16.own_ref), channel_id=1, source_target_pairs={{0,24},{8,16},{16,8},{24,0},{1,25},{9,17},{17,9},{25,1},{2,26},{10... | collective-permute-start | bytes 73736 | tf_op jit(solution)/shard_map/ppermute | solution.py:286
  22.9 4.7 %collective-permute-start.3 = (f32[16,384]{1,0:T(8,128)S(1)}, f32[16,384]{1,0:T(8,128)S(1)}, u32[]{:S(2)}, u32[]{:S(2)}) collective-permute-start(f32[16,384]{1,0:T(8,128)S(1)} %get-tuple-element.16.own_ref), channel_id=1, source_target_pairs={{0,16},{8,24},{16,0},{24,8},{1,17},{9,25},{17,1},{25,9},{2,18},{10... | collective-permute-start | bytes 73736 | tf_op jit(solution)/shard_map/ppermute | solution.py:286
  22.9 4.7 %collective-permute-start.2 = (f32[16,384]{1,0:T(8,128)S(1)}, f32[16,384]{1,0:T(8,128)S(1)}, u32[]{:S(2)}, u32[]{:S(2)}) collective-permute-start(f32[16,384]{1,0:T(8,128)S(1)} %get-tuple-element.16.own_ref), channel_id=1, source_target_pairs={{0,8},{8,0},{16,24},{24,16},{1,9},{9,1},{17,25},{25,17},{2,10},{10... | collective-permute-start | bytes 73736 | tf_op jit(solution)/shard_map/ppermute | solution.py:286
  32.5 10.4 %copy-start.1 = (bf16[25,16,256]{2,1,0:T(8,128)(2,1)S(1)}, bf16[25,16,256]{2,1,0:T(8,128)(2,1)}, u32[]{:S(2)}) copy-start(bf16[25,16,256]{2,1,0:T(8,128)(2,1)} %members_ref.11) | copy-start | bytes 614404
  32.5 5.6 %collective-permute-start.7 = (f32[16,256]{1,0:T(8,128)S(1)}, f32[16,256]{1,0:T(8,128)S(1)}, u32[]{:S(2)}, u32[]{:S(2)}) collective-permute-start(f32[16,256]{1,0:T(8,128)S(1)} %get-tuple-element.19.own_ref), channel_id=1, source_target_pairs={{0,24},{8,16},{16,8},{24,0},{1,25},{9,17},{17,9},{25,1},{2,26},{10... | collective-permute-start | bytes 49160 | tf_op jit(solution)/shard_map/ppermute | solution.py:286
  34.0 4.7 %collective-permute-start.6 = (f32[16,256]{1,0:T(8,128)S(1)}, f32[16,256]{1,0:T(8,128)S(1)}, u32[]{:S(2)}, u32[]{:S(2)}) collective-permute-start(f32[16,256]{1,0:T(8,128)S(1)} %get-tuple-element.19.own_ref), channel_id=1, source_target_pairs={{0,16},{8,24},{16,0},{24,8},{1,17},{9,25},{17,1},{25,9},{2,18},{10... | collective-permute-start | bytes 49160 | tf_op jit(solution)/shard_map/ppermute | solution.py:286
  34.6 4.2 %collective-permute-start.5 = (f32[16,256]{1,0:T(8,128)S(1)}, f32[16,256]{1,0:T(8,128)S(1)}, u32[]{:S(2)}, u32[]{:S(2)}) collective-permute-start(f32[16,256]{1,0:T(8,128)S(1)} %get-tuple-element.19.own_ref), channel_id=1, source_target_pairs={{0,8},{8,0},{16,24},{24,16},{1,9},{9,1},{17,25},{25,17},{2,10},{10... | collective-permute-start | bytes 49160 | tf_op jit(solution)/shard_map/ppermute | solution.py:286
  39.5 8.6 %all-to-all-start = ((f32[8,1,128]{2,1,0:T(1,128)}), f32[8,1,128]{2,1,0:T(1,128)S(1)}, u32[]{:S(2)}, u32[]{:S(2)}) async-start(f32[8,1,128]{2,1,0:T(1,128)} %get-tuple-element.20), calls=%async_computation | async-start | bytes 8192 | tf_op jit(solution)/shard_map/all_to_all | solution.py:334

commit v2 on v0

v2 whole, which is shorter than its diff:
```python
import functools

import jax
import jax.numpy as jnp
from jax import lax
from jax.experimental import pallas as pl
from jax.experimental.pallas import tpu as pltpu
from jax.sharding import PartitionSpec as P

DIFF = 2
LANES = 128
REACH = 2 * DIFF
HALO = 2 * REACH
SLOT = 4 * HALO
SLOTS = LANES // SLOT
F32 = jnp.float32
HIGHEST = lax.Precision.HIGHEST
VMEM_LIMIT = 32 * 1024 * 1024


def lane_roll(value, shift):
    return pltpu.roll(value, shift % value.shape[-1], value.ndim - 1)


def lane_index(shape):
    return lax.broadcasted_iota(jnp.int32, shape, len(shape) - 1)


def widen(column, like):
    copies = like.shape[-1] // LANES
    return column if copies == 1 else jnp.concatenate([column] * copies, axis=-1)


def level_column(diffusivity_ref, levels):
    row = lax.broadcasted_iota(jnp.int32, (levels, LANES), 0)
    column = jnp.zeros((levels, LANES), F32)
    for level in range(levels):
        column = jnp.where(row == level, diffusivity_ref[level], column)
    return column


def smooth(field, taps):
    near = lane_roll(field, 1) + lane_roll(field, -1)
    far = lane_roll(field, 2) + lane_roll(field, -2)
    return taps[0] * field + taps[1] * near + taps[2] * far


def mixed(mix_ref, field_ref):
    out = None
    for k in range(mix_ref.shape[0]):
        row = field_ref[k : k + 1, :]
        term = widen(mix_ref[k], row) * row
        out = term if out is None else out + term
    return out


def wide_taps(taps_ref, like):
    return [widen(taps_ref[i], like) for i in range(3)]


def apply_ensemble(parts, taps_ref, mix_ref, scratches):
    totals = []
    for (members_ref, field), (x_ref, y_ref) in zip(parts, scratches):
        taps = wide_taps(taps_ref, field)
        for m in range(members_ref.shape[0]):
            x_ref[m] = smooth(members_ref[m].astype(F32) * field, taps)
    for (members_ref, field), (x_ref, y_ref) in zip(parts, scratches):
        for m in range(members_ref.shape[0]):
            y_ref[m] = mixed(mix_ref, x_ref.at[m])
    for (members_ref, field), (x_ref, y_ref) in zip(parts, scratches):
        taps = wide_taps(taps_ref, field)
        total = jnp.zeros(field.shape, F32)
        for m in range(members_ref.shape[0]):
            total = total + members_ref[m].astype(F32) * smooth(y_ref[m], taps)
        totals.append(total)
    return totals


def all_slots(value):
    shift = SLOT
    while shift < LANES:
        value = value + lane_roll(value, shift)
        shift *= 2
    return value


def ends_of(first, last, lane):
    return jnp.where(lane < HALO, first, jnp.where(lane >= LANES - HALO, last, 0.0))


def patch(main, edge, width, slot=0):
    size = main.shape[-1]
    first = lane_roll(edge, -(slot * SLOT + HALO))
    last = lane_roll(edge, -(slot * SLOT + 3 * HALO))
    lane = lane_index(main.shape)
    out = jnp.where(lane < width, widen(first, main), main)
    return jnp.where(lane >= size - width, widen(last, main), out)


def pack_kernel(
    members_hbm, innovations_hbm, precision_hbm, counts_hbm,
    members_ref, fields_ref, low_ref, high_ref, innovations_ref, precision_ref, counts_ref, sems,
):
    copies = [
        pltpu.make_async_copy(source, target, sems.at[i])
        for i, (source, target) in enumerate(
            (
                (members_hbm, members_ref),
                (innovations_hbm, innovations_ref),
                (precision_hbm, precision_ref),
                (counts_hbm, counts_ref),
            )
        )
    ]
    for copy in copies:
        copy.start()
    for copy in copies[1:]:
        copy.wait()
    weight = counts_ref[...].astype(F32) * precision_ref[...]
    fields_ref[0] = weight * innovations_ref[...]
    fields_ref[1] = weight
    copies[0].wait()
    count, levels, size = members_ref.shape
    lane = lane_index((levels, LANES))
    for tile in range(low_ref.shape[0]):
        low, high = jnp.zeros((levels, LANES), F32), jnp.zeros((levels, LANES), F32)
        for slot in range(SLOTS):
            m = tile * SLOTS + slot
            if m < count:
                first, last = members_ref[m, :, :LANES].astype(F32), members_ref[m, :, size - LANES :].astype(F32)
            elif m < count + 2:
                first, last = fields_ref[m - count, :, :LANES], fields_ref[m - count, :, size - LANES :]
            else:
                continue
            ends = ends_of(first, last, lane)
            low = low + lane_roll(ends, slot * SLOT + HALO)
            high = high + lane_roll(ends, slot * SLOT + 3 * HALO)
        low_ref[tile] = low
        high_ref[tile] = high


def main_kernel(
    diffusivity_ref, map_ref, members_ref, fields_ref, taps_ref, square_ref, adjoint_ref, out_ref, x_ref, y_ref
):
    levels = members_ref.shape[1]
    matrix = map_ref[...]
    dims = (((1,), (1,)), ((), ()))
    square = lax.dot_general(matrix, matrix, dims, precision=HIGHEST, preferred_element_type=F32)
    turned = matrix.T
    for k in range(levels):
        square_ref[k] = jnp.broadcast_to(square[:, k : k + 1], (levels, LANES))
        adjoint_ref[k] = jnp.broadcast_to(turned[:, k : k + 1], (levels, LANES))
    coef = level_column(diffusivity_ref, levels)
    keep = 1.0 - 2.0 * coef
    taps_ref[0] = keep * keep + 2.0 * coef * coef
    taps_ref[1] = 2.0 * keep * coef
    taps_ref[2] = coef * coef
    (out_ref[...],) = apply_ensemble([(members_ref, fields_ref[0])], taps_ref, square_ref, [(x_ref, y_ref)])


def edge_kernel(
    count, low_ref, high_ref, before_ref, after_ref, taps_ref, square_ref, main_ref,
    edge_members_ref, edge_fields_ref, out_ref, x_ref, y_ref,
):
    tiles, levels, _ = low_ref.shape
    size = main_ref.shape[1]
    lane = lane_index((levels, LANES))
    at, slot_of = lane % SLOT, lane // SLOT
    for tile in range(tiles):
        own = jnp.where(at >= 2 * HALO, high_ref[tile], low_ref[tile])
        value = jnp.where(at >= 3 * HALO, after_ref[tile], jnp.where(at < HALO, before_ref[tile], own))
        for i in range(2):
            place, slot = divmod(count + i, SLOTS)
            if place == tile:
                edge_fields_ref[i] = all_slots(jnp.where(slot_of == slot, value, 0.0))
        held = min(max(count - tile * SLOTS, 0), SLOTS)
        edge_members_ref[tile] = value if held == SLOTS else jnp.where(slot_of < held, value, 0.0)
    (edge,) = apply_ensemble([(edge_members_ref, edge_fields_ref[0])], taps_ref, square_ref, [(x_ref, y_ref)])
    edge = all_slots(edge)
    out_ref[:, :size] = patch(main_ref[...], edge, REACH)
    out_ref[:, size:] = edge


def tree_sum(own_ref, a_ref, b_ref, c_ref):
    return (own_ref[...] + a_ref[...]) + (b_ref[...] + c_ref[...])


def second_kernel(
    members_ref, edge_members_ref, fields_ref, edge_fields_ref, taps_ref, square_ref, own_ref, a_ref, b_ref, c_ref, _,
    first_ref, weighted_ref, edge_weighted_ref, out_ref, x_ref, y_ref, edge_x_ref, edge_y_ref,
):
    _, levels, size = members_ref.shape
    lane = lane_index((levels, LANES))
    at = lane % SLOT
    total = tree_sum(own_ref, a_ref, b_ref, c_ref)
    first, edge = total[:, :size], total[:, size:]
    ends = ends_of(first[:, :LANES], first[:, size - LANES :], lane)
    own = jnp.where(lane >= 2 * HALO, lane_roll(ends, 3 * HALO), lane_roll(ends, HALO))
    own = all_slots(jnp.where(lane < SLOT, own, 0.0))
    edge = jnp.where((at >= HALO) & (at < 3 * HALO), own, edge)
    weighted = fields_ref[1] * first
    edge_weighted = edge_fields_ref[1] * edge
    first_ref[...] = first
    weighted_ref[...] = weighted
    edge_weighted_ref[...] = edge_weighted
    main, edge = apply_ensemble(
        [(members_ref, weighted), (edge_members_ref, edge_weighted)], taps_ref, square_ref,
        [(x_ref, y_ref), (edge_x_ref, edge_y_ref)],
    )
    out_ref[...] = patch(main, all_slots(edge), REACH)


def moments_kernel(
    fields_ref, first_ref, weighted_ref, own_ref, a_ref, b_ref, c_ref, _, second_ref, moments_ref
):
    size = first_ref.shape[1]
    source, weight = fields_ref[0], fields_ref[1]
    first, weighted = first_ref[...], weighted_ref[...]
    second = tree_sum(own_ref, a_ref, b_ref, c_ref)
    second_ref[...] = second
    lane = lane_index((1, LANES))
    width = LANES // 4
    out = jnp.zeros((1, LANES), F32)
    for i, product in enumerate((source * first, weighted * first, weighted * second, weight * second * second)):
        row = sum(product[:, at : at + LANES] for at in range(0, size, LANES))
        row = jnp.sum(row, axis=0, keepdims=True)
        row = row + lane_roll(row, LANES // 2)
        row = row + lane_roll(row, LANES // 4)
        out = jnp.where((lane >= i * width) & (lane < (i + 1) * width), row, out)
    moments_ref[...] = jnp.broadcast_to(out[None], moments_ref.shape)


def adjoint_kernel(
    members_ref, edge_members_ref, field_ref, edge_field_ref, taps_ref, adjoint_ref, out_ref, x_ref, edge_x_ref
):
    field, edge_field = field_ref[...], edge_field_ref[...]
    taps, edge_taps = wide_taps(taps_ref, field), wide_taps(taps_ref, edge_field)
    for tile in range(edge_members_ref.shape[0]):
        edge_x_ref[tile] = smooth(edge_members_ref[tile] * edge_field, edge_taps)
    for m in range(members_ref.shape[0]):
        main = smooth(members_ref[m].astype(F32) * field, taps)
        x_ref[m] = patch(main, edge_x_ref[m // SLOTS], DIFF, m % SLOTS)
    for m in range(members_ref.shape[0]):
        out_ref[m] = mixed(adjoint_ref, x_ref.at[m])


def final_kernel(moments_ref, start_ref, image_ref, first_ref, second_ref, control_ref, increment_ref):
    lane = lane_index((1, LANES))
    width = LANES // 4
    row = jnp.sum(moments_ref[...], axis=0)
    sums = [
        jnp.sum(jnp.where((lane >= i * width) & (lane < (i + 1) * width), row, 0.0), axis=1, keepdims=True)
        for i in range(4)
    ]
    m1, m2, m3 = (value / sums[0] for value in sums[1:])
    alpha = 1.0 / (1.0 + m1)
    spread = jnp.maximum(m2 - m1 * m1, 0.0)
    bend = jnp.maximum(m3 - 2.0 * m1 * m2 + m1 * m1 * m1, 0.0)
    beta = alpha * alpha * spread
    below = spread + bend - alpha * spread * spread
    usable = (spread > 0.0) & (below > 0.0)
    later = jnp.where(usable, jnp.minimum(spread / jnp.where(usable, below, 1.0), 1.0), 0.0)
    on_start = alpha + later * (alpha * m1 + beta)
    on_image = -later * alpha
    increment_ref[...] = on_start * first_ref[...] + on_image * second_ref[...]
    for m in range(start_ref.shape[0]):
        control_ref[m] = on_start * start_ref[m] + on_image * image_ref[m]


def vmem():
    return pl.BlockSpec(memory_space=pltpu.VMEM)


def elsewhere():
    return pl.BlockSpec(memory_space=pl.ANY)


def smem():
    return pl.BlockSpec(memory_space=pltpu.SMEM)


def call(kernel, name, outs, args, scratch=(), specs=None, flops=0):
    specs = specs or {}
    moved = sum(a.size * a.dtype.itemsize for a in (*args, *outs))
    return pl.pallas_call(
        kernel,
        name=name,
        out_shape=list(outs),
        in_specs=[specs.get(i, vmem)() for i in range(len(args))],
        out_specs=[vmem()] * len(outs),
        scratch_shapes=list(scratch),
        cost_estimate=pl.CostEstimate(flops=flops, bytes_accessed=moved, transcendentals=0),
        compiler_params=pltpu.CompilerParams(vmem_limit_bytes=VMEM_LIMIT),
    )(*args)


def shape_of(*dims, dtype=F32):
    return jax.ShapeDtypeStruct(dims, dtype)


def from_partners(value, axis):
    size = lax.axis_size(axis)
    return [lax.ppermute(value, axis, [(i, i ^ step) for i in range(size)]) for step in range(1, size)]


def local(perturbations, innovations, precision_field, obs_counts, vertical_map, diffusivity):
    count, levels, size = perturbations.shape
    tiles = -(-(count + 2) // SLOTS)
    domains = lax.axis_size("domain")
    up = [(i, (i + 1) % domains) for i in range(domains)]
    down = [(j, i) for i, j in up]
    level = shape_of(levels, size)
    members_f32 = shape_of(count, levels, size)
    edge_tiles = shape_of(tiles, levels, LANES)
    column = shape_of(levels, levels, LANES)
    work, edge_work = count * levels * size * 50, tiles * levels * LANES * 50
    scratch = [pltpu.VMEM((count, levels, size), F32)] * 2
    edge_scratch = [pltpu.VMEM((tiles, levels, LANES), F32)] * 2

    members, fields, low, high = call(
        pack_kernel, "pack_edges",
        [shape_of(count, levels, size, dtype=perturbations.dtype), shape_of(2, levels, size), edge_tiles, edge_tiles],
        (perturbations, innovations, precision_field, obs_counts.reshape(1, size)),
        [pltpu.VMEM((levels, size), F32)] * 2 + [pltpu.VMEM((1, size), jnp.int32), pltpu.SemaphoreType.DMA((4,))],
        dict.fromkeys(range(4), elsewhere), tiles * levels * LANES * 20,
    )
    before = lax.ppermute(low, "domain", up)
    after = lax.ppermute(high, "domain", down)
    taps, square, mapped, main = call(
        main_kernel, "first_inner", [shape_of(3, levels, LANES), column, column, level],
        (diffusivity, vertical_map, members, fields), scratch, {0: smem}, work,
    )
    edge_members, edge_fields, part = call(
        functools.partial(edge_kernel, count), "first_edges",
        [edge_tiles, shape_of(2, levels, LANES), shape_of(levels, size + LANES)],
        (low, high, before, after, taps, square, main), edge_scratch, flops=edge_work,
    )

    def adjoint(name, field, edge_field):
        (out,) = call(
            adjoint_kernel, name, [members_f32], (members, edge_members, field, edge_field, taps, mapped),
            [scratch[0], edge_scratch[0]], flops=work,
        )
        return out

    others = from_partners(part, "member")
    start = adjoint("start_vector", fields[0], edge_fields[0])
    first, weighted, edge_weighted, part = call(
        second_kernel, "second_apply", [level, level, shape_of(levels, LANES), level],
        (members, edge_members, fields, edge_fields, taps, square, part, *others, start),
        scratch + edge_scratch, {10: elsewhere}, work + edge_work,
    )
    others = from_partners(part, "member")
    image = adjoint("image_vector", weighted, edge_weighted)
    second, moments = call(
        moments_kernel, "moments", [level, shape_of(domains, 1, LANES)],
        (fields, first, weighted, part, *others, image), (), {7: elsewhere},
    )
    moments = lax.all_to_all(moments, "domain", 0, 0)
    return tuple(
        call(final_kernel, "combine", [members_f32, level], (moments, start, image, first, second))
    )


def solution(mesh):
    in_specs = (
        P("member", None, "domain"),
        P(None, "domain"),
        P(None, "domain"),
        P("domain"),
        P(),
        P(),
    )
    out_specs = (P("member", None, "domain"), P(None, "domain"))
    return jax.shard_map(local, mesh=mesh, in_specs=in_specs, out_specs=out_specs, check_vma=False)
```

time: 283 us -> 36.1 us (0.13)
  blocking collectives: 171 us -> 7.28 us
  waiting for transfers between devices: 78.3 us -> 4.23 us
  Pallas kernels: 0 us -> 6.83 us
  other arithmetic: 6.39 us -> 0 us
  matrix products: 5.07 us -> 0 us
  between operations: 4.89 us -> 0.71 us
    psum x6 -> x0, blocking collectives: 171 us -> none  [the longest x2 79.5 us: total_sum(): return lax.psum(value, ('member', 'domain'))]
    ppermute x24 -> x8, waiting for transfers between devices: 78.3 us -> 4.23 us  [the longest x6 4.22 us: from_partners(): lax.ppermute(value, axis, [(i, i ^ step) for i in range(size)])]
    all_to_all x0 -> x1, blocking collectives: none -> 7.28 us  [local(): moments = lax.all_to_all(moments, 'domain', 0, 0)]
    pallas_call x0 -> x8, Pallas kernels: none -> 6.83 us  [call(): pl.pallas_call(kernel, name=name, out_shape=list(outs), in_specs=[specs.g...]
    dot_general x6 -> x0, matrix products: 5.07 us -> none  [the longest x3 3.59 us: adjoint(): jnp.einsum('kl,mkh->mlh', vertical_map, smooth, precision=lax.Precision.H...]
    unnamed x10 -> x12, local copies, waits for them, and re-layouts: 0.3 us -> 3.73 us
    ppermute x24 -> x8, starting transfers between devices: 13.9 us -> 12.8 us  [the longest x6 9.39 us: from_partners(): lax.ppermute(value, axis, [(i, i ^ step) for i in range(size)])]
  transfers between devices with their start and end apart: 24 -> 8, of which waited for: 24 -> 5; matrix products, arithmetic and copies ran while one was open for 0% -> 0% of each run, Pallas kernels for 0% -> 10%
where the time goes in v2:
time: 36.1 us; the launch traced here: 35.6 us
  starting transfers between devices  12.8 us (35%)
  blocking collectives  7.28 us (20%)
  Pallas kernels  6.83 us (19%)
  waiting for transfers between devices  4.23 us (12%)
  local copies, waits for them, and re-layouts  3.73 us (10%)
  between operations  0.71 us (2%)
    ppermute x6, starting transfers between devices, from_partners(): lax.ppermute(value, axis, [(i, i ^ step) for i in range(size)])  9.39 us
    all_to_all x1, blocking collectives, local(): moments = lax.all_to_all(moments, 'domain', 0, 0)  7.28 us
    pallas_call x8, Pallas kernels, call(): pl.pallas_call(kernel, name=name, out_shape=list(outs), in_specs=[specs.g...  6.83 us
    ppermute x6, waiting for transfers between devices, from_partners(): lax.ppermute(value, axis, [(i, i ^ step) for i in range(size)])  4.22 us
    unnamed x12, local copies, waits for them, and re-layouts  3.73 us
    ppermute x1, starting transfers between devices, local(): after = lax.ppermute(high, 'domain', down)  2.95 us
  transfers between devices with their start and end apart: 8, of which 5 were waited for; matrix products, arithmetic and copies ran while one was open for 0% of the time, Pallas kernels for 10%

profile of v2, /device:TPU:0, one launch (start us, length us, event | category | flops | bytes accessed | tf_op | source)
XLA Modules:
  0.0 35.6 jit_solution(4402515255152152730)
XLA Ops:
  0.6 0.0 copy-start.4
  0.6 0.7 %copy-done.4 = s32[256]{0:T(256)S(1)} copy-done((s32[256]{0:T(256)S(1)}, s32[256]{0:T(256)}, u32[]{:S(2)}) %copy-start.4) | copy-done | bytes 1048
  1.3 0.0 copy-start
  1.3 0.9 %copy-done = bf16[25,16,256]{2,1,0:T(8,128)(2,1)S(1)} copy-done((bf16[25,16,256]{2,1,0:T(8,128)(2,1)S(1)}, bf16[25,16,256]{2,1,0:T(8,128)(2,1)}, u32[]{:S(2)}) %copy-start) | copy-done | bytes 204824
  2.2 0.0 copy-start.1
  2.2 0.7 %copy-done.1 = f32[16,256]{1,0:T(8,128)S(1)} copy-done((f32[16,256]{1,0:T(8,128)S(1)}, f32[16,256]{1,0:T(8,128)}, u32[]{:S(2)}) %copy-start.1) | copy-done | bytes 16408
  3.0 0.0 copy-start.2
  3.0 0.7 %copy-done.2 = f32[16,256]{1,0:T(8,128)S(1)} copy-done((f32[16,256]{1,0:T(8,128)S(1)}, f32[16,256]{1,0:T(8,128)}, u32[]{:S(2)}) %copy-start.2) | copy-done | bytes 16408
  3.7 0.5 %pack_edges.1 = (bf16[25,16,256]{2,1,0:T(8,128)(2,1)S(1)}, f32[2,16,256]{2,1,0:T(8,128)S(1)}, f32[7,16,128]{2,1,0:T(8,128)S(1)}, f32[7,16,128]{2,1,0:T(8,128)S(1)}) custom-call(bf16[25,16,256]{2,1,0:T(8,128)(2,1)S(1)} %copy-done, f32[16,256]{1,0:T(8,128)S(1)} %copy-done.1, f32[16,256]{1,0:T(8,128)S(1)} %copy-done.2, s32[1,256]{1,0:T(1,128)S(1)} %bitcast.5), custom_call_target="tpu_custom_call" | custom-call | flops 286720 | bytes 590848 | tf_op jit(solution)/shard_map/pack_edges/pallas_call | solution.py:285
  4.1 0.5 %collective-permute-start = (f32[7,16,128]{2,1,0:T(8,128)S(1)}, f32[7,16,128]{2,1,0:T(8,128)S(1)}, u32[]{:S(2)}, u32[]{:S(2)}) collective-permute-start(f32[7,16,128]{2,1,0:T(8,128)S(1)} %get-tuple-element.21.low_ref), channel_id=1, source_target_pairs={{0,1},{1,2},{2,3},{3,4},{4,5},{5,6},{6,7},{7,0},{8,9},{9,10},{10,1... | collective-permute-start | bytes 172040 | tf_op jit(solution)/shard_map/ppermute | solution.py:327
  4.6 2.9 %collective-permute-start.1 = (f32[7,16,128]{2,1,0:T(8,128)S(1)}, f32[7,16,128]{2,1,0:T(8,128)S(1)}, u32[]{:S(2)}, u32[]{:S(2)}) collective-permute-start(f32[7,16,128]{2,1,0:T(8,128)S(1)} %get-tuple-element.22.high_ref), channel_id=1, source_target_pairs={{1,0},{2,1},{3,2},{4,3},{5,4},{6,5},{7,6},{0,7},{9,8},{10,9},{11,1... | collective-permute-start | bytes 172040 | tf_op jit(solution)/shard_map/ppermute | solution.py:328
  7.6 0.0 copy-start.3
  7.6 0.0 copy-start.5
  7.6 0.7 %copy-done.3 = f32[16,16]{1,0:T(8,128)S(1)} copy-done((f32[16,16]{1,0:T(8,128)S(1)}, f32[16,16]{1,0:T(8,128)}, u32[]{:S(2)}) %copy-start.3) | copy-done | bytes 1048
  8.3 0.0 copy-done.5
  8.3 1.7 %first_inner.1 = (f32[3,16,128]{2,1,0:T(8,128)S(1)}, f32[16,16,128]{2,1,0:T(8,128)S(1)}, f32[16,16,128]{2,1,0:T(8,128)S(1)}, f32[16,256]{1,0:T(8,128)S(1)}) custom-call(f32[16]{0:T(128)S(1)} %copy-done.5, f32[16,16]{1,0:T(8,128)S(1)} %copy-done.3, bf16[25,16,256]{2,1,0:T(8,128)(2,1)S(1)} %get-tuple-element.20.members_ref, ...), custom_call_target="tpu_custom_call" | custom-call | flops 5120000 | bytes 541760 | tf_op jit(solution)/shard_map/first_inner/pallas_call | solution.py:285
  10.0 0.0 collective-permute-done.before_ref
  10.0 0.0 collective-permute-done.1.after_ref
  10.1 0.6 %first_edges.1 = (f32[7,16,128]{2,1,0:T(8,128)S(1)}, f32[2,16,128]{2,1,0:T(8,128)S(1)}, f32[16,384]{1,0:T(8,128)S(1)}) custom-call(f32[7,16,128]{2,1,0:T(8,128)S(1)} %get-tuple-element.21.low_ref, f32[7,16,128]{2,1,0:T(8,128)S(1)} %get-tuple-element.22.high_ref, f32[7,16,128]{2,1,0:T(8,128)S(1)} %collective-permute-done.before_ref, ...), custom_call_target="tpu_custom_call" | custom-call | flops 716800 | bytes 499712 | tf_op jit(solution)/shard_map/first_edges/pallas_call | solution.py:285
  10.7 4.3 %collective-permute-start.4 = (f32[16,384]{1,0:T(8,128)S(1)}, f32[16,384]{1,0:T(8,128)S(1)}, u32[]{:S(2)}, u32[]{:S(2)}) collective-permute-start(f32[16,384]{1,0:T(8,128)S(1)} %get-tuple-element.28.own_ref), channel_id=1, source_target_pairs={{0,24},{8,16},{16,8},{24,0},{1,25},{9,17},{17,9},{25,1},{2,26},{10... | collective-permute-start | bytes 73736 | tf_op jit(solution)/shard_map/ppermute | solution.py:303
  15.0 0.0 collective-permute-start.3
  15.0 0.6 %collective-permute-start.2 = (f32[16,384]{1,0:T(8,128)S(1)}, f32[16,384]{1,0:T(8,128)S(1)}, u32[]{:S(2)}, u32[]{:S(2)}) collective-permute-start(f32[16,384]{1,0:T(8,128)S(1)} %get-tuple-element.28.own_ref), channel_id=1, source_target_pairs={{0,8},{8,0},{16,24},{24,16},{1,9},{9,1},{17,25},{25,17},{2,10},{10... | collective-permute-start | bytes 73736 | tf_op jit(solution)/shard_map/ppermute | solution.py:303
  15.6 0.9 %start_vector.1._.start_ref = f32[25,16,256]{2,1,0:T(8,128)S(1)} custom-call(bf16[25,16,256]{2,1,0:T(8,128)(2,1)S(1)} %get-tuple-element.20.members_ref, f32[7,16,128]{2,1,0:T(8,128)S(1)} %get-tuple-element.26.edge_members_ref, f32[16,256]{1,0:T(8,128)S(1)} %slice_bitcast_fusion.field_ref, f32[16,128]{1,0:T(8,128)S(1)} %slice_bitcast_fusion.1.edge_field_ref, ...), custom_call_target="tpu_custom_call" | custom-call | flops 5120000 | bytes 851968 | tf_op jit(solution)/shard_map/start_vector/pallas_call | solution.py:285
  16.5 0.3 collective-permute-done.4.c_ref
  16.8 2.9 %collective-permute-done.3.b_ref = f32[16,384]{1,0:T(8,128)S(1)} collective-permute-done((f32[16,384]{1,0:T(8,128)S(1)}, f32[16,384]{1,0:T(8,128)S(1)}, u32[]{:S(2)}, u32[]{:S(2)}) %collective-permute-start.3) | collective-permute-done | bytes 24608 | tf_op jit(solution)/shard_map/ppermute | solution.py:303
  19.7 0.0 collective-permute-done.2.a_ref
  19.7 1.2 %second_apply.1 = (f32[16,256]{1,0:T(8,128)S(1)}, f32[16,256]{1,0:T(8,128)S(1)}, f32[16,128]{1,0:T(8,128)S(1)}, f32[16,256]{1,0:T(8,128)S(1)}) custom-call(bf16[25,16,256]{2,1,0:T(8,128)(2,1)S(1)} %get-tuple-element.20.members_ref, f32[7,16,128]{2,1,0:T(8,128)S(1)} %get-tuple-element.26.edge_members_ref, f32[2,16,256]{2,1,0:T(8,128)S(1)} %get-tuple-element.19.fields_ref, ...), custom_call_target="tpu_custom_call" | custom-call | flops 5836800 | bytes 1032192 | tf_op jit(solution)/shard_map/second_apply/pallas_call | solution.py:285
  20.9 1.5 %collective-permute-start.7 = (f32[16,256]{1,0:T(8,128)S(1)}, f32[16,256]{1,0:T(8,128)S(1)}, u32[]{:S(2)}, u32[]{:S(2)}) collective-permute-start(f32[16,256]{1,0:T(8,128)S(1)} %get-tuple-element.32.own_ref), channel_id=1, source_target_pairs={{0,24},{8,16},{16,8},{24,0},{1,25},{9,17},{17,9},{25,1},{2,26},{10... | collective-permute-start | bytes 49160 | tf_op jit(solution)/shard_map/ppermute | solution.py:303
  22.4 0.6 %collective-permute-start.6 = (f32[16,256]{1,0:T(8,128)S(1)}, f32[16,256]{1,0:T(8,128)S(1)}, u32[]{:S(2)}, u32[]{:S(2)}) collective-permute-start(f32[16,256]{1,0:T(8,128)S(1)} %get-tuple-element.32.own_ref), channel_id=1, source_target_pairs={{0,16},{8,24},{16,0},{24,8},{1,17},{9,25},{17,1},{25,9},{2,18},{10... | collective-permute-start | bytes 49160 | tf_op jit(solution)/shard_map/ppermute | solution.py:303
  23.1 2.3 %collective-permute-start.5 = (f32[16,256]{1,0:T(8,128)S(1)}, f32[16,256]{1,0:T(8,128)S(1)}, u32[]{:S(2)}, u32[]{:S(2)}) collective-permute-start(f32[16,256]{1,0:T(8,128)S(1)} %get-tuple-element.32.own_ref), channel_id=1, source_target_pairs={{0,8},{8,0},{16,24},{24,16},{1,9},{9,1},{17,25},{25,17},{2,10},{10... | collective-permute-start | bytes 49160 | tf_op jit(solution)/shard_map/ppermute | solution.py:303
  25.4 0.9 %image_vector.1._.image_ref = f32[25,16,256]{2,1,0:T(8,128)S(1)} custom-call(bf16[25,16,256]{2,1,0:T(8,128)(2,1)S(1)} %get-tuple-element.20.members_ref, f32[7,16,128]{2,1,0:T(8,128)S(1)} %get-tuple-element.26.edge_members_ref, f32[16,256]{1,0:T(8,128)S(1)} %get-tuple-element.31.field_ref.weighted_ref, f32[16,128]{1,0:T(8,128)S(1)} %get-tuple-element.33.edge_field_ref, ...), custom_call_target="tpu_custom_call" | custom-call | flops 5120000 | bytes 851968 | tf_op jit(solution)/shard_map/image_vector/pallas_call | solution.py:285
  26.2 0.3 collective-permute-done.7.c_ref
  26.5 0.6 %collective-permute-done.6.b_ref = f32[16,256]{1,0:T(8,128)S(1)} collective-permute-done((f32[16,256]{1,0:T(8,128)S(1)}, f32[16,256]{1,0:T(8,128)S(1)}, u32[]{:S(2)}, u32[]{:S(2)}) %collective-permute-start.6) | collective-permute-done | bytes 16416 | tf_op jit(solution)/shard_map/ppermute | solution.py:303
  27.1 0.2 collective-permute-done.5.a_ref
  27.3 0.2 moments.1
  27.4 7.3 %all_to_all.5.moments_ref = f32[8,1,128]{2,1,0:T(1,128)S(1)} all-to-all(f32[8,1,128]{2,1,0:T(1,128)S(1)} %get-tuple-element.34), channel_id=1, replica_groups=mesh['member'=4,'domain'=8] {'domain'}, dimensions={0} | all-to-all | bytes 8192 | tf_op jit(solution)/shard_map/all_to_all | solution.py:359
  34.7 0.9 %combine.1 = (f32[25,16,256]{2,1,0:T(8,128)}, f32[16,256]{1,0:T(8,128)}) custom-call(f32[8,1,128]{2,1,0:T(1,128)S(1)} %all_to_all.5.moments_ref, f32[25,16,256]{2,1,0:T(8,128)S(1)} %start_vector.1._.start_ref, f32[25,16,256]{2,1,0:T(8,128)S(1)} %image_vector.1._.image_ref, f32[16,256]{1,0:T(8,128)S(1)} %get-tuple-element.30.first_ref, ...), custom_call_target="tpu_custom_call" | custom-call | bytes 1282048 | tf_op jit(solution)/shard_map/combine/pallas_call | solution.py:285
  (2 shorter events, 0.0 us)
Async XLA Ops:
  0.6 0.7 %copy-start.4 = (s32[256]{0:T(256)S(1)}, s32[256]{0:T(256)}, u32[]{:S(2)}) copy-start(s32[256]{0:T(256)} %param.9) | copy-start | bytes 3076
  1.3 0.9 %copy-start = (bf16[25,16,256]{2,1,0:T(8,128)(2,1)S(1)}, bf16[25,16,256]{2,1,0:T(8,128)(2,1)}, u32[]{:S(2)}) copy-start(bf16[25,16,256]{2,1,0:T(8,128)(2,1)} %members_hbm.1) | copy-start | bytes 614404
  2.2 0.7 %copy-start.1 = (f32[16,256]{1,0:T(8,128)S(1)}, f32[16,256]{1,0:T(8,128)}, u32[]{:S(2)}) copy-start(f32[16,256]{1,0:T(8,128)} %innovations_hbm.1) | copy-start | bytes 49156
  3.0 0.7 %copy-start.2 = (f32[16,256]{1,0:T(8,128)S(1)}, f32[16,256]{1,0:T(8,128)}, u32[]{:S(2)}) copy-start(f32[16,256]{1,0:T(8,128)} %precision_hbm.1) | copy-start | bytes 49156
  4.1 5.9 %collective-permute-start = (f32[7,16,128]{2,1,0:T(8,128)S(1)}, f32[7,16,128]{2,1,0:T(8,128)S(1)}, u32[]{:S(2)}, u32[]{:S(2)}) collective-permute-start(f32[7,16,128]{2,1,0:T(8,128)S(1)} %get-tuple-element.21.low_ref), channel_id=1, source_target_pairs={{0,1},{1,2},{2,3},{3,4},{4,5},{5,6},{6,7},{7,0},{8,9},{9,10},{10,1... | collective-permute-start | bytes 172040 | tf_op jit(solution)/shard_map/ppermute | solution.py:327
  4.6 5.4 %collective-permute-start.1 = (f32[7,16,128]{2,1,0:T(8,128)S(1)}, f32[7,16,128]{2,1,0:T(8,128)S(1)}, u32[]{:S(2)}, u32[]{:S(2)}) collective-permute-start(f32[7,16,128]{2,1,0:T(8,128)S(1)} %get-tuple-element.22.high_ref), channel_id=1, source_target_pairs={{1,0},{2,1},{3,2},{4,3},{5,4},{6,5},{7,6},{0,7},{9,8},{10,9},{11,1... | collective-permute-start | bytes 172040 | tf_op jit(solution)/shard_map/ppermute | solution.py:328
  7.6 0.7 %copy-start.3 = (f32[16,16]{1,0:T(8,128)S(1)}, f32[16,16]{1,0:T(8,128)}, u32[]{:S(2)}) copy-start(f32[16,16]{1,0:T(8,128)} %map_ref.1) | copy-start | bytes 3076
  7.6 0.7 %copy-start.5 = (f32[16]{0:T(128)S(1)}, f32[16]{0:T(128)}, u32[]{:S(2)}) copy-start(f32[16]{0:T(128)} %diffusivity_ref.1) | copy-start | bytes 196
  10.7 6.1 %collective-permute-start.4 = (f32[16,384]{1,0:T(8,128)S(1)}, f32[16,384]{1,0:T(8,128)S(1)}, u32[]{:S(2)}, u32[]{:S(2)}) collective-permute-start(f32[16,384]{1,0:T(8,128)S(1)} %get-tuple-element.28.own_ref), channel_id=1, source_target_pairs={{0,24},{8,16},{16,8},{24,0},{1,25},{9,17},{17,9},{25,1},{2,26},{10... | collective-permute-start | bytes 73736 | tf_op jit(solution)/shard_map/ppermute | solution.py:303
  15.0 4.7 %collective-permute-start.3 = (f32[16,384]{1,0:T(8,128)S(1)}, f32[16,384]{1,0:T(8,128)S(1)}, u32[]{:S(2)}, u32[]{:S(2)}) collective-permute-start(f32[16,384]{1,0:T(8,128)S(1)} %get-tuple-element.28.own_ref), channel_id=1, source_target_pairs={{0,16},{8,24},{16,0},{24,8},{1,17},{9,25},{17,1},{25,9},{2,18},{10... | collective-permute-start | bytes 73736 | tf_op jit(solution)/shard_map/ppermute | solution.py:303
  15.0 4.7 %collective-permute-start.2 = (f32[16,384]{1,0:T(8,128)S(1)}, f32[16,384]{1,0:T(8,128)S(1)}, u32[]{:S(2)}, u32[]{:S(2)}) collective-permute-start(f32[16,384]{1,0:T(8,128)S(1)} %get-tuple-element.28.own_ref), channel_id=1, source_target_pairs={{0,8},{8,0},{16,24},{24,16},{1,9},{9,1},{17,25},{25,17},{2,10},{10... | collective-permute-start | bytes 73736 | tf_op jit(solution)/shard_map/ppermute | solution.py:303
  20.9 5.6 %collective-permute-start.7 = (f32[16,256]{1,0:T(8,128)S(1)}, f32[16,256]{1,0:T(8,128)S(1)}, u32[]{:S(2)}, u32[]{:S(2)}) collective-permute-start(f32[16,256]{1,0:T(8,128)S(1)} %get-tuple-element.32.own_ref), channel_id=1, source_target_pairs={{0,24},{8,16},{16,8},{24,0},{1,25},{9,17},{17,9},{25,1},{2,26},{10... | collective-permute-start | bytes 49160 | tf_op jit(solution)/shard_map/ppermute | solution.py:303
  22.4 4.7 %collective-permute-start.6 = (f32[16,256]{1,0:T(8,128)S(1)}, f32[16,256]{1,0:T(8,128)S(1)}, u32[]{:S(2)}, u32[]{:S(2)}) collective-permute-start(f32[16,256]{1,0:T(8,128)S(1)} %get-tuple-element.32.own_ref), channel_id=1, source_target_pairs={{0,16},{8,24},{16,0},{24,8},{1,17},{9,25},{17,1},{25,9},{2,18},{10... | collective-permute-start | bytes 49160 | tf_op jit(solution)/shard_map/ppermute | solution.py:303
  23.1 4.2 %collective-permute-start.5 = (f32[16,256]{1,0:T(8,128)S(1)}, f32[16,256]{1,0:T(8,128)S(1)}, u32[]{:S(2)}, u32[]{:S(2)}) collective-permute-start(f32[16,256]{1,0:T(8,128)S(1)} %get-tuple-element.32.own_ref), channel_id=1, source_target_pairs={{0,8},{8,0},{16,24},{24,16},{1,9},{9,1},{17,25},{25,17},{2,10},{10... | collective-permute-start | bytes 49160 | tf_op jit(solution)/shard_map/ppermute | solution.py:303

commit v3 on v2

--- a/solution.py
+++ b/solution.py
@@ -31,12 +31,11 @@
     return column if copies == 1 else jnp.concatenate([column] * copies, axis=-1)
 
 
-def level_column(diffusivity_ref, levels):
-    row = lax.broadcasted_iota(jnp.int32, (levels, LANES), 0)
-    column = jnp.zeros((levels, LANES), F32)
-    for level in range(levels):
-        column = jnp.where(row == level, diffusivity_ref[level], column)
-    return column
+def level_column(row):
+    levels = row.shape[1]
+    square = jnp.broadcast_to(row, (levels, levels))
+    own = lax.broadcasted_iota(jnp.int32, square.shape, 0) == lane_index(square.shape)
+    return jnp.broadcast_to(jnp.sum(jnp.where(own, square, 0.0), axis=1, keepdims=True), (levels, LANES))
 
 
 def smooth(field, taps):
@@ -88,6 +87,10 @@
     return jnp.where(lane < HALO, first, jnp.where(lane >= LANES - HALO, last, 0.0))
 
 
+def added(total, term):
+    return term if total is None else total + term
+
+
 def patch(main, edge, width, slot=0):
     size = main.shape[-1]
     first = lane_roll(edge, -(slot * SLOT + HALO))
@@ -99,7 +102,8 @@
 
 def pack_kernel(
     members_hbm, innovations_hbm, precision_hbm, counts_hbm,
-    members_ref, fields_ref, low_ref, high_ref, innovations_ref, precision_ref, counts_ref, sems,
+    low_ref, high_ref, low_message_ref, high_message_ref,
+    members_ref, innovations_ref, precision_ref, counts_ref, sems,
 ):
     copies = [
         pltpu.make_async_copy(source, target, sems.at[i])
@@ -117,30 +121,39 @@
     for copy in copies[1:]:
         copy.wait()
     weight = counts_ref[...].astype(F32) * precision_ref[...]
-    fields_ref[0] = weight * innovations_ref[...]
-    fields_ref[1] = weight
+    fields = (weight * innovations_ref[...], weight)
     copies[0].wait()
     count, levels, size = members_ref.shape
     lane = lane_index((levels, LANES))
+    at = lane % SLOT
+    low_message, high_message = [None] * low_message_ref.shape[0], [None] * low_message_ref.shape[0]
     for tile in range(low_ref.shape[0]):
-        low, high = jnp.zeros((levels, LANES), F32), jnp.zeros((levels, LANES), F32)
+        low = high = None
         for slot in range(SLOTS):
             m = tile * SLOTS + slot
             if m < count:
                 first, last = members_ref[m, :, :LANES].astype(F32), members_ref[m, :, size - LANES :].astype(F32)
             elif m < count + 2:
-                first, last = fields_ref[m - count, :, :LANES], fields_ref[m - count, :, size - LANES :]
+                first, last = fields[m - count][:, :LANES], fields[m - count][:, size - LANES :]
             else:
                 continue
             ends = ends_of(first, last, lane)
-            low = low + lane_roll(ends, slot * SLOT + HALO)
-            high = high + lane_roll(ends, slot * SLOT + 3 * HALO)
+            low = added(low, lane_roll(ends, slot * SLOT + HALO))
+            high = added(high, lane_roll(ends, slot * SLOT + 3 * HALO))
         low_ref[tile] = low
         high_ref[tile] = high
+        place, shift = divmod(tile, SLOT // HALO)
+        low_message[place] = added(low_message[place], lane_roll(jnp.where(at < HALO, low, 0.0), shift * HALO))
+        high = lane_roll(jnp.where(at >= 3 * HALO, high, 0.0), shift * HALO - 3 * HALO)
+        high_message[place] = added(high_message[place], high)
+    for place in range(low_message_ref.shape[0]):
+        low_message_ref[place] = low_message[place]
+        high_message_ref[place] = high_message[place]
 
 
 def main_kernel(
-    diffusivity_ref, map_ref, members_ref, fields_ref, taps_ref, square_ref, adjoint_ref, out_ref, x_ref, y_ref
+    diffusivity_ref, map_ref, members_ref, innovations_ref, precision_ref, counts_ref,
+    taps_ref, square_ref, adjoint_ref, source_ref, weight_ref, out_ref, x_ref, y_ref,
 ):
     levels = members_ref.shape[1]
     matrix = map_ref[...]
@@ -150,32 +163,38 @@
     for k in range(levels):
         square_ref[k] = jnp.broadcast_to(square[:, k : k + 1], (levels, LANES))
         adjoint_ref[k] = jnp.broadcast_to(turned[:, k : k + 1], (levels, LANES))
-    coef = level_column(diffusivity_ref, levels)
+    coef = level_column(diffusivity_ref[...])
     keep = 1.0 - 2.0 * coef
     taps_ref[0] = keep * keep + 2.0 * coef * coef
     taps_ref[1] = 2.0 * keep * coef
     taps_ref[2] = coef * coef
-    (out_ref[...],) = apply_ensemble([(members_ref, fields_ref[0])], taps_ref, square_ref, [(x_ref, y_ref)])
+    weight = counts_ref[...].astype(F32) * precision_ref[...]
+    source = weight * innovations_ref[...]
+    source_ref[...], weight_ref[...] = source, weight
+    (out_ref[...],) = apply_ensemble([(members_ref, source)], taps_ref, square_ref, [(x_ref, y_ref)])
 
 
 def edge_kernel(
     count, low_ref, high_ref, before_ref, after_ref, taps_ref, square_ref, main_ref,
-    edge_members_ref, edge_fields_ref, out_ref, x_ref, y_ref,
+    edge_members_ref, edge_source_ref, edge_weight_ref, out_ref, x_ref, y_ref,
 ):
     tiles, levels, _ = low_ref.shape
     size = main_ref.shape[1]
     lane = lane_index((levels, LANES))
     at, slot_of = lane % SLOT, lane // SLOT
     for tile in range(tiles):
+        place, shift = divmod(tile, SLOT // HALO)
+        before = lane_roll(before_ref[place], -shift * HALO)
+        after = lane_roll(after_ref[place], (3 - shift) * HALO)
         own = jnp.where(at >= 2 * HALO, high_ref[tile], low_ref[tile])
-        value = jnp.where(at >= 3 * HALO, after_ref[tile], jnp.where(at < HALO, before_ref[tile], own))
-        for i in range(2):
+        value = jnp.where(at >= 3 * HALO, after, jnp.where(at < HALO, before, own))
+        for i, field_ref in enumerate((edge_source_ref, edge_weight_ref)):
             place, slot = divmod(count + i, SLOTS)
             if place == tile:
-                edge_fields_ref[i] = all_slots(jnp.where(slot_of == slot, value, 0.0))
+                field_ref[...] = all_slots(jnp.where(slot_of == slot, value, 0.0))
         held = min(max(count - tile * SLOTS, 0), SLOTS)
         edge_members_ref[tile] = value if held == SLOTS else jnp.where(slot_of < held, value, 0.0)
-    (edge,) = apply_ensemble([(edge_members_ref, edge_fields_ref[0])], taps_ref, square_ref, [(x_ref, y_ref)])
+    (edge,) = apply_ensemble([(edge_members_ref, edge_source_ref[...])], taps_ref, square_ref, [(x_ref, y_ref)])
     edge = all_slots(edge)
     out_ref[:, :size] = patch(main_ref[...], edge, REACH)
     out_ref[:, size:] = edge
@@ -186,7 +205,7 @@
 
 
 def second_kernel(
-    members_ref, edge_members_ref, fields_ref, edge_fields_ref, taps_ref, square_ref, own_ref, a_ref, b_ref, c_ref, _,
+    members_ref, edge_members_ref, weight_ref, edge_weight_ref, taps_ref, square_ref, own_ref, a_ref, b_ref, c_ref, _,
     first_ref, weighted_ref, edge_weighted_ref, out_ref, x_ref, y_ref, edge_x_ref, edge_y_ref,
 ):
     _, levels, size = members_ref.shape
@@ -198,8 +217,8 @@
     own = jnp.where(lane >= 2 * HALO, lane_roll(ends, 3 * HALO), lane_roll(ends, HALO))
     own = all_slots(jnp.where(lane < SLOT, own, 0.0))
     edge = jnp.where((at >= HALO) & (at < 3 * HALO), own, edge)
-    weighted = fields_ref[1] * first
-    edge_weighted = edge_fields_ref[1] * edge
+    weighted = weight_ref[...] * first
+    edge_weighted = edge_weight_ref[...] * edge
     first_ref[...] = first
     weighted_ref[...] = weighted
     edge_weighted_ref[...] = edge_weighted
@@ -211,10 +230,10 @@
 
 
 def moments_kernel(
-    fields_ref, first_ref, weighted_ref, own_ref, a_ref, b_ref, c_ref, _, second_ref, moments_ref
+    source_ref, weight_ref, first_ref, weighted_ref, own_ref, a_ref, b_ref, c_ref, _, second_ref, moments_ref
 ):
     size = first_ref.shape[1]
-    source, weight = fields_ref[0], fields_ref[1]
+    source, weight = source_ref[...], weight_ref[...]
     first, weighted = first_ref[...], weighted_ref[...]
     second = tree_sum(own_ref, a_ref, b_ref, c_ref)
     second_ref[...] = second
@@ -227,7 +246,7 @@
         row = row + lane_roll(row, LANES // 2)
         row = row + lane_roll(row, LANES // 4)
         out = jnp.where((lane >= i * width) & (lane < (i + 1) * width), row, out)
-    moments_ref[...] = jnp.broadcast_to(out[None], moments_ref.shape)
+    moments_ref[...] = out
 
 
 def adjoint_kernel(
@@ -244,10 +263,12 @@
         out_ref[m] = mixed(adjoint_ref, x_ref.at[m])
 
 
-def final_kernel(moments_ref, start_ref, image_ref, first_ref, second_ref, control_ref, increment_ref):
+def final_kernel(
+    own_ref, a_ref, b_ref, c_ref, start_ref, image_ref, first_ref, second_ref, control_ref, increment_ref
+):
     lane = lane_index((1, LANES))
     width = LANES // 4
-    row = jnp.sum(moments_ref[...], axis=0)
+    row = tree_sum(own_ref, a_ref, b_ref, c_ref)
     sums = [
         jnp.sum(jnp.where((lane >= i * width) & (lane < (i + 1) * width), row, 0.0), axis=1, keepdims=True)
         for i in range(4)
@@ -275,11 +296,7 @@
     return pl.BlockSpec(memory_space=pl.ANY)
 
 
-def smem():
-    return pl.BlockSpec(memory_space=pltpu.SMEM)
-
-
-def call(kernel, name, outs, args, scratch=(), specs=None, flops=0):
+def call(kernel, name, outs, args, scratch=(), specs=None, flops=0, limit=VMEM_LIMIT):
     specs = specs or {}
     moved = sum(a.size * a.dtype.itemsize for a in (*args, *outs))
     return pl.pallas_call(
@@ -290,7 +307,7 @@
         out_specs=[vmem()] * len(outs),
         scratch_shapes=list(scratch),
         cost_estimate=pl.CostEstimate(flops=flops, bytes_accessed=moved, transcendentals=0),
-        compiler_params=pltpu.CompilerParams(vmem_limit_bytes=VMEM_LIMIT),
+        compiler_params=pltpu.CompilerParams(vmem_limit_bytes=limit),
     )(*args)
 
 
@@ -301,6 +318,22 @@
 def from_partners(value, axis):
     size = lax.axis_size(axis)
     return [lax.ppermute(value, axis, [(i, i ^ step) for i in range(size)]) for step in range(1, size)]
+
+
+def partner(value, axis, step):
+    return lax.ppermute(value, axis, [(i, i ^ step) for i in range(lax.axis_size(axis))])
+
+
+def domain_terms(value, axis):
+    size = lax.axis_size(axis)
+    value, step = value + partner(value, axis, 1), 2
+    while 4 * step < size:
+        if (size // step).bit_length() % 2:
+            terms = [partner(value, axis, k * step) for k in (1, 2, 3)]
+            value, step = (value + terms[0]) + (terms[1] + terms[2]), 4 * step
+        else:
+            value, step = value + partner(value, axis, step), 2 * step
+    return [value, *(partner(value, axis, k * step) for k in (1, 2, 3))]
 
 
 def local(perturbations, innovations, precision_field, obs_counts, vertical_map, diffusivity):
@@ -312,53 +345,60 @@
     level = shape_of(levels, size)
     members_f32 = shape_of(count, levels, size)
     edge_tiles = shape_of(tiles, levels, LANES)
+    edge_row = shape_of(1, LANES)
+    edge_level = shape_of(levels, LANES)
+    message = shape_of(-(-tiles * HALO // SLOT), levels, LANES)
     column = shape_of(levels, levels, LANES)
     work, edge_work = count * levels * size * 50, tiles * levels * LANES * 50
     scratch = [pltpu.VMEM((count, levels, size), F32)] * 2
     edge_scratch = [pltpu.VMEM((tiles, levels, LANES), F32)] * 2
 
-    members, fields, low, high = call(
-        pack_kernel, "pack_edges",
-        [shape_of(count, levels, size, dtype=perturbations.dtype), shape_of(2, levels, size), edge_tiles, edge_tiles],
-        (perturbations, innovations, precision_field, obs_counts.reshape(1, size)),
-        [pltpu.VMEM((levels, size), F32)] * 2 + [pltpu.VMEM((1, size), jnp.int32), pltpu.SemaphoreType.DMA((4,))],
-        dict.fromkeys(range(4), elsewhere), tiles * levels * LANES * 20,
-    )
-    before = lax.ppermute(low, "domain", up)
-    after = lax.ppermute(high, "domain", down)
-    taps, square, mapped, main = call(
-        main_kernel, "first_inner", [shape_of(3, levels, LANES), column, column, level],
-        (diffusivity, vertical_map, members, fields), scratch, {0: smem}, work,
-    )
-    edge_members, edge_fields, part = call(
+    counts = obs_counts.reshape(1, size)
+    low, high, low_message, high_message = call(
+        pack_kernel, "pack_edges", [edge_tiles, edge_tiles, message, message],
+        (perturbations, innovations, precision_field, counts),
+        [
+            pltpu.VMEM((count, levels, size), perturbations.dtype), pltpu.VMEM((levels, size), F32),
+            pltpu.VMEM((levels, size), F32), pltpu.VMEM((1, size), jnp.int32), pltpu.SemaphoreType.DMA((4,)),
+        ],
+        dict.fromkeys(range(4), elsewhere), tiles * levels * LANES * 20, None,
+    )
+    before = lax.ppermute(low_message, "domain", up)
+    after = lax.ppermute(high_message, "domain", down)
+    taps, square, mapped, source, weight, main = call(
+        main_kernel, "first_inner", [shape_of(3, levels, LANES), column, column, level, level, level],
+        (diffusivity.reshape(1, levels), vertical_map, perturbations, innovations, precision_field, counts),
+        scratch, flops=work,
+    )
+    edge_members, edge_source, edge_weight, part = call(
         functools.partial(edge_kernel, count), "first_edges",
-        [edge_tiles, shape_of(2, levels, LANES), shape_of(levels, size + LANES)],
+        [edge_tiles, edge_level, edge_level, shape_of(levels, size + LANES)],
         (low, high, before, after, taps, square, main), edge_scratch, flops=edge_work,
     )
 
     def adjoint(name, field, edge_field):
         (out,) = call(
-            adjoint_kernel, name, [members_f32], (members, edge_members, field, edge_field, taps, mapped),
+            adjoint_kernel, name, [members_f32], (perturbations, edge_members, field, edge_field, taps, mapped),
             [scratch[0], edge_scratch[0]], flops=work,
         )
         return out
 
     others = from_partners(part, "member")
-    start = adjoint("start_vector", fields[0], edge_fields[0])
+    start = adjoint("start_vector", source, edge_source)
     first, weighted, edge_weighted, part = call(
-        second_kernel, "second_apply", [level, level, shape_of(levels, LANES), level],
-        (members, edge_members, fields, edge_fields, taps, square, part, *others, start),
+        second_kernel, "second_apply", [level, level, edge_level, level],
+        (perturbations, edge_members, weight, edge_weight, taps, square, part, *others, start),
         scratch + edge_scratch, {10: elsewhere}, work + edge_work,
     )
     others = from_partners(part, "member")
     image = adjoint("image_vector", weighted, edge_weighted)
     second, moments = call(
-        moments_kernel, "moments", [level, shape_of(domains, 1, LANES)],
-        (fields, first, weighted, part, *others, image), (), {7: elsewhere},
-    )
-    moments = lax.all_to_all(moments, "domain", 0, 0)
+        moments_kernel, "moments", [level, edge_row],
+        (source, weight, first, weighted, part, *others, image), (), {8: elsewhere},
+    )
+    moments = domain_terms(moments, "domain")
     return tuple(
-        call(final_kernel, "combine", [members_f32, level], (moments, start, image, first, second))
+        call(final_kernel, "combine", [members_f32, level], (*moments, start, image, first, second))
     )
 
 

time: 36.1 us -> 33.5 us (0.928)
  blocking collectives: 7.28 us -> 0 us
  starting transfers between devices: 12.8 us -> 16.3 us
  waiting for transfers between devices: 4.23 us -> 7.65 us
  local copies, waits for them, and re-layouts: 3.73 us -> 0.7 us
  Pallas kernels: 6.83 us -> 7.89 us
    all_to_all x1 -> x0, blocking collectives: 7.28 us -> none  [local(): moments = lax.all_to_all(moments, 'domain', 0, 0)]
    ppermute x2 -> x6, starting transfers between devices: 3.45 us -> 6.96 us  [the longest x4 3.5 us: partner(): lax.ppermute(value, axis, [(i, i ^ step) for i in range(lax.axis_size(axi...]
    ppermute x2 -> x6, waiting for transfers between devices: 0.01 us -> 3.41 us  [the longest x4 3.4 us: partner(): lax.ppermute(value, axis, [(i, i ^ step) for i in range(lax.axis_size(axi...]
    unnamed x12 -> x16, local copies, waits for them, and re-layouts: 3.73 us -> 0.7 us
    pallas_call x8, Pallas kernels: 6.83 us -> 7.89 us  [call(): pl.pallas_call(kernel, name=name, out_shape=list(outs), in_specs=[specs.g...]
  transfers between devices with their start and end apart: 8 -> 12, of which waited for: 5 -> 9; matrix products, arithmetic and copies ran while one was open for 0% -> 0% of each run, Pallas kernels for 10% -> 9%
where the time goes in v3:
time: 33.5 us; the launch traced here: 33.4 us
  starting transfers between devices  16.3 us (49%)
  Pallas kernels  7.89 us (24%)
  waiting for transfers between devices  7.65 us (23%)
  between operations  0.77 us (2%)
  local copies, waits for them, and re-layouts  0.7 us (2%)
    ppermute x6, starting transfers between devices, from_partners(): lax.ppermute(value, axis, [(i, i ^ step) for i in range(size)])  9.38 us
    pallas_call x8, Pallas kernels, call(): pl.pallas_call(kernel, name=name, out_shape=list(outs), in_specs=[specs.g...  7.89 us
    ppermute x6, waiting for transfers between devices, from_partners(): lax.ppermute(value, axis, [(i, i ^ step) for i in range(size)])  4.24 us
    ppermute x4, starting transfers between devices, partner(): lax.ppermute(value, axis, [(i, i ^ step) for i in range(lax.axis_size(axi...  3.5 us
    ppermute x4, waiting for transfers between devices, partner(): lax.ppermute(value, axis, [(i, i ^ step) for i in range(lax.axis_size(axi...  3.4 us
    ppermute x1, starting transfers between devices, local(): after = lax.ppermute(high_message, 'domain', down)  2.96 us
    unnamed x16, local copies, waits for them, and re-layouts  0.7 us
  transfers between devices with their start and end apart: 12, of which 9 were waited for; matrix products, arithmetic and copies ran while one was open for 0% of the time, Pallas kernels for 9%

profile of v3, /device:TPU:0, one launch (start us, length us, event | category | flops | bytes accessed | tf_op | source)
XLA Modules:
  0.0 33.4 jit_solution(12622097707202467675)
XLA Ops:
  0.6 0.0 copy-start
  0.6 0.0 copy-start.1
  0.7 0.0 copy-start.2
  0.7 0.0 copy-start.5
  0.7 1.8 %pack_edges.1 = (f32[7,16,128]{2,1,0:T(8,128)}, f32[7,16,128]{2,1,0:T(8,128)}, f32[2,16,128]{2,1,0:T(8,128)}, f32[2,16,128]{2,1,0:T(8,128)}) custom-call(bf16[25,16,256]{2,1,0:T(8,128)(2,1)} %members_ref.7, f32[16,256]{1,0:T(8,128)} %innovations_hbm.1, f32[16,256]{1,0:T(8,128)} %precision_hbm.1, s32[1,256]{1,0:T(1,128)} %bitcast.2), custom_call_target="tpu_custom_call" | custom-call | flops 286720 | bytes 386048 | tf_op jit(solution)/shard_map/pack_edges/pallas_call | solution.py:302
  2.5 0.5 %collective-permute-start = (f32[2,16,128]{2,1,0:T(8,128)}, f32[2,16,128]{2,1,0:T(8,128)S(1)}, u32[]{:S(2)}, u32[]{:S(2)}) collective-permute-start(f32[2,16,128]{2,1,0:T(8,128)} %get-tuple-element.26), channel_id=1, source_target_pairs={{0,1},{1,2},{2,3},{3,4},{4,5},{5,6},{6,7},{7,0},{8,9},{9,10},{10,1... | collective-permute-start | bytes 49160 | tf_op jit(solution)/shard_map/ppermute | solution.py:366
  3.0 0.0 copy-start.7
  3.0 3.0 %collective-permute-start.1 = (f32[2,16,128]{2,1,0:T(8,128)}, f32[2,16,128]{2,1,0:T(8,128)S(1)}, u32[]{:S(2)}, u32[]{:S(2)}) collective-permute-start(f32[2,16,128]{2,1,0:T(8,128)} %get-tuple-element.27), channel_id=1, source_target_pairs={{1,0},{2,1},{3,2},{4,3},{5,4},{6,5},{7,6},{0,7},{9,8},{10,9},{11,1... | collective-permute-start | bytes 49160 | tf_op jit(solution)/shard_map/ppermute | solution.py:367
  6.0 0.0 copy-done
  6.0 0.0 copy-done.1
  6.0 0.0 copy-done.2
  6.0 0.0 copy-done.5
  6.0 0.0 copy-done.7
  6.0 0.0 copy-start.6
  6.0 0.7 %copy-done.6 = s32[256]{0:T(256)S(1)} copy-done((s32[256]{0:T(256)S(1)}, s32[256]{0:T(256)}, u32[]{:S(2)}) %copy-start.6) | copy-done | bytes 1048
  6.7 0.0 copy-start.3
  6.7 0.0 copy-start.4
  6.7 1.3 %first_inner.1 = (f32[3,16,128]{2,1,0:T(8,128)S(1)}, f32[16,16,128]{2,1,0:T(8,128)S(1)}, f32[16,16,128]{2,1,0:T(8,128)S(1)}, f32[16,256]{1,0:T(8,128)S(1)}, f32[...) custom-call(f32[1,16]{1,0:T(1,128)S(1)} %bitcast.4, f32[16,16]{1,0:T(8,128)S(1)} %copy-done.5, bf16[25,16,256]{2,1,0:T(8,128)(2,1)S(1)} %copy-done, ...), custom_call_target="tpu_custom_call" | custom-call | flops 5120000 | bytes 575552 | tf_op jit(solution)/shard_map/first_inner/pallas_call | solution.py:302
  8.0 0.0 collective-permute-done.before_ref
  8.0 0.0 collective-permute-done.1.after_ref
  8.0 0.0 copy-done.3
  8.0 0.0 copy-done.4
  8.0 0.7 %first_edges.1 = (f32[7,16,128]{2,1,0:T(8,128)S(1)}, f32[16,128]{1,0:T(8,128)S(1)}, f32[16,128]{1,0:T(8,128)S(1)}, f32[16,384]{1,0:T(8,128)S(1)}) custom-call(f32[7,16,128]{2,1,0:T(8,128)S(1)} %copy-done.3, f32[7,16,128]{2,1,0:T(8,128)S(1)} %copy-done.4, f32[2,16,128]{2,1,0:T(8,128)S(1)} %collective-permute-done.before_ref, ...), custom_call_target="tpu_custom_call" | custom-call | flops 716800 | bytes 417792 | tf_op jit(solution)/shard_map/first_edges/pallas_call | solution.py:302
  8.7 4.3 %collective-permute-start.4 = (f32[16,384]{1,0:T(8,128)S(1)}, f32[16,384]{1,0:T(8,128)S(1)}, u32[]{:S(2)}, u32[]{:S(2)}) collective-permute-start(f32[16,384]{1,0:T(8,128)S(1)} %get-tuple-element.33.own_ref), channel_id=1, source_target_pairs={{0,24},{8,16},{16,8},{24,0},{1,25},{9,17},{17,9},{25,1},{2,26},{10... | collective-permute-start | bytes 73736 | tf_op jit(solution)/shard_map/ppermute | solution.py:320
  13.0 0.0 collective-permute-start.3
  13.0 0.6 %collective-permute-start.2 = (f32[16,384]{1,0:T(8,128)S(1)}, f32[16,384]{1,0:T(8,128)S(1)}, u32[]{:S(2)}, u32[]{:S(2)}) collective-permute-start(f32[16,384]{1,0:T(8,128)S(1)} %get-tuple-element.33.own_ref), channel_id=1, source_target_pairs={{0,8},{8,0},{16,24},{24,16},{1,9},{9,1},{17,25},{25,17},{2,10},{10... | collective-permute-start | bytes 73736 | tf_op jit(solution)/shard_map/ppermute | solution.py:320
  13.6 0.9 %start_vector.1._.start_ref = f32[25,16,256]{2,1,0:T(8,128)S(1)} custom-call(bf16[25,16,256]{2,1,0:T(8,128)(2,1)S(1)} %copy-done, f32[7,16,128]{2,1,0:T(8,128)S(1)} %get-tuple-element.31.edge_members_ref, f32[16,256]{1,0:T(8,128)S(1)} %get-tuple-element.22.field_ref.source_ref, f32[16,128]{1,0:T(8,128)S(1)} %get-tuple-element.34.edge_field_ref, ...), custom_call_target="tpu_custom_call" | custom-call | flops 5120000 | bytes 851968 | tf_op jit(solution)/shard_map/start_vector/pallas_call | solution.py:302
  14.5 0.3 collective-permute-done.4.c_ref
  14.8 2.9 %collective-permute-done.3.b_ref = f32[16,384]{1,0:T(8,128)S(1)} collective-permute-done((f32[16,384]{1,0:T(8,128)S(1)}, f32[16,384]{1,0:T(8,128)S(1)}, u32[]{:S(2)}, u32[]{:S(2)}) %collective-permute-start.3) | collective-permute-done | bytes 24608 | tf_op jit(solution)/shard_map/ppermute | solution.py:320
  17.7 0.0 collective-permute-done.2.a_ref
  17.7 1.3 %second_apply.1 = (f32[16,256]{1,0:T(8,128)S(1)}, f32[16,256]{1,0:T(8,128)S(1)}, f32[16,128]{1,0:T(8,128)S(1)}, f32[16,256]{1,0:T(8,128)S(1)}) custom-call(bf16[25,16,256]{2,1,0:T(8,128)(2,1)S(1)} %copy-done, f32[7,16,128]{2,1,0:T(8,128)S(1)} %get-tuple-element.31.edge_members_ref, f32[16,256]{1,0:T(8,128)S(1)} %get-tuple-element.23.weight_ref, ...), custom_call_target="tpu_custom_call" | custom-call | flops 5836800 | bytes 1007616 | tf_op jit(solution)/shard_map/second_apply/pallas_call | solution.py:302
  19.0 1.5 %collective-permute-start.7 = (f32[16,256]{1,0:T(8,128)S(1)}, f32[16,256]{1,0:T(8,128)S(1)}, u32[]{:S(2)}, u32[]{:S(2)}) collective-permute-start(f32[16,256]{1,0:T(8,128)S(1)} %get-tuple-element.38.own_ref), channel_id=1, source_target_pairs={{0,24},{8,16},{16,8},{24,0},{1,25},{9,17},{17,9},{25,1},{2,26},{10... | collective-permute-start | bytes 49160 | tf_op jit(solution)/shard_map/ppermute | solution.py:320
  20.6 0.6 %collective-permute-start.6 = (f32[16,256]{1,0:T(8,128)S(1)}, f32[16,256]{1,0:T(8,128)S(1)}, u32[]{:S(2)}, u32[]{:S(2)}) collective-permute-start(f32[16,256]{1,0:T(8,128)S(1)} %get-tuple-element.38.own_ref), channel_id=1, source_target_pairs={{0,16},{8,24},{16,0},{24,8},{1,17},{9,25},{17,1},{25,9},{2,18},{10... | collective-permute-start | bytes 49160 | tf_op jit(solution)/shard_map/ppermute | solution.py:320
  21.2 2.3 %collective-permute-start.5 = (f32[16,256]{1,0:T(8,128)S(1)}, f32[16,256]{1,0:T(8,128)S(1)}, u32[]{:S(2)}, u32[]{:S(2)}) collective-permute-start(f32[16,256]{1,0:T(8,128)S(1)} %get-tuple-element.38.own_ref), channel_id=1, source_target_pairs={{0,8},{8,0},{16,24},{24,16},{1,9},{9,1},{17,25},{25,17},{2,10},{10... | collective-permute-start | bytes 49160 | tf_op jit(solution)/shard_map/ppermute | solution.py:320
  23.5 0.9 %image_vector.1._.image_ref = f32[25,16,256]{2,1,0:T(8,128)S(1)} custom-call(bf16[25,16,256]{2,1,0:T(8,128)(2,1)S(1)} %copy-done, f32[7,16,128]{2,1,0:T(8,128)S(1)} %get-tuple-element.31.edge_members_ref, f32[16,256]{1,0:T(8,128)S(1)} %get-tuple-element.37.field_ref.weighted_ref, f32[16,128]{1,0:T(8,128)S(1)} %get-tuple-element.39.edge_field_ref, ...), custom_call_target="tpu_custom_call" | custom-call | flops 5120000 | bytes 851968 | tf_op jit(solution)/shard_map/image_vector/pallas_call | solution.py:302
  24.3 0.3 collective-permute-done.7.c_ref
  24.6 0.6 %collective-permute-done.6.b_ref = f32[16,256]{1,0:T(8,128)S(1)} collective-permute-done((f32[16,256]{1,0:T(8,128)S(1)}, f32[16,256]{1,0:T(8,128)S(1)}, u32[]{:S(2)}, u32[]{:S(2)}) %collective-permute-start.6) | collective-permute-done | bytes 16416 | tf_op jit(solution)/shard_map/ppermute | solution.py:320
  25.2 0.2 collective-permute-done.5.a_ref
  25.4 0.2 moments.1
  25.5 0.0 collective-permute-start.8
  25.5 1.1 %collective-permute-done.8 = f32[1,128]{1,0:T(1,128)S(1)} collective-permute-done((f32[1,128]{1,0:T(1,128)S(1)}, f32[1,128]{1,0:T(1,128)S(1)}, u32[]{:S(2)}, u32[]{:S(2)}) %collective-permute-start.8) | collective-permute-done | bytes 544 | tf_op jit(solution)/shard_map/ppermute | solution.py:324
  26.7 1.6 %collective-permute-start.11 = (f32[1,128]{1,0:T(1,128)S(1)}, f32[1,128]{1,0:T(1,128)S(1)}, u32[]{:S(2)}, u32[]{:S(2)}) collective-permute-start(f32[1,128]{1,0:T(1,128)S(1)} %add.3.own_ref), channel_id=1, source_target_pairs={{0,6},{1,7},{2,4},{3,5},{4,2},{5,3},{6,0},{7,1},{8,14},{9,15},{10,... | collective-permute-start | bytes 1544 | tf_op jit(solution)/shard_map/ppermute | solution.py:324
  28.3 0.6 %collective-permute-start.10 = (f32[1,128]{1,0:T(1,128)S(1)}, f32[1,128]{1,0:T(1,128)S(1)}, u32[]{:S(2)}, u32[]{:S(2)}) collective-permute-start(f32[1,128]{1,0:T(1,128)S(1)} %add.3.own_ref), channel_id=1, source_target_pairs={{0,4},{1,5},{2,6},{3,7},{4,0},{5,1},{6,2},{7,3},{8,12},{9,13},{10,... | collective-permute-start | bytes 1544 | tf_op jit(solution)/shard_map/ppermute | solution.py:324
  28.9 1.2 %collective-permute-start.9 = (f32[1,128]{1,0:T(1,128)S(1)}, f32[1,128]{1,0:T(1,128)S(1)}, u32[]{:S(2)}, u32[]{:S(2)}) collective-permute-start(f32[1,128]{1,0:T(1,128)S(1)} %add.3.own_ref), channel_id=1, source_target_pairs={{0,2},{1,3},{2,0},{3,1},{4,6},{5,7},{6,4},{7,5},{8,10},{9,11},{10,... | collective-permute-start | bytes 1544 | tf_op jit(solution)/shard_map/ppermute | solution.py:324
  30.1 0.9 %collective-permute-done.11.c_ref = f32[1,128]{1,0:T(1,128)S(1)} collective-permute-done((f32[1,128]{1,0:T(1,128)S(1)}, f32[1,128]{1,0:T(1,128)S(1)}, u32[]{:S(2)}, u32[]{:S(2)}) %collective-permute-start.11) | collective-permute-done | bytes 544 | tf_op jit(solution)/shard_map/ppermute | solution.py:324
  31.1 0.7 %collective-permute-done.10.b_ref = f32[1,128]{1,0:T(1,128)S(1)} collective-permute-done((f32[1,128]{1,0:T(1,128)S(1)}, f32[1,128]{1,0:T(1,128)S(1)}, u32[]{:S(2)}, u32[]{:S(2)}) %collective-permute-start.10) | collective-permute-done | bytes 544 | tf_op jit(solution)/shard_map/ppermute | solution.py:324
  31.8 0.6 %collective-permute-done.9.a_ref = f32[1,128]{1,0:T(1,128)S(1)} collective-permute-done((f32[1,128]{1,0:T(1,128)S(1)}, f32[1,128]{1,0:T(1,128)S(1)}, u32[]{:S(2)}, u32[]{:S(2)}) %collective-permute-start.9) | collective-permute-done | bytes 544 | tf_op jit(solution)/shard_map/ppermute | solution.py:324
  32.4 0.9 %combine.1 = (f32[25,16,256]{2,1,0:T(8,128)}, f32[16,256]{1,0:T(8,128)}) custom-call(f32[1,128]{1,0:T(1,128)S(1)} %add.3.own_ref, f32[1,128]{1,0:T(1,128)S(1)} %collective-permute-done.9.a_ref, f32[1,128]{1,0:T(1,128)S(1)} %collective-permute-done.10.b_ref, f32[1,128]{1,0:T(1,128)S(1)} %collective-permute-done.11.c_ref, ...), custom_call_target="tpu_custom_call" | custom-call | bytes 1280000 | tf_op jit(solution)/shard_map/combine/pallas_call | solution.py:302
  (1 shorter events, 0.0 us)
Async XLA Ops:
  0.6 5.3 %copy-start = (bf16[25,16,256]{2,1,0:T(8,128)(2,1)S(1)}, bf16[25,16,256]{2,1,0:T(8,128)(2,1)}, u32[]{:S(2)}) copy-start(bf16[25,16,256]{2,1,0:T(8,128)(2,1)} %members_ref.7) | copy-start | bytes 614404
  0.6 5.3 %copy-start.1 = (f32[16,256]{1,0:T(8,128)S(1)}, f32[16,256]{1,0:T(8,128)}, u32[]{:S(2)}) copy-start(f32[16,256]{1,0:T(8,128)} %innovations_hbm.1) | copy-start | bytes 49156
  0.7 5.3 %copy-start.2 = (f32[16,256]{1,0:T(8,128)S(1)}, f32[16,256]{1,0:T(8,128)}, u32[]{:S(2)}) copy-start(f32[16,256]{1,0:T(8,128)} %precision_hbm.1) | copy-start | bytes 49156
  0.7 5.3 %copy-start.5 = (f32[16,16]{1,0:T(8,128)S(1)}, f32[16,16]{1,0:T(8,128)}, u32[]{:S(2)}) copy-start(f32[16,16]{1,0:T(8,128)} %map_ref.1) | copy-start | bytes 3076
  2.5 5.5 %collective-permute-start = (f32[2,16,128]{2,1,0:T(8,128)}, f32[2,16,128]{2,1,0:T(8,128)S(1)}, u32[]{:S(2)}, u32[]{:S(2)}) collective-permute-start(f32[2,16,128]{2,1,0:T(8,128)} %get-tuple-element.26), channel_id=1, source_target_pairs={{0,1},{1,2},{2,3},{3,4},{4,5},{5,6},{6,7},{7,0},{8,9},{9,10},{10,1... | collective-permute-start | bytes 49160 | tf_op jit(solution)/shard_map/ppermute | solution.py:366
  3.0 3.0 %copy-start.7 = (f32[16]{0:T(128)S(1)}, f32[16]{0:T(128)}, u32[]{:S(2)}) copy-start(f32[16]{0:T(128)} %param.11) | copy-start | bytes 196
  3.0 5.0 %collective-permute-start.1 = (f32[2,16,128]{2,1,0:T(8,128)}, f32[2,16,128]{2,1,0:T(8,128)S(1)}, u32[]{:S(2)}, u32[]{:S(2)}) collective-permute-start(f32[2,16,128]{2,1,0:T(8,128)} %get-tuple-element.27), channel_id=1, source_target_pairs={{1,0},{2,1},{3,2},{4,3},{5,4},{6,5},{7,6},{0,7},{9,8},{10,9},{11,1... | collective-permute-start | bytes 49160 | tf_op jit(solution)/shard_map/ppermute | solution.py:367
  6.0 0.7 %copy-start.6 = (s32[256]{0:T(256)S(1)}, s32[256]{0:T(256)}, u32[]{:S(2)}) copy-start(s32[256]{0:T(256)} %param.9) | copy-start | bytes 3076
  6.7 1.3 %copy-start.3 = (f32[7,16,128]{2,1,0:T(8,128)S(1)}, f32[7,16,128]{2,1,0:T(8,128)}, u32[]{:S(2)}) copy-start(f32[7,16,128]{2,1,0:T(8,128)} %get-tuple-element.24.low_ref) | copy-start | bytes 172036
  6.7 1.3 %copy-start.4 = (f32[7,16,128]{2,1,0:T(8,128)S(1)}, f32[7,16,128]{2,1,0:T(8,128)}, u32[]{:S(2)}) copy-start(f32[7,16,128]{2,1,0:T(8,128)} %get-tuple-element.25.high_ref) | copy-start | bytes 172036
  8.7 6.1 %collective-permute-start.4 = (f32[16,384]{1,0:T(8,128)S(1)}, f32[16,384]{1,0:T(8,128)S(1)}, u32[]{:S(2)}, u32[]{:S(2)}) collective-permute-start(f32[16,384]{1,0:T(8,128)S(1)} %get-tuple-element.33.own_ref), channel_id=1, source_target_pairs={{0,24},{8,16},{16,8},{24,0},{1,25},{9,17},{17,9},{25,1},{2,26},{10... | collective-permute-start | bytes 73736 | tf_op jit(solution)/shard_map/ppermute | solution.py:320
  13.0 4.7 %collective-permute-start.3 = (f32[16,384]{1,0:T(8,128)S(1)}, f32[16,384]{1,0:T(8,128)S(1)}, u32[]{:S(2)}, u32[]{:S(2)}) collective-permute-start(f32[16,384]{1,0:T(8,128)S(1)} %get-tuple-element.33.own_ref), channel_id=1, source_target_pairs={{0,16},{8,24},{16,0},{24,8},{1,17},{9,25},{17,1},{25,9},{2,18},{10... | collective-permute-start | bytes 73736 | tf_op jit(solution)/shard_map/ppermute | solution.py:320
  13.0 4.7 %collective-permute-start.2 = (f32[16,384]{1,0:T(8,128)S(1)}, f32[16,384]{1,0:T(8,128)S(1)}, u32[]{:S(2)}, u32[]{:S(2)}) collective-permute-start(f32[16,384]{1,0:T(8,128)S(1)} %get-tuple-element.33.own_ref), channel_id=1, source_target_pairs={{0,8},{8,0},{16,24},{24,16},{1,9},{9,1},{17,25},{25,17},{2,10},{10... | collective-permute-start | bytes 73736 | tf_op jit(solution)/shard_map/ppermute | solution.py:320
  19.0 5.6 %collective-permute-start.7 = (f32[16,256]{1,0:T(8,128)S(1)}, f32[16,256]{1,0:T(8,128)S(1)}, u32[]{:S(2)}, u32[]{:S(2)}) collective-permute-start(f32[16,256]{1,0:T(8,128)S(1)} %get-tuple-element.38.own_ref), channel_id=1, source_target_pairs={{0,24},{8,16},{16,8},{24,0},{1,25},{9,17},{17,9},{25,1},{2,26},{10... | collective-permute-start | bytes 49160 | tf_op jit(solution)/shard_map/ppermute | solution.py:320
  20.6 4.7 %collective-permute-start.6 = (f32[16,256]{1,0:T(8,128)S(1)}, f32[16,256]{1,0:T(8,128)S(1)}, u32[]{:S(2)}, u32[]{:S(2)}) collective-permute-start(f32[16,256]{1,0:T(8,128)S(1)} %get-tuple-element.38.own_ref), channel_id=1, source_target_pairs={{0,16},{8,24},{16,0},{24,8},{1,17},{9,25},{17,1},{25,9},{2,18},{10... | collective-permute-start | bytes 49160 | tf_op jit(solution)/shard_map/ppermute | solution.py:320
  21.2 4.2 %collective-permute-start.5 = (f32[16,256]{1,0:T(8,128)S(1)}, f32[16,256]{1,0:T(8,128)S(1)}, u32[]{:S(2)}, u32[]{:S(2)}) collective-permute-start(f32[16,256]{1,0:T(8,128)S(1)} %get-tuple-element.38.own_ref), channel_id=1, source_target_pairs={{0,8},{8,0},{16,24},{24,16},{1,9},{9,1},{17,25},{25,17},{2,10},{10... | collective-permute-start | bytes 49160 | tf_op jit(solution)/shard_map/ppermute | solution.py:320
  25.5 1.1 %collective-permute-start.8 = (f32[1,128]{1,0:T(1,128)S(1)}, f32[1,128]{1,0:T(1,128)S(1)}, u32[]{:S(2)}, u32[]{:S(2)}) collective-permute-start(f32[1,128]{1,0:T(1,128)S(1)} %get-tuple-element.40), channel_id=1, source_target_pairs={{0,1},{1,0},{2,3},{3,2},{4,5},{5,4},{6,7},{7,6},{8,9},{9,8},{10,11... | collective-permute-start | bytes 1544 | tf_op jit(solution)/shard_map/ppermute | solution.py:324
  26.7 4.4 %collective-permute-start.11 = (f32[1,128]{1,0:T(1,128)S(1)}, f32[1,128]{1,0:T(1,128)S(1)}, u32[]{:S(2)}, u32[]{:S(2)}) collective-permute-start(f32[1,128]{1,0:T(1,128)S(1)} %add.3.own_ref), channel_id=1, source_target_pairs={{0,6},{1,7},{2,4},{3,5},{4,2},{5,3},{6,0},{7,1},{8,14},{9,15},{10,... | collective-permute-start | bytes 1544 | tf_op jit(solution)/shard_map/ppermute | solution.py:324
  28.3 3.5 %collective-permute-start.10 = (f32[1,128]{1,0:T(1,128)S(1)}, f32[1,128]{1,0:T(1,128)S(1)}, u32[]{:S(2)}, u32[]{:S(2)}) collective-permute-start(f32[1,128]{1,0:T(1,128)S(1)} %add.3.own_ref), channel_id=1, source_target_pairs={{0,4},{1,5},{2,6},{3,7},{4,0},{5,1},{6,2},{7,3},{8,12},{9,13},{10,... | collective-permute-start | bytes 1544 | tf_op jit(solution)/shard_map/ppermute | solution.py:324
  28.9 3.5 %collective-permute-start.9 = (f32[1,128]{1,0:T(1,128)S(1)}, f32[1,128]{1,0:T(1,128)S(1)}, u32[]{:S(2)}, u32[]{:S(2)}) collective-permute-start(f32[1,128]{1,0:T(1,128)S(1)} %add.3.own_ref), channel_id=1, source_target_pairs={{0,2},{1,3},{2,0},{3,1},{4,6},{5,7},{6,4},{7,5},{8,10},{9,11},{10,... | collective-permute-start | bytes 1544 | tf_op jit(solution)/shard_map/ppermute | solution.py:324

commit v4 on v3

--- a/solution.py
+++ b/solution.py
@@ -152,9 +152,16 @@
 
 
 def main_kernel(
-    diffusivity_ref, map_ref, members_ref, innovations_ref, precision_ref, counts_ref,
+    diffusivity_hbm, map_ref, members_ref, innovations_ref, precision_ref, counts_hbm,
     taps_ref, square_ref, adjoint_ref, source_ref, weight_ref, out_ref, x_ref, y_ref,
-):
+    diffusivity_ref, counts_ref, sems,
+):
+    copies = [
+        pltpu.make_async_copy(diffusivity_hbm, diffusivity_ref, sems.at[0]),
+        pltpu.make_async_copy(counts_hbm, counts_ref, sems.at[1]),
+    ]
+    for copy in copies:
+        copy.start()
     levels = members_ref.shape[1]
     matrix = map_ref[...]
     dims = (((1,), (1,)), ((), ()))
@@ -163,6 +170,8 @@
     for k in range(levels):
         square_ref[k] = jnp.broadcast_to(square[:, k : k + 1], (levels, LANES))
         adjoint_ref[k] = jnp.broadcast_to(turned[:, k : k + 1], (levels, LANES))
+    for copy in copies:
+        copy.wait()
     coef = level_column(diffusivity_ref[...])
     keep = 1.0 - 2.0 * coef
     taps_ref[0] = keep * keep + 2.0 * coef * coef
@@ -329,11 +338,11 @@
     value, step = value + partner(value, axis, 1), 2
     while 4 * step < size:
         if (size // step).bit_length() % 2:
-            terms = [partner(value, axis, k * step) for k in (1, 2, 3)]
+            terms = [partner(value, axis, (k * step) ^ 1) for k in (1, 2, 3)]
             value, step = (value + terms[0]) + (terms[1] + terms[2]), 4 * step
         else:
-            value, step = value + partner(value, axis, step), 2 * step
-    return [value, *(partner(value, axis, k * step) for k in (1, 2, 3))]
+            value, step = value + partner(value, axis, step ^ 1), 2 * step
+    return [value, *(partner(value, axis, (k * step) ^ 1) for k in (1, 2, 3))]
 
 
 def local(perturbations, innovations, precision_field, obs_counts, vertical_map, diffusivity):
@@ -368,7 +377,8 @@
     taps, square, mapped, source, weight, main = call(
         main_kernel, "first_inner", [shape_of(3, levels, LANES), column, column, level, level, level],
         (diffusivity.reshape(1, levels), vertical_map, perturbations, innovations, precision_field, counts),
-        scratch, flops=work,
+        scratch + [pltpu.VMEM((1, levels), F32), pltpu.VMEM((1, size), jnp.int32), pltpu.SemaphoreType.DMA((2,))],
+        {0: elsewhere, 5: elsewhere}, work,
     )
     edge_members, edge_source, edge_weight, part = call(
         functools.partial(edge_kernel, count), "first_edges",

time: 33.5 us -> 32.7 us (0.976)
  waiting for transfers between devices: 7.65 us -> 7.19 us
  starting transfers between devices: 16.3 us -> 15.9 us
    ppermute x4, starting transfers between devices: 3.5 us -> 3.03 us  [partner(): lax.ppermute(value, axis, [(i, i ^ step) for i in range(lax.axis_size(axi...]
    ppermute x4, waiting for transfers between devices: 3.4 us -> 2.94 us  [partner(): lax.ppermute(value, axis, [(i, i ^ step) for i in range(lax.axis_size(axi...]
  transfers between devices with their start and end apart: 12 -> 12, of which waited for: 9 -> 9; matrix products, arithmetic and copies ran while one was open for 0% -> 0% of each run, Pallas kernels for 9% -> 10%
where the time goes in v4:
time: 32.7 us; the launch traced here: 32.5 us
  starting transfers between devices  15.9 us (49%)
  Pallas kernels  7.96 us (24%)
  waiting for transfers between devices  7.19 us (22%)
  between operations  0.78 us (2%)
  local copies, waits for them, and re-layouts  0.7 us (2%)
    ppermute x6, starting transfers between devices, from_partners(): lax.ppermute(value, axis, [(i, i ^ step) for i in range(size)])  9.38 us
    pallas_call x8, Pallas kernels, call(): pl.pallas_call(kernel, name=name, out_shape=list(outs), in_specs=[specs.g...  7.96 us
    ppermute x6, waiting for transfers between devices, from_partners(): lax.ppermute(value, axis, [(i, i ^ step) for i in range(size)])  4.24 us
    ppermute x4, starting transfers between devices, partner(): lax.ppermute(value, axis, [(i, i ^ step) for i in range(lax.axis_size(axi...  3.03 us
    ppermute x1, starting transfers between devices, local(): after = lax.ppermute(high_message, 'domain', down)  2.96 us
    ppermute x4, waiting for transfers between devices, partner(): lax.ppermute(value, axis, [(i, i ^ step) for i in range(lax.axis_size(axi...  2.94 us
    unnamed x16, local copies, waits for them, and re-layouts  0.7 us
  transfers between devices with their start and end apart: 12, of which 9 were waited for; matrix products, arithmetic and copies ran while one was open for 0% of the time, Pallas kernels for 10%

profile of v4, /device:TPU:0, one launch (start us, length us, event | category | flops | bytes accessed | tf_op | source)
XLA Modules:
  0.0 32.5 jit_solution(12149729217967017895)
XLA Ops:
  0.6 0.0 copy-start
  0.6 0.0 copy-start.1
  0.7 0.0 copy-start.2
  0.7 0.0 copy-start.5
  0.7 1.8 %pack_edges.1 = (f32[7,16,128]{2,1,0:T(8,128)}, f32[7,16,128]{2,1,0:T(8,128)}, f32[2,16,128]{2,1,0:T(8,128)}, f32[2,16,128]{2,1,0:T(8,128)}) custom-call(bf16[25,16,256]{2,1,0:T(8,128)(2,1)} %members_ref.7, f32[16,256]{1,0:T(8,128)} %innovations_hbm.1, f32[16,256]{1,0:T(8,128)} %precision_hbm.1, s32[1,256]{1,0:T(1,128)} %bitcast.2), custom_call_target="tpu_custom_call" | custom-call | flops 286720 | bytes 386048 | tf_op jit(solution)/shard_map/pack_edges/pallas_call | solution.py:311
  2.5 0.5 %collective-permute-start = (f32[2,16,128]{2,1,0:T(8,128)}, f32[2,16,128]{2,1,0:T(8,128)S(1)}, u32[]{:S(2)}, u32[]{:S(2)}) collective-permute-start(f32[2,16,128]{2,1,0:T(8,128)} %get-tuple-element.26), channel_id=1, source_target_pairs={{0,1},{1,2},{2,3},{3,4},{4,5},{5,6},{6,7},{7,0},{8,9},{9,10},{10,1... | collective-permute-start | bytes 49160 | tf_op jit(solution)/shard_map/ppermute | solution.py:375
  3.0 0.0 copy-start.7
  3.0 3.0 %collective-permute-start.1 = (f32[2,16,128]{2,1,0:T(8,128)}, f32[2,16,128]{2,1,0:T(8,128)S(1)}, u32[]{:S(2)}, u32[]{:S(2)}) collective-permute-start(f32[2,16,128]{2,1,0:T(8,128)} %get-tuple-element.27), channel_id=1, source_target_pairs={{1,0},{2,1},{3,2},{4,3},{5,4},{6,5},{7,6},{0,7},{9,8},{10,9},{11,1... | collective-permute-start | bytes 49160 | tf_op jit(solution)/shard_map/ppermute | solution.py:376
  6.0 0.0 copy-done
  6.0 0.0 copy-done.1
  6.0 0.0 copy-done.2
  6.0 0.0 copy-done.5
  6.0 0.0 copy-done.7
  6.0 0.0 copy-start.6
  6.0 0.7 %copy-done.6 = s32[256]{0:T(256)S(1)} copy-done((s32[256]{0:T(256)S(1)}, s32[256]{0:T(256)}, u32[]{:S(2)}) %copy-start.6) | copy-done | bytes 1048
  6.7 0.0 copy-start.3
  6.7 0.0 copy-start.4
  6.7 1.4 %first_inner.1 = (f32[3,16,128]{2,1,0:T(8,128)S(1)}, f32[16,16,128]{2,1,0:T(8,128)S(1)}, f32[16,16,128]{2,1,0:T(8,128)S(1)}, f32[16,256]{1,0:T(8,128)S(1)}, f32[...) custom-call(f32[1,16]{1,0:T(1,128)S(1)} %bitcast.4, f32[16,16]{1,0:T(8,128)S(1)} %copy-done.5, bf16[25,16,256]{2,1,0:T(8,128)(2,1)S(1)} %copy-done, ...), custom_call_target="tpu_custom_call" | custom-call | flops 5120000 | bytes 575552 | tf_op jit(solution)/shard_map/first_inner/pallas_call | solution.py:311
  8.1 0.0 collective-permute-done.before_ref
  8.1 0.0 collective-permute-done.1.after_ref
  8.1 0.0 copy-done.3
  8.1 0.0 copy-done.4
  8.1 0.7 %first_edges.1 = (f32[7,16,128]{2,1,0:T(8,128)S(1)}, f32[16,128]{1,0:T(8,128)S(1)}, f32[16,128]{1,0:T(8,128)S(1)}, f32[16,384]{1,0:T(8,128)S(1)}) custom-call(f32[7,16,128]{2,1,0:T(8,128)S(1)} %copy-done.3, f32[7,16,128]{2,1,0:T(8,128)S(1)} %copy-done.4, f32[2,16,128]{2,1,0:T(8,128)S(1)} %collective-permute-done.before_ref, ...), custom_call_target="tpu_custom_call" | custom-call | flops 716800 | bytes 417792 | tf_op jit(solution)/shard_map/first_edges/pallas_call | solution.py:311
  8.8 4.3 %collective-permute-start.4 = (f32[16,384]{1,0:T(8,128)S(1)}, f32[16,384]{1,0:T(8,128)S(1)}, u32[]{:S(2)}, u32[]{:S(2)}) collective-permute-start(f32[16,384]{1,0:T(8,128)S(1)} %get-tuple-element.33.own_ref), channel_id=1, source_target_pairs={{0,24},{8,16},{16,8},{24,0},{1,25},{9,17},{17,9},{25,1},{2,26},{10... | collective-permute-start | bytes 73736 | tf_op jit(solution)/shard_map/ppermute | solution.py:329
  13.1 0.0 collective-permute-start.3
  13.1 0.6 %collective-permute-start.2 = (f32[16,384]{1,0:T(8,128)S(1)}, f32[16,384]{1,0:T(8,128)S(1)}, u32[]{:S(2)}, u32[]{:S(2)}) collective-permute-start(f32[16,384]{1,0:T(8,128)S(1)} %get-tuple-element.33.own_ref), channel_id=1, source_target_pairs={{0,8},{8,0},{16,24},{24,16},{1,9},{9,1},{17,25},{25,17},{2,10},{10... | collective-permute-start | bytes 73736 | tf_op jit(solution)/shard_map/ppermute | solution.py:329
  13.7 0.9 %start_vector.1._.start_ref = f32[25,16,256]{2,1,0:T(8,128)S(1)} custom-call(bf16[25,16,256]{2,1,0:T(8,128)(2,1)S(1)} %copy-done, f32[7,16,128]{2,1,0:T(8,128)S(1)} %get-tuple-element.31.edge_members_ref, f32[16,256]{1,0:T(8,128)S(1)} %get-tuple-element.22.field_ref.source_ref, f32[16,128]{1,0:T(8,128)S(1)} %get-tuple-element.34.edge_field_ref, ...), custom_call_target="tpu_custom_call" | custom-call | flops 5120000 | bytes 851968 | tf_op jit(solution)/shard_map/start_vector/pallas_call | solution.py:311
  14.6 0.3 collective-permute-done.4.c_ref
  14.9 2.9 %collective-permute-done.3.b_ref = f32[16,384]{1,0:T(8,128)S(1)} collective-permute-done((f32[16,384]{1,0:T(8,128)S(1)}, f32[16,384]{1,0:T(8,128)S(1)}, u32[]{:S(2)}, u32[]{:S(2)}) %collective-permute-start.3) | collective-permute-done | bytes 24608 | tf_op jit(solution)/shard_map/ppermute | solution.py:329
  17.8 0.0 collective-permute-done.2.a_ref
  17.8 1.3 %second_apply.1 = (f32[16,256]{1,0:T(8,128)S(1)}, f32[16,256]{1,0:T(8,128)S(1)}, f32[16,128]{1,0:T(8,128)S(1)}, f32[16,256]{1,0:T(8,128)S(1)}) custom-call(bf16[25,16,256]{2,1,0:T(8,128)(2,1)S(1)} %copy-done, f32[7,16,128]{2,1,0:T(8,128)S(1)} %get-tuple-element.31.edge_members_ref, f32[16,256]{1,0:T(8,128)S(1)} %get-tuple-element.23.weight_ref, ...), custom_call_target="tpu_custom_call" | custom-call | flops 5836800 | bytes 1007616 | tf_op jit(solution)/shard_map/second_apply/pallas_call | solution.py:311
  19.1 1.5 %collective-permute-start.7 = (f32[16,256]{1,0:T(8,128)S(1)}, f32[16,256]{1,0:T(8,128)S(1)}, u32[]{:S(2)}, u32[]{:S(2)}) collective-permute-start(f32[16,256]{1,0:T(8,128)S(1)} %get-tuple-element.38.own_ref), channel_id=1, source_target_pairs={{0,24},{8,16},{16,8},{24,0},{1,25},{9,17},{17,9},{25,1},{2,26},{10... | collective-permute-start | bytes 49160 | tf_op jit(solution)/shard_map/ppermute | solution.py:329
  20.6 0.6 %collective-permute-start.6 = (f32[16,256]{1,0:T(8,128)S(1)}, f32[16,256]{1,0:T(8,128)S(1)}, u32[]{:S(2)}, u32[]{:S(2)}) collective-permute-start(f32[16,256]{1,0:T(8,128)S(1)} %get-tuple-element.38.own_ref), channel_id=1, source_target_pairs={{0,16},{8,24},{16,0},{24,8},{1,17},{9,25},{17,1},{25,9},{2,18},{10... | collective-permute-start | bytes 49160 | tf_op jit(solution)/shard_map/ppermute | solution.py:329
  21.3 2.3 %collective-permute-start.5 = (f32[16,256]{1,0:T(8,128)S(1)}, f32[16,256]{1,0:T(8,128)S(1)}, u32[]{:S(2)}, u32[]{:S(2)}) collective-permute-start(f32[16,256]{1,0:T(8,128)S(1)} %get-tuple-element.38.own_ref), channel_id=1, source_target_pairs={{0,8},{8,0},{16,24},{24,16},{1,9},{9,1},{17,25},{25,17},{2,10},{10... | collective-permute-start | bytes 49160 | tf_op jit(solution)/shard_map/ppermute | solution.py:329
  23.6 0.9 %image_vector.1._.image_ref = f32[25,16,256]{2,1,0:T(8,128)S(1)} custom-call(bf16[25,16,256]{2,1,0:T(8,128)(2,1)S(1)} %copy-done, f32[7,16,128]{2,1,0:T(8,128)S(1)} %get-tuple-element.31.edge_members_ref, f32[16,256]{1,0:T(8,128)S(1)} %get-tuple-element.37.field_ref.weighted_ref, f32[16,128]{1,0:T(8,128)S(1)} %get-tuple-element.39.edge_field_ref, ...), custom_call_target="tpu_custom_call" | custom-call | flops 5120000 | bytes 851968 | tf_op jit(solution)/shard_map/image_vector/pallas_call | solution.py:311
  24.4 0.3 collective-permute-done.7.c_ref
  24.7 0.6 %collective-permute-done.6.b_ref = f32[16,256]{1,0:T(8,128)S(1)} collective-permute-done((f32[16,256]{1,0:T(8,128)S(1)}, f32[16,256]{1,0:T(8,128)S(1)}, u32[]{:S(2)}, u32[]{:S(2)}) %collective-permute-start.6) | collective-permute-done | bytes 16416 | tf_op jit(solution)/shard_map/ppermute | solution.py:329
  25.3 0.2 collective-permute-done.5.a_ref
  25.4 0.2 moments.1
  25.6 0.0 collective-permute-start.8
  25.6 1.1 %collective-permute-done.8 = f32[1,128]{1,0:T(1,128)S(1)} collective-permute-done((f32[1,128]{1,0:T(1,128)S(1)}, f32[1,128]{1,0:T(1,128)S(1)}, u32[]{:S(2)}, u32[]{:S(2)}) %collective-permute-start.8) | collective-permute-done | bytes 544 | tf_op jit(solution)/shard_map/ppermute | solution.py:333
  26.7 1.4 %collective-permute-start.11 = (f32[1,128]{1,0:T(1,128)S(1)}, f32[1,128]{1,0:T(1,128)S(1)}, u32[]{:S(2)}, u32[]{:S(2)}) collective-permute-start(f32[1,128]{1,0:T(1,128)S(1)} %add.3.own_ref), channel_id=1, source_target_pairs={{0,7},{1,6},{2,5},{3,4},{4,3},{5,2},{6,1},{7,0},{8,15},{9,14},{10,... | collective-permute-start | bytes 1544 | tf_op jit(solution)/shard_map/ppermute | solution.py:333
  28.1 0.5 %collective-permute-start.10 = (f32[1,128]{1,0:T(1,128)S(1)}, f32[1,128]{1,0:T(1,128)S(1)}, u32[]{:S(2)}, u32[]{:S(2)}) collective-permute-start(f32[1,128]{1,0:T(1,128)S(1)} %add.3.own_ref), channel_id=1, source_target_pairs={{0,5},{1,4},{2,7},{3,6},{4,1},{5,0},{6,3},{7,2},{8,13},{9,12},{10,... | collective-permute-start | bytes 1544 | tf_op jit(solution)/shard_map/ppermute | solution.py:333
  28.6 1.1 %collective-permute-start.9 = (f32[1,128]{1,0:T(1,128)S(1)}, f32[1,128]{1,0:T(1,128)S(1)}, u32[]{:S(2)}, u32[]{:S(2)}) collective-permute-start(f32[1,128]{1,0:T(1,128)S(1)} %add.3.own_ref), channel_id=1, source_target_pairs={{0,3},{1,2},{2,1},{3,0},{4,7},{5,6},{6,5},{7,4},{8,11},{9,10},{10,... | collective-permute-start | bytes 1544 | tf_op jit(solution)/shard_map/ppermute | solution.py:333
  29.8 0.8 %collective-permute-done.11.c_ref = f32[1,128]{1,0:T(1,128)S(1)} collective-permute-done((f32[1,128]{1,0:T(1,128)S(1)}, f32[1,128]{1,0:T(1,128)S(1)}, u32[]{:S(2)}, u32[]{:S(2)}) %collective-permute-start.11) | collective-permute-done | bytes 544 | tf_op jit(solution)/shard_map/ppermute | solution.py:333
  30.6 0.5 %collective-permute-done.10.b_ref = f32[1,128]{1,0:T(1,128)S(1)} collective-permute-done((f32[1,128]{1,0:T(1,128)S(1)}, f32[1,128]{1,0:T(1,128)S(1)}, u32[]{:S(2)}, u32[]{:S(2)}) %collective-permute-start.10) | collective-permute-done | bytes 544 | tf_op jit(solution)/shard_map/ppermute | solution.py:333
  31.1 0.5 %collective-permute-done.9.a_ref = f32[1,128]{1,0:T(1,128)S(1)} collective-permute-done((f32[1,128]{1,0:T(1,128)S(1)}, f32[1,128]{1,0:T(1,128)S(1)}, u32[]{:S(2)}, u32[]{:S(2)}) %collective-permute-start.9) | collective-permute-done | bytes 544 | tf_op jit(solution)/shard_map/ppermute | solution.py:333
  31.6 0.9 %combine.1 = (f32[25,16,256]{2,1,0:T(8,128)}, f32[16,256]{1,0:T(8,128)}) custom-call(f32[1,128]{1,0:T(1,128)S(1)} %add.3.own_ref, f32[1,128]{1,0:T(1,128)S(1)} %collective-permute-done.9.a_ref, f32[1,128]{1,0:T(1,128)S(1)} %collective-permute-done.10.b_ref, f32[1,128]{1,0:T(1,128)S(1)} %collective-permute-done.11.c_ref, ...), custom_call_target="tpu_custom_call" | custom-call | bytes 1280000 | tf_op jit(solution)/shard_map/combine/pallas_call | solution.py:311
  (1 shorter events, 0.0 us)
Async XLA Ops:
  0.6 5.3 %copy-start = (bf16[25,16,256]{2,1,0:T(8,128)(2,1)S(1)}, bf16[25,16,256]{2,1,0:T(8,128)(2,1)}, u32[]{:S(2)}) copy-start(bf16[25,16,256]{2,1,0:T(8,128)(2,1)} %members_ref.7) | copy-start | bytes 614404
  0.6 5.3 %copy-start.1 = (f32[16,256]{1,0:T(8,128)S(1)}, f32[16,256]{1,0:T(8,128)}, u32[]{:S(2)}) copy-start(f32[16,256]{1,0:T(8,128)} %innovations_hbm.1) | copy-start | bytes 49156
  0.7 5.3 %copy-start.2 = (f32[16,256]{1,0:T(8,128)S(1)}, f32[16,256]{1,0:T(8,128)}, u32[]{:S(2)}) copy-start(f32[16,256]{1,0:T(8,128)} %precision_hbm.1) | copy-start | bytes 49156
  0.7 5.3 %copy-start.5 = (f32[16,16]{1,0:T(8,128)S(1)}, f32[16,16]{1,0:T(8,128)}, u32[]{:S(2)}) copy-start(f32[16,16]{1,0:T(8,128)} %map_ref.1) | copy-start | bytes 3076
  2.5 5.6 %collective-permute-start = (f32[2,16,128]{2,1,0:T(8,128)}, f32[2,16,128]{2,1,0:T(8,128)S(1)}, u32[]{:S(2)}, u32[]{:S(2)}) collective-permute-start(f32[2,16,128]{2,1,0:T(8,128)} %get-tuple-element.26), channel_id=1, source_target_pairs={{0,1},{1,2},{2,3},{3,4},{4,5},{5,6},{6,7},{7,0},{8,9},{9,10},{10,1... | collective-permute-start | bytes 49160 | tf_op jit(solution)/shard_map/ppermute | solution.py:375
  3.0 3.0 %copy-start.7 = (f32[16]{0:T(128)S(1)}, f32[16]{0:T(128)}, u32[]{:S(2)}) copy-start(f32[16]{0:T(128)} %param.11) | copy-start | bytes 196
  3.0 5.1 %collective-permute-start.1 = (f32[2,16,128]{2,1,0:T(8,128)}, f32[2,16,128]{2,1,0:T(8,128)S(1)}, u32[]{:S(2)}, u32[]{:S(2)}) collective-permute-start(f32[2,16,128]{2,1,0:T(8,128)} %get-tuple-element.27), channel_id=1, source_target_pairs={{1,0},{2,1},{3,2},{4,3},{5,4},{6,5},{7,6},{0,7},{9,8},{10,9},{11,1... | collective-permute-start | bytes 49160 | tf_op jit(solution)/shard_map/ppermute | solution.py:376
  6.0 0.7 %copy-start.6 = (s32[256]{0:T(256)S(1)}, s32[256]{0:T(256)}, u32[]{:S(2)}) copy-start(s32[256]{0:T(256)} %param.9) | copy-start | bytes 3076
  6.7 1.4 %copy-start.3 = (f32[7,16,128]{2,1,0:T(8,128)S(1)}, f32[7,16,128]{2,1,0:T(8,128)}, u32[]{:S(2)}) copy-start(f32[7,16,128]{2,1,0:T(8,128)} %get-tuple-element.24.low_ref) | copy-start | bytes 172036
  6.7 1.4 %copy-start.4 = (f32[7,16,128]{2,1,0:T(8,128)S(1)}, f32[7,16,128]{2,1,0:T(8,128)}, u32[]{:S(2)}) copy-start(f32[7,16,128]{2,1,0:T(8,128)} %get-tuple-element.25.high_ref) | copy-start | bytes 172036
  8.8 6.1 %collective-permute-start.4 = (f32[16,384]{1,0:T(8,128)S(1)}, f32[16,384]{1,0:T(8,128)S(1)}, u32[]{:S(2)}, u32[]{:S(2)}) collective-permute-start(f32[16,384]{1,0:T(8,128)S(1)} %get-tuple-element.33.own_ref), channel_id=1, source_target_pairs={{0,24},{8,16},{16,8},{24,0},{1,25},{9,17},{17,9},{25,1},{2,26},{10... | collective-permute-start | bytes 73736 | tf_op jit(solution)/shard_map/ppermute | solution.py:329
  13.1 4.7 %collective-permute-start.3 = (f32[16,384]{1,0:T(8,128)S(1)}, f32[16,384]{1,0:T(8,128)S(1)}, u32[]{:S(2)}, u32[]{:S(2)}) collective-permute-start(f32[16,384]{1,0:T(8,128)S(1)} %get-tuple-element.33.own_ref), channel_id=1, source_target_pairs={{0,16},{8,24},{16,0},{24,8},{1,17},{9,25},{17,1},{25,9},{2,18},{10... | collective-permute-start | bytes 73736 | tf_op jit(solution)/shard_map/ppermute | solution.py:329
  13.1 4.7 %collective-permute-start.2 = (f32[16,384]{1,0:T(8,128)S(1)}, f32[16,384]{1,0:T(8,128)S(1)}, u32[]{:S(2)}, u32[]{:S(2)}) collective-permute-start(f32[16,384]{1,0:T(8,128)S(1)} %get-tuple-element.33.own_ref), channel_id=1, source_target_pairs={{0,8},{8,0},{16,24},{24,16},{1,9},{9,1},{17,25},{25,17},{2,10},{10... | collective-permute-start | bytes 73736 | tf_op jit(solution)/shard_map/ppermute | solution.py:329
  19.1 5.6 %collective-permute-start.7 = (f32[16,256]{1,0:T(8,128)S(1)}, f32[16,256]{1,0:T(8,128)S(1)}, u32[]{:S(2)}, u32[]{:S(2)}) collective-permute-start(f32[16,256]{1,0:T(8,128)S(1)} %get-tuple-element.38.own_ref), channel_id=1, source_target_pairs={{0,24},{8,16},{16,8},{24,0},{1,25},{9,17},{17,9},{25,1},{2,26},{10... | collective-permute-start | bytes 49160 | tf_op jit(solution)/shard_map/ppermute | solution.py:329
  20.6 4.7 %collective-permute-start.6 = (f32[16,256]{1,0:T(8,128)S(1)}, f32[16,256]{1,0:T(8,128)S(1)}, u32[]{:S(2)}, u32[]{:S(2)}) collective-permute-start(f32[16,256]{1,0:T(8,128)S(1)} %get-tuple-element.38.own_ref), channel_id=1, source_target_pairs={{0,16},{8,24},{16,0},{24,8},{1,17},{9,25},{17,1},{25,9},{2,18},{10... | collective-permute-start | bytes 49160 | tf_op jit(solution)/shard_map/ppermute | solution.py:329
  21.3 4.2 %collective-permute-start.5 = (f32[16,256]{1,0:T(8,128)S(1)}, f32[16,256]{1,0:T(8,128)S(1)}, u32[]{:S(2)}, u32[]{:S(2)}) collective-permute-start(f32[16,256]{1,0:T(8,128)S(1)} %get-tuple-element.38.own_ref), channel_id=1, source_target_pairs={{0,8},{8,0},{16,24},{24,16},{1,9},{9,1},{17,25},{25,17},{2,10},{10... | collective-permute-start | bytes 49160 | tf_op jit(solution)/shard_map/ppermute | solution.py:329
  25.6 1.1 %collective-permute-start.8 = (f32[1,128]{1,0:T(1,128)S(1)}, f32[1,128]{1,0:T(1,128)S(1)}, u32[]{:S(2)}, u32[]{:S(2)}) collective-permute-start(f32[1,128]{1,0:T(1,128)S(1)} %get-tuple-element.40), channel_id=1, source_target_pairs={{0,1},{1,0},{2,3},{3,2},{4,5},{5,4},{6,7},{7,6},{8,9},{9,8},{10,11... | collective-permute-start | bytes 1544 | tf_op jit(solution)/shard_map/ppermute | solution.py:333
  26.7 3.9 %collective-permute-start.11 = (f32[1,128]{1,0:T(1,128)S(1)}, f32[1,128]{1,0:T(1,128)S(1)}, u32[]{:S(2)}, u32[]{:S(2)}) collective-permute-start(f32[1,128]{1,0:T(1,128)S(1)} %add.3.own_ref), channel_id=1, source_target_pairs={{0,7},{1,6},{2,5},{3,4},{4,3},{5,2},{6,1},{7,0},{8,15},{9,14},{10,... | collective-permute-start | bytes 1544 | tf_op jit(solution)/shard_map/ppermute | solution.py:333
  28.1 3.0 %collective-permute-start.10 = (f32[1,128]{1,0:T(1,128)S(1)}, f32[1,128]{1,0:T(1,128)S(1)}, u32[]{:S(2)}, u32[]{:S(2)}) collective-permute-start(f32[1,128]{1,0:T(1,128)S(1)} %add.3.own_ref), channel_id=1, source_target_pairs={{0,5},{1,4},{2,7},{3,6},{4,1},{5,0},{6,3},{7,2},{8,13},{9,12},{10,... | collective-permute-start | bytes 1544 | tf_op jit(solution)/shard_map/ppermute | solution.py:333
  28.6 3.0 %collective-permute-start.9 = (f32[1,128]{1,0:T(1,128)S(1)}, f32[1,128]{1,0:T(1,128)S(1)}, u32[]{:S(2)}, u32[]{:S(2)}) collective-permute-start(f32[1,128]{1,0:T(1,128)S(1)} %add.3.own_ref), channel_id=1, source_target_pairs={{0,3},{1,2},{2,1},{3,0},{4,7},{5,6},{6,5},{7,4},{8,11},{9,10},{10,... | collective-permute-start | bytes 1544 | tf_op jit(solution)/shard_map/ppermute | solution.py:333

commit v5 on v4

--- a/solution.py
+++ b/solution.py
@@ -13,6 +13,7 @@
 HALO = 2 * REACH
 SLOT = 4 * HALO
 SLOTS = LANES // SLOT
+SHIFTS = range(-DIFF, DIFF + 1)
 F32 = jnp.float32
 HIGHEST = lax.Precision.HIGHEST
 VMEM_LIMIT = 32 * 1024 * 1024
@@ -55,6 +56,46 @@
 
 def wide_taps(taps_ref, like):
     return [widen(taps_ref[i], like) for i in range(3)]
+
+
+def shifted_by(value, shift):
+    return value if shift == 0 else lane_roll(value, shift)
+
+
+def smooth_product(shifted_ref, m, steps):
+    out = None
+    for i, step in enumerate(steps):
+        term = shifted_ref[i, m].astype(F32) * step
+        out = term if out is None else out + term
+    return out
+
+
+def field_steps(field, taps_ref):
+    taps = wide_taps(taps_ref, field)
+    return [taps[abs(s)] * shifted_by(field, s) for s in SHIFTS]
+
+
+def apply_shifted(shifted_ref, field, taps_ref, blocks_ref, split_ref, y_ref):
+    _, count, levels, size = shifted_ref.shape
+    rows = blocks_ref.shape[0]
+    group = rows // levels
+    steps = field_steps(field, taps_ref)
+    for m in range(count):
+        value = smooth_product(shifted_ref, m, steps)
+        high = value.astype(jnp.bfloat16)
+        low = (value - high.astype(F32)).astype(jnp.bfloat16)
+        place, at = m // group, m % group * levels
+        for base, part in ((0, high), (rows, high), (2 * rows, low)):
+            split_ref[place, base + at : base + at + levels] = part
+    for place in range(count // group):
+        value = jnp.dot(blocks_ref[...], split_ref[place], preferred_element_type=F32)
+        y_ref[place * group : (place + 1) * group] = value.reshape(group, levels, size)
+    totals = [jnp.zeros((levels, size), F32)] * len(SHIFTS)
+    for m in range(count):
+        value = y_ref[m]
+        totals = [total + shifted_ref[i, m].astype(F32) * value for i, total in enumerate(totals)]
+    taps = wide_taps(taps_ref, field)
+    return sum(taps[abs(s)] * shifted_by(total, -s) for s, total in zip(SHIFTS, totals))
 
 
 def apply_ensemble(parts, taps_ref, mix_ref, scratches):
@@ -153,8 +194,8 @@
 
 def main_kernel(
     diffusivity_hbm, map_ref, members_ref, innovations_ref, precision_ref, counts_hbm,
-    taps_ref, square_ref, adjoint_ref, source_ref, weight_ref, out_ref, x_ref, y_ref,
-    diffusivity_ref, counts_ref, sems,
+    taps_ref, square_ref, adjoint_ref, blocks_ref, shifted_ref, source_ref, weight_ref, out_ref,
+    split_ref, y_ref, diffusivity_ref, counts_ref, sems,
 ):
     copies = [
         pltpu.make_async_copy(diffusivity_hbm, diffusivity_ref, sems.at[0]),
@@ -167,9 +208,22 @@
     dims = (((1,), (1,)), ((), ()))
     square = lax.dot_general(matrix, matrix, dims, precision=HIGHEST, preferred_element_type=F32)
     turned = matrix.T
+    rows, width = blocks_ref.shape
+    column = lane_index((levels, -(-width // LANES) * LANES))
+    block = jnp.zeros(column.shape, F32)
     for k in range(levels):
         square_ref[k] = jnp.broadcast_to(square[:, k : k + 1], (levels, LANES))
+        block = jnp.where(column % levels == k, widen(square_ref[k], block), block)
         adjoint_ref[k] = jnp.broadcast_to(turned[:, k : k + 1], (levels, LANES))
+    high = block.astype(jnp.bfloat16).astype(F32)
+    block = jnp.where(column // rows == 1, block - high, high)
+    for i in range(rows // levels):
+        value = jnp.where(column % rows // levels == i, block, 0.0).astype(jnp.bfloat16)
+        blocks_ref[i * levels : (i + 1) * levels] = value[:, :width]
+    for m in range(members_ref.shape[0]):
+        value = members_ref[m].astype(F32)
+        for i, s in enumerate(SHIFTS):
+            shifted_ref[i, m] = shifted_by(value, s).astype(shifted_ref.dtype)
     for copy in copies:
         copy.wait()
     coef = level_column(diffusivity_ref[...])
@@ -180,7 +234,7 @@
     weight = counts_ref[...].astype(F32) * precision_ref[...]
     source = weight * innovations_ref[...]
     source_ref[...], weight_ref[...] = source, weight
-    (out_ref[...],) = apply_ensemble([(members_ref, source)], taps_ref, square_ref, [(x_ref, y_ref)])
+    out_ref[...] = apply_shifted(shifted_ref, source, taps_ref, blocks_ref, split_ref, y_ref)
 
 
 def edge_kernel(
@@ -214,10 +268,11 @@
 
 
 def second_kernel(
-    members_ref, edge_members_ref, weight_ref, edge_weight_ref, taps_ref, square_ref, own_ref, a_ref, b_ref, c_ref, _,
-    first_ref, weighted_ref, edge_weighted_ref, out_ref, x_ref, y_ref, edge_x_ref, edge_y_ref,
-):
-    _, levels, size = members_ref.shape
+    shifted_ref, edge_members_ref, weight_ref, edge_weight_ref, taps_ref, square_ref, blocks_ref,
+    own_ref, a_ref, b_ref, c_ref, _,
+    first_ref, weighted_ref, edge_weighted_ref, out_ref, split_ref, y_ref, edge_x_ref, edge_y_ref,
+):
+    levels, size = weight_ref.shape
     lane = lane_index((levels, LANES))
     at = lane % SLOT
     total = tree_sum(own_ref, a_ref, b_ref, c_ref)
@@ -231,9 +286,9 @@
     first_ref[...] = first
     weighted_ref[...] = weighted
     edge_weighted_ref[...] = edge_weighted
-    main, edge = apply_ensemble(
-        [(members_ref, weighted), (edge_members_ref, edge_weighted)], taps_ref, square_ref,
-        [(x_ref, y_ref), (edge_x_ref, edge_y_ref)],
+    main = apply_shifted(shifted_ref, weighted, taps_ref, blocks_ref, split_ref, y_ref)
+    (edge,) = apply_ensemble(
+        [(edge_members_ref, edge_weighted)], taps_ref, square_ref, [(edge_x_ref, edge_y_ref)]
     )
     out_ref[...] = patch(main, all_slots(edge), REACH)
 
@@ -259,16 +314,16 @@
 
 
 def adjoint_kernel(
-    members_ref, edge_members_ref, field_ref, edge_field_ref, taps_ref, adjoint_ref, out_ref, x_ref, edge_x_ref
+    shifted_ref, edge_members_ref, field_ref, edge_field_ref, taps_ref, adjoint_ref, out_ref, x_ref, edge_x_ref
 ):
     field, edge_field = field_ref[...], edge_field_ref[...]
-    taps, edge_taps = wide_taps(taps_ref, field), wide_taps(taps_ref, edge_field)
+    steps, edge_taps = field_steps(field, taps_ref), wide_taps(taps_ref, edge_field)
     for tile in range(edge_members_ref.shape[0]):
         edge_x_ref[tile] = smooth(edge_members_ref[tile] * edge_field, edge_taps)
-    for m in range(members_ref.shape[0]):
-        main = smooth(members_ref[m].astype(F32) * field, taps)
+    for m in range(out_ref.shape[0]):
+        main = smooth_product(shifted_ref, m, steps)
         x_ref[m] = patch(main, edge_x_ref[m // SLOTS], DIFF, m % SLOTS)
-    for m in range(members_ref.shape[0]):
+    for m in range(out_ref.shape[0]):
         out_ref[m] = mixed(adjoint_ref, x_ref.at[m])
 
 
@@ -374,10 +429,17 @@
     )
     before = lax.ppermute(low_message, "domain", up)
     after = lax.ppermute(high_message, "domain", down)
-    taps, square, mapped, source, weight, main = call(
-        main_kernel, "first_inner", [shape_of(3, levels, LANES), column, column, level, level, level],
+    group = max(g for g in range(1, 6) if count % g == 0)
+    blocks = shape_of(group * levels, 3 * group * levels, dtype=jnp.bfloat16)
+    split = pltpu.VMEM((count // group, 3 * group * levels, size), jnp.bfloat16)
+    taps, square, mapped, blocks, shifted, source, weight, main = call(
+        main_kernel, "first_inner",
+        [
+            shape_of(3, levels, LANES), column, column, blocks, shape_of(len(SHIFTS), count, levels, size, dtype=perturbations.dtype),
+            level, level, level,
+        ],
         (diffusivity.reshape(1, levels), vertical_map, perturbations, innovations, precision_field, counts),
-        scratch + [pltpu.VMEM((1, levels), F32), pltpu.VMEM((1, size), jnp.int32), pltpu.SemaphoreType.DMA((2,))],
+        [split, scratch[0], pltpu.VMEM((1, levels), F32), pltpu.VMEM((1, size), jnp.int32), pltpu.SemaphoreType.DMA((2,))],
         {0: elsewhere, 5: elsewhere}, work,
     )
     edge_members, edge_source, edge_weight, part = call(
@@ -388,7 +450,7 @@
 
     def adjoint(name, field, edge_field):
         (out,) = call(
-            adjoint_kernel, name, [members_f32], (perturbations, edge_members, field, edge_field, taps, mapped),
+            adjoint_kernel, name, [members_f32], (shifted, edge_members, field, edge_field, taps, mapped),
             [scratch[0], edge_scratch[0]], flops=work,
         )
         return out
@@ -397,8 +459,8 @@
     start = adjoint("start_vector", source, edge_source)
     first, weighted, edge_weighted, part = call(
         second_kernel, "second_apply", [level, level, edge_level, level],
-        (perturbations, edge_members, weight, edge_weight, taps, square, part, *others, start),
-        scratch + edge_scratch, {10: elsewhere}, work + edge_work,
+        (shifted, edge_members, weight, edge_weight, taps, square, blocks, part, *others, start),
+        [split, scratch[0], *edge_scratch], {11: elsewhere}, work + edge_work,
     )
     others = from_partners(part, "member")
     image = adjoint("image_vector", weighted, edge_weighted)

time: 32.7 us -> 32.1 us (0.982)
  Pallas kernels: 7.96 us -> 7.12 us
    pallas_call x8, Pallas kernels: 7.96 us -> 7.12 us  [call(): pl.pallas_call(kernel, name=name, out_shape=list(outs), in_specs=[specs.g...]
  transfers between devices with their start and end apart: 12 -> 12, of which waited for: 9 -> 9; matrix products, arithmetic and copies ran while one was open for 0% -> 0% of each run, Pallas kernels for 10% -> 8%
where the time goes in v5:
time: 32.1 us; the launch traced here: 31.9 us
  starting transfers between devices  15.8 us (49%)
  waiting for transfers between devices  7.45 us (23%)
  Pallas kernels  7.12 us (22%)
  between operations  0.77 us (2%)
  local copies, waits for them, and re-layouts  0.7 us (2%)
    ppermute x6, starting transfers between devices, from_partners(): lax.ppermute(value, axis, [(i, i ^ step) for i in range(size)])  9.35 us
    pallas_call x8, Pallas kernels, call(): pl.pallas_call(kernel, name=name, out_shape=list(outs), in_specs=[specs.g...  7.12 us
    ppermute x6, waiting for transfers between devices, from_partners(): lax.ppermute(value, axis, [(i, i ^ step) for i in range(size)])  4.4 us
    ppermute x4, waiting for transfers between devices, partner(): lax.ppermute(value, axis, [(i, i ^ step) for i in range(lax.axis_size(axi...  3.05 us
    ppermute x4, starting transfers between devices, partner(): lax.ppermute(value, axis, [(i, i ^ step) for i in range(lax.axis_size(axi...  3.03 us
    ppermute x1, starting transfers between devices, local(): after = lax.ppermute(high_message, 'domain', down)  2.96 us
    unnamed x16, local copies, waits for them, and re-layouts  0.7 us
  transfers between devices with their start and end apart: 12, of which 9 were waited for; matrix products, arithmetic and copies ran while one was open for 0% of the time, Pallas kernels for 8%

profile of v5, /device:TPU:0, one launch (start us, length us, event | category | flops | bytes accessed | tf_op | source)
XLA Modules:
  0.0 31.9 jit_solution(12618493713396033480)
XLA Ops:
  0.6 0.0 copy-start
  0.6 0.0 copy-start.1
  0.7 0.0 copy-start.2
  0.7 0.0 copy-start.5
  0.7 1.8 %pack_edges.1 = (f32[7,16,128]{2,1,0:T(8,128)}, f32[7,16,128]{2,1,0:T(8,128)}, f32[2,16,128]{2,1,0:T(8,128)}, f32[2,16,128]{2,1,0:T(8,128)}) custom-call(bf16[25,16,256]{2,1,0:T(8,128)(2,1)} %members_hbm.1, f32[16,256]{1,0:T(8,128)} %innovations_hbm.1, f32[16,256]{1,0:T(8,128)} %precision_hbm.1, s32[1,256]{1,0:T(1,128)} %bitcast.2), custom_call_target="tpu_custom_call" | custom-call | flops 286720 | bytes 386048 | tf_op jit(solution)/shard_map/pack_edges/pallas_call | solution.py:366
  2.5 0.5 %collective-permute-start = (f32[2,16,128]{2,1,0:T(8,128)}, f32[2,16,128]{2,1,0:T(8,128)S(1)}, u32[]{:S(2)}, u32[]{:S(2)}) collective-permute-start(f32[2,16,128]{2,1,0:T(8,128)} %get-tuple-element.29), channel_id=1, source_target_pairs={{0,1},{1,2},{2,3},{3,4},{4,5},{5,6},{6,7},{7,0},{8,9},{9,10},{10,1... | collective-permute-start | bytes 49160 | tf_op jit(solution)/shard_map/ppermute | solution.py:430
  3.0 0.0 copy-start.7
  3.0 3.0 %collective-permute-start.1 = (f32[2,16,128]{2,1,0:T(8,128)}, f32[2,16,128]{2,1,0:T(8,128)S(1)}, u32[]{:S(2)}, u32[]{:S(2)}) collective-permute-start(f32[2,16,128]{2,1,0:T(8,128)} %get-tuple-element.30), channel_id=1, source_target_pairs={{1,0},{2,1},{3,2},{4,3},{5,4},{6,5},{7,6},{0,7},{9,8},{10,9},{11,1... | collective-permute-start | bytes 49160 | tf_op jit(solution)/shard_map/ppermute | solution.py:431
  6.0 0.0 copy-done
  6.0 0.0 copy-done.1
  6.0 0.0 copy-done.2
  6.0 0.0 copy-done.5
  6.0 0.0 copy-done.7
  6.0 0.0 copy-start.6
  6.0 0.7 %copy-done.6 = s32[256]{0:T(256)S(1)} copy-done((s32[256]{0:T(256)S(1)}, s32[256]{0:T(256)}, u32[]{:S(2)}) %copy-start.6) | copy-done | bytes 1048
  6.7 0.0 copy-start.3
  6.7 0.0 copy-start.4
  6.7 1.1 %first_inner.1 = (f32[3,16,128]{2,1,0:T(8,128)S(1)}, f32[16,16,128]{2,1,0:T(8,128)S(1)}, f32[16,16,128]{2,1,0:T(8,128)S(1)}, bf16[80,240]{1,0:T(8,128)(2,1)S(1)}...) custom-call(f32[1,16]{1,0:T(1,128)S(1)} %bitcast.4, ...), custom_call_target="tpu_custom_call" | custom-call | flops 5120000 | bytes 1637952 | tf_op jit(solution)/shard_map/first_inner/pallas_call | solution.py:366
  7.8 0.0 collective-permute-done.before_ref
  7.8 0.0 collective-permute-done.1.after_ref
  7.8 0.0 copy-done.3
  7.8 0.0 copy-done.4
  7.8 0.7 %first_edges.1 = (f32[7,16,128]{2,1,0:T(8,128)S(1)}, f32[16,128]{1,0:T(8,128)S(1)}, f32[16,128]{1,0:T(8,128)S(1)}, f32[16,384]{1,0:T(8,128)S(1)}) custom-call(f32[7,16,128]{2,1,0:T(8,128)S(1)} %copy-done.3, f32[7,16,128]{2,1,0:T(8,128)S(1)} %copy-done.4, f32[2,16,128]{2,1,0:T(8,128)S(1)} %collective-permute-done.before_ref, ...), custom_call_target="tpu_custom_call" | custom-call | flops 716800 | bytes 417792 | tf_op jit(solution)/shard_map/first_edges/pallas_call | solution.py:366
  8.5 4.3 %collective-permute-start.4 = (f32[16,384]{1,0:T(8,128)S(1)}, f32[16,384]{1,0:T(8,128)S(1)}, u32[]{:S(2)}, u32[]{:S(2)}) collective-permute-start(f32[16,384]{1,0:T(8,128)S(1)} %get-tuple-element.37.own_ref), channel_id=1, source_target_pairs={{0,24},{8,16},{16,8},{24,0},{1,25},{9,17},{17,9},{25,1},{2,26},{10... | collective-permute-start | bytes 73736 | tf_op jit(solution)/shard_map/ppermute | solution.py:384
  12.8 0.0 collective-permute-start.3
  12.8 0.6 %collective-permute-start.2 = (f32[16,384]{1,0:T(8,128)S(1)}, f32[16,384]{1,0:T(8,128)S(1)}, u32[]{:S(2)}, u32[]{:S(2)}) collective-permute-start(f32[16,384]{1,0:T(8,128)S(1)} %get-tuple-element.37.own_ref), channel_id=1, source_target_pairs={{0,8},{8,0},{16,24},{24,16},{1,9},{9,1},{17,25},{25,17},{2,10},{10... | collective-permute-start | bytes 73736 | tf_op jit(solution)/shard_map/ppermute | solution.py:384
  13.4 0.8 %start_vector.1._.start_ref = f32[25,16,256]{2,1,0:T(8,128)S(1)} custom-call(bf16[5,25,16,256]{3,2,1,0:T(8,128)(2,1)S(1)} %get-tuple-element.26.shifted_ref, f32[7,16,128]{2,1,0:T(8,128)S(1)} %get-tuple-element.34.edge_members_ref, f32[16,256]{1,0:T(8,128)S(1)} %get-tuple-element.24.field_ref.source_ref, f32[16,128]{1,0:T(8,128)S(1)} %get-tuple-element.38.edge_field_ref, ...), custom_call_target="tpu_custom_call" | custom-call | flops 5120000 | bytes 1671168 | tf_op jit(solution)/shard_map/start_vector/pallas_call | solution.py:366
  14.2 0.4 %collective-permute-done.4.c_ref = f32[16,384]{1,0:T(8,128)S(1)} collective-permute-done((f32[16,384]{1,0:T(8,128)S(1)}, f32[16,384]{1,0:T(8,128)S(1)}, u32[]{:S(2)}, u32[]{:S(2)}) %collective-permute-start.4) | collective-permute-done | bytes 24608 | tf_op jit(solution)/shard_map/ppermute | solution.py:384
  14.7 2.9 %collective-permute-done.3.b_ref = f32[16,384]{1,0:T(8,128)S(1)} collective-permute-done((f32[16,384]{1,0:T(8,128)S(1)}, f32[16,384]{1,0:T(8,128)S(1)}, u32[]{:S(2)}, u32[]{:S(2)}) %collective-permute-start.3) | collective-permute-done | bytes 24608 | tf_op jit(solution)/shard_map/ppermute | solution.py:384
  17.5 0.0 collective-permute-done.2.a_ref
  17.5 0.9 %second_apply.1 = (f32[16,256]{1,0:T(8,128)S(1)}, f32[16,256]{1,0:T(8,128)S(1)}, f32[16,128]{1,0:T(8,128)S(1)}, f32[16,256]{1,0:T(8,128)S(1)}) custom-call(bf16[5,25,16,256]{3,2,1,0:T(8,128)(2,1)S(1)} %get-tuple-element.26.shifted_ref, f32[7,16,128]{2,1,0:T(8,128)S(1)} %get-tuple-element.34.edge_members_ref, f32[16,256]{1,0:T(8,128)S(1)} %get-tuple-element.25.weight_ref, ...), custom_call_target="tpu_custom_call" | custom-call | flops 5836800 | bytes 1865216 | tf_op jit(solution)/shard_map/second_apply/pallas_call | solution.py:366
  18.4 1.5 %collective-permute-start.7 = (f32[16,256]{1,0:T(8,128)S(1)}, f32[16,256]{1,0:T(8,128)S(1)}, u32[]{:S(2)}, u32[]{:S(2)}) collective-permute-start(f32[16,256]{1,0:T(8,128)S(1)} %get-tuple-element.42.own_ref), channel_id=1, source_target_pairs={{0,24},{8,16},{16,8},{24,0},{1,25},{9,17},{17,9},{25,1},{2,26},{10... | collective-permute-start | bytes 49160 | tf_op jit(solution)/shard_map/ppermute | solution.py:384
  19.9 0.6 %collective-permute-start.6 = (f32[16,256]{1,0:T(8,128)S(1)}, f32[16,256]{1,0:T(8,128)S(1)}, u32[]{:S(2)}, u32[]{:S(2)}) collective-permute-start(f32[16,256]{1,0:T(8,128)S(1)} %get-tuple-element.42.own_ref), channel_id=1, source_target_pairs={{0,16},{8,24},{16,0},{24,8},{1,17},{9,25},{17,1},{25,9},{2,18},{10... | collective-permute-start | bytes 49160 | tf_op jit(solution)/shard_map/ppermute | solution.py:384
  20.5 2.3 %collective-permute-start.5 = (f32[16,256]{1,0:T(8,128)S(1)}, f32[16,256]{1,0:T(8,128)S(1)}, u32[]{:S(2)}, u32[]{:S(2)}) collective-permute-start(f32[16,256]{1,0:T(8,128)S(1)} %get-tuple-element.42.own_ref), channel_id=1, source_target_pairs={{0,8},{8,0},{16,24},{24,16},{1,9},{9,1},{17,25},{25,17},{2,10},{10... | collective-permute-start | bytes 49160 | tf_op jit(solution)/shard_map/ppermute | solution.py:384
  22.8 0.8 %image_vector.1._.image_ref = f32[25,16,256]{2,1,0:T(8,128)S(1)} custom-call(bf16[5,25,16,256]{3,2,1,0:T(8,128)(2,1)S(1)} %get-tuple-element.26.shifted_ref, f32[7,16,128]{2,1,0:T(8,128)S(1)} %get-tuple-element.34.edge_members_ref, f32[16,256]{1,0:T(8,128)S(1)} %get-tuple-element.41.field_ref.weighted_ref, f32[16,128]{1,0:T(8,128)S(1)} %get-tuple-element.43.edge_field_ref, ...), custom_call_target="tpu_custom_call" | custom-call | flops 5120000 | bytes 1671168 | tf_op jit(solution)/shard_map/image_vector/pallas_call | solution.py:366
  23.6 0.4 %collective-permute-done.7.c_ref = f32[16,256]{1,0:T(8,128)S(1)} collective-permute-done((f32[16,256]{1,0:T(8,128)S(1)}, f32[16,256]{1,0:T(8,128)S(1)}, u32[]{:S(2)}, u32[]{:S(2)}) %collective-permute-start.7) | collective-permute-done | bytes 16416 | tf_op jit(solution)/shard_map/ppermute | solution.py:384
  24.0 0.5 %collective-permute-done.6.b_ref = f32[16,256]{1,0:T(8,128)S(1)} collective-permute-done((f32[16,256]{1,0:T(8,128)S(1)}, f32[16,256]{1,0:T(8,128)S(1)}, u32[]{:S(2)}, u32[]{:S(2)}) %collective-permute-start.6) | collective-permute-done | bytes 16416 | tf_op jit(solution)/shard_map/ppermute | solution.py:384
  24.5 0.2 collective-permute-done.5.a_ref
  24.7 0.2 moments.1
  24.9 0.0 collective-permute-start.8
  24.9 1.1 %collective-permute-done.8 = f32[1,128]{1,0:T(1,128)S(1)} collective-permute-done((f32[1,128]{1,0:T(1,128)S(1)}, f32[1,128]{1,0:T(1,128)S(1)}, u32[]{:S(2)}, u32[]{:S(2)}) %collective-permute-start.8) | collective-permute-done | bytes 544 | tf_op jit(solution)/shard_map/ppermute | solution.py:388
  26.0 1.6 %collective-permute-start.11 = (f32[1,128]{1,0:T(1,128)S(1)}, f32[1,128]{1,0:T(1,128)S(1)}, u32[]{:S(2)}, u32[]{:S(2)}) collective-permute-start(f32[1,128]{1,0:T(1,128)S(1)} %add.3.own_ref), channel_id=1, source_target_pairs={{0,7},{1,6},{2,5},{3,4},{4,3},{5,2},{6,1},{7,0},{8,15},{9,14},{10,... | collective-permute-start | bytes 1544 | tf_op jit(solution)/shard_map/ppermute | solution.py:388
  27.6 0.4 %collective-permute-start.10 = (f32[1,128]{1,0:T(1,128)S(1)}, f32[1,128]{1,0:T(1,128)S(1)}, u32[]{:S(2)}, u32[]{:S(2)}) collective-permute-start(f32[1,128]{1,0:T(1,128)S(1)} %add.3.own_ref), channel_id=1, source_target_pairs={{0,5},{1,4},{2,7},{3,6},{4,1},{5,0},{6,3},{7,2},{8,13},{9,12},{10,... | collective-permute-start | bytes 1544 | tf_op jit(solution)/shard_map/ppermute | solution.py:388
  28.0 1.0 %collective-permute-start.9 = (f32[1,128]{1,0:T(1,128)S(1)}, f32[1,128]{1,0:T(1,128)S(1)}, u32[]{:S(2)}, u32[]{:S(2)}) collective-permute-start(f32[1,128]{1,0:T(1,128)S(1)} %add.3.own_ref), channel_id=1, source_target_pairs={{0,3},{1,2},{2,1},{3,0},{4,7},{5,6},{6,5},{7,4},{8,11},{9,10},{10,... | collective-permute-start | bytes 1544 | tf_op jit(solution)/shard_map/ppermute | solution.py:388
  29.0 0.8 %collective-permute-done.11.c_ref = f32[1,128]{1,0:T(1,128)S(1)} collective-permute-done((f32[1,128]{1,0:T(1,128)S(1)}, f32[1,128]{1,0:T(1,128)S(1)}, u32[]{:S(2)}, u32[]{:S(2)}) %collective-permute-start.11) | collective-permute-done | bytes 544 | tf_op jit(solution)/shard_map/ppermute | solution.py:388
  29.9 0.7 %collective-permute-done.10.b_ref = f32[1,128]{1,0:T(1,128)S(1)} collective-permute-done((f32[1,128]{1,0:T(1,128)S(1)}, f32[1,128]{1,0:T(1,128)S(1)}, u32[]{:S(2)}, u32[]{:S(2)}) %collective-permute-start.10) | collective-permute-done | bytes 544 | tf_op jit(solution)/shard_map/ppermute | solution.py:388
  30.6 0.4 %collective-permute-done.9.a_ref = f32[1,128]{1,0:T(1,128)S(1)} collective-permute-done((f32[1,128]{1,0:T(1,128)S(1)}, f32[1,128]{1,0:T(1,128)S(1)}, u32[]{:S(2)}, u32[]{:S(2)}) %collective-permute-start.9) | collective-permute-done | bytes 544 | tf_op jit(solution)/shard_map/ppermute | solution.py:388
  31.0 0.9 %combine.1 = (f32[25,16,256]{2,1,0:T(8,128)}, f32[16,256]{1,0:T(8,128)}) custom-call(f32[1,128]{1,0:T(1,128)S(1)} %add.3.own_ref, f32[1,128]{1,0:T(1,128)S(1)} %collective-permute-done.9.a_ref, f32[1,128]{1,0:T(1,128)S(1)} %collective-permute-done.10.b_ref, f32[1,128]{1,0:T(1,128)S(1)} %collective-permute-done.11.c_ref, ...), custom_call_target="tpu_custom_call" | custom-call | bytes 1280000 | tf_op jit(solution)/shard_map/combine/pallas_call | solution.py:366
  (1 shorter events, 0.0 us)
Async XLA Ops:
  0.6 5.3 %copy-start = (bf16[25,16,256]{2,1,0:T(8,128)(2,1)S(1)}, bf16[25,16,256]{2,1,0:T(8,128)(2,1)}, u32[]{:S(2)}) copy-start(bf16[25,16,256]{2,1,0:T(8,128)(2,1)} %members_hbm.1) | copy-start | bytes 614404
  0.6 5.3 %copy-start.1 = (f32[16,256]{1,0:T(8,128)S(1)}, f32[16,256]{1,0:T(8,128)}, u32[]{:S(2)}) copy-start(f32[16,256]{1,0:T(8,128)} %innovations_hbm.1) | copy-start | bytes 49156
  0.7 5.3 %copy-start.2 = (f32[16,256]{1,0:T(8,128)S(1)}, f32[16,256]{1,0:T(8,128)}, u32[]{:S(2)}) copy-start(f32[16,256]{1,0:T(8,128)} %precision_hbm.1) | copy-start | bytes 49156
  0.7 5.3 %copy-start.5 = (f32[16,16]{1,0:T(8,128)S(1)}, f32[16,16]{1,0:T(8,128)}, u32[]{:S(2)}) copy-start(f32[16,16]{1,0:T(8,128)} %map_ref.1) | copy-start | bytes 3076
  2.5 5.3 %collective-permute-start = (f32[2,16,128]{2,1,0:T(8,128)}, f32[2,16,128]{2,1,0:T(8,128)S(1)}, u32[]{:S(2)}, u32[]{:S(2)}) collective-permute-start(f32[2,16,128]{2,1,0:T(8,128)} %get-tuple-element.29), channel_id=1, source_target_pairs={{0,1},{1,2},{2,3},{3,4},{4,5},{5,6},{6,7},{7,0},{8,9},{9,10},{10,1... | collective-permute-start | bytes 49160 | tf_op jit(solution)/shard_map/ppermute | solution.py:430
  3.0 3.0 %copy-start.7 = (f32[16]{0:T(128)S(1)}, f32[16]{0:T(128)}, u32[]{:S(2)}) copy-start(f32[16]{0:T(128)} %param.11) | copy-start | bytes 196
  3.0 4.8 %collective-permute-start.1 = (f32[2,16,128]{2,1,0:T(8,128)}, f32[2,16,128]{2,1,0:T(8,128)S(1)}, u32[]{:S(2)}, u32[]{:S(2)}) collective-permute-start(f32[2,16,128]{2,1,0:T(8,128)} %get-tuple-element.30), channel_id=1, source_target_pairs={{1,0},{2,1},{3,2},{4,3},{5,4},{6,5},{7,6},{0,7},{9,8},{10,9},{11,1... | collective-permute-start | bytes 49160 | tf_op jit(solution)/shard_map/ppermute | solution.py:431
  6.0 0.7 %copy-start.6 = (s32[256]{0:T(256)S(1)}, s32[256]{0:T(256)}, u32[]{:S(2)}) copy-start(s32[256]{0:T(256)} %param.9) | copy-start | bytes 3076
  6.7 1.1 %copy-start.3 = (f32[7,16,128]{2,1,0:T(8,128)S(1)}, f32[7,16,128]{2,1,0:T(8,128)}, u32[]{:S(2)}) copy-start(f32[7,16,128]{2,1,0:T(8,128)} %get-tuple-element.27.low_ref) | copy-start | bytes 172036
  6.7 1.1 %copy-start.4 = (f32[7,16,128]{2,1,0:T(8,128)S(1)}, f32[7,16,128]{2,1,0:T(8,128)}, u32[]{:S(2)}) copy-start(f32[7,16,128]{2,1,0:T(8,128)} %get-tuple-element.28.high_ref) | copy-start | bytes 172036
  8.5 6.2 %collective-permute-start.4 = (f32[16,384]{1,0:T(8,128)S(1)}, f32[16,384]{1,0:T(8,128)S(1)}, u32[]{:S(2)}, u32[]{:S(2)}) collective-permute-start(f32[16,384]{1,0:T(8,128)S(1)} %get-tuple-element.37.own_ref), channel_id=1, source_target_pairs={{0,24},{8,16},{16,8},{24,0},{1,25},{9,17},{17,9},{25,1},{2,26},{10... | collective-permute-start | bytes 73736 | tf_op jit(solution)/shard_map/ppermute | solution.py:384
  12.8 4.7 %collective-permute-start.3 = (f32[16,384]{1,0:T(8,128)S(1)}, f32[16,384]{1,0:T(8,128)S(1)}, u32[]{:S(2)}, u32[]{:S(2)}) collective-permute-start(f32[16,384]{1,0:T(8,128)S(1)} %get-tuple-element.37.own_ref), channel_id=1, source_target_pairs={{0,16},{8,24},{16,0},{24,8},{1,17},{9,25},{17,1},{25,9},{2,18},{10... | collective-permute-start | bytes 73736 | tf_op jit(solution)/shard_map/ppermute | solution.py:384
  12.8 4.7 %collective-permute-start.2 = (f32[16,384]{1,0:T(8,128)S(1)}, f32[16,384]{1,0:T(8,128)S(1)}, u32[]{:S(2)}, u32[]{:S(2)}) collective-permute-start(f32[16,384]{1,0:T(8,128)S(1)} %get-tuple-element.37.own_ref), channel_id=1, source_target_pairs={{0,8},{8,0},{16,24},{24,16},{1,9},{9,1},{17,25},{25,17},{2,10},{10... | collective-permute-start | bytes 73736 | tf_op jit(solution)/shard_map/ppermute | solution.py:384
  18.4 5.6 %collective-permute-start.7 = (f32[16,256]{1,0:T(8,128)S(1)}, f32[16,256]{1,0:T(8,128)S(1)}, u32[]{:S(2)}, u32[]{:S(2)}) collective-permute-start(f32[16,256]{1,0:T(8,128)S(1)} %get-tuple-element.42.own_ref), channel_id=1, source_target_pairs={{0,24},{8,16},{16,8},{24,0},{1,25},{9,17},{17,9},{25,1},{2,26},{10... | collective-permute-start | bytes 49160 | tf_op jit(solution)/shard_map/ppermute | solution.py:384
  19.9 4.7 %collective-permute-start.6 = (f32[16,256]{1,0:T(8,128)S(1)}, f32[16,256]{1,0:T(8,128)S(1)}, u32[]{:S(2)}, u32[]{:S(2)}) collective-permute-start(f32[16,256]{1,0:T(8,128)S(1)} %get-tuple-element.42.own_ref), channel_id=1, source_target_pairs={{0,16},{8,24},{16,0},{24,8},{1,17},{9,25},{17,1},{25,9},{2,18},{10... | collective-permute-start | bytes 49160 | tf_op jit(solution)/shard_map/ppermute | solution.py:384
  20.5 4.2 %collective-permute-start.5 = (f32[16,256]{1,0:T(8,128)S(1)}, f32[16,256]{1,0:T(8,128)S(1)}, u32[]{:S(2)}, u32[]{:S(2)}) collective-permute-start(f32[16,256]{1,0:T(8,128)S(1)} %get-tuple-element.42.own_ref), channel_id=1, source_target_pairs={{0,8},{8,0},{16,24},{24,16},{1,9},{9,1},{17,25},{25,17},{2,10},{10... | collective-permute-start | bytes 49160 | tf_op jit(solution)/shard_map/ppermute | solution.py:384
  24.9 1.1 %collective-permute-start.8 = (f32[1,128]{1,0:T(1,128)S(1)}, f32[1,128]{1,0:T(1,128)S(1)}, u32[]{:S(2)}, u32[]{:S(2)}) collective-permute-start(f32[1,128]{1,0:T(1,128)S(1)} %get-tuple-element.44), channel_id=1, source_target_pairs={{0,1},{1,0},{2,3},{3,2},{4,5},{5,4},{6,7},{7,6},{8,9},{9,8},{10,11... | collective-permute-start | bytes 1544 | tf_op jit(solution)/shard_map/ppermute | solution.py:388
  26.0 3.9 %collective-permute-start.11 = (f32[1,128]{1,0:T(1,128)S(1)}, f32[1,128]{1,0:T(1,128)S(1)}, u32[]{:S(2)}, u32[]{:S(2)}) collective-permute-start(f32[1,128]{1,0:T(1,128)S(1)} %add.3.own_ref), channel_id=1, source_target_pairs={{0,7},{1,6},{2,5},{3,4},{4,3},{5,2},{6,1},{7,0},{8,15},{9,14},{10,... | collective-permute-start | bytes 1544 | tf_op jit(solution)/shard_map/ppermute | solution.py:388
  27.6 3.0 %collective-permute-start.10 = (f32[1,128]{1,0:T(1,128)S(1)}, f32[1,128]{1,0:T(1,128)S(1)}, u32[]{:S(2)}, u32[]{:S(2)}) collective-permute-start(f32[1,128]{1,0:T(1,128)S(1)} %add.3.own_ref), channel_id=1, source_target_pairs={{0,5},{1,4},{2,7},{3,6},{4,1},{5,0},{6,3},{7,2},{8,13},{9,12},{10,... | collective-permute-start | bytes 1544 | tf_op jit(solution)/shard_map/ppermute | solution.py:388
  28.0 3.0 %collective-permute-start.9 = (f32[1,128]{1,0:T(1,128)S(1)}, f32[1,128]{1,0:T(1,128)S(1)}, u32[]{:S(2)}, u32[]{:S(2)}) collective-permute-start(f32[1,128]{1,0:T(1,128)S(1)} %add.3.own_ref), channel_id=1, source_target_pairs={{0,3},{1,2},{2,1},{3,0},{4,7},{5,6},{6,5},{7,4},{8,11},{9,10},{10,... | collective-permute-start | bytes 1544 | tf_op jit(solution)/shard_map/ppermute | solution.py:388

commit v6 on v5

--- a/solution.py
+++ b/solution.py
@@ -117,11 +117,8 @@
 
 
 def all_slots(value):
-    shift = SLOT
-    while shift < LANES:
-        value = value + lane_roll(value, shift)
-        shift *= 2
-    return value
+    one, two, three = (lane_roll(value, k * SLOT) for k in (1, 2, 3))
+    return (value + two) + (one + three)
 
 
 def ends_of(first, last, lane):
@@ -301,15 +298,11 @@
     first, weighted = first_ref[...], weighted_ref[...]
     second = tree_sum(own_ref, a_ref, b_ref, c_ref)
     second_ref[...] = second
-    lane = lane_index((1, LANES))
-    width = LANES // 4
-    out = jnp.zeros((1, LANES), F32)
+    kind = lax.broadcasted_iota(jnp.int32, moments_ref.shape, 0)
+    out = jnp.zeros(moments_ref.shape, F32)
     for i, product in enumerate((source * first, weighted * first, weighted * second, weight * second * second)):
         row = sum(product[:, at : at + LANES] for at in range(0, size, LANES))
-        row = jnp.sum(row, axis=0, keepdims=True)
-        row = row + lane_roll(row, LANES // 2)
-        row = row + lane_roll(row, LANES // 4)
-        out = jnp.where((lane >= i * width) & (lane < (i + 1) * width), row, out)
+        out = jnp.where(kind == i, jnp.sum(row, axis=0, keepdims=True), out)
     moments_ref[...] = out
 
 
@@ -330,15 +323,12 @@
 def final_kernel(
     own_ref, a_ref, b_ref, c_ref, start_ref, image_ref, first_ref, second_ref, control_ref, increment_ref
 ):
-    lane = lane_index((1, LANES))
-    width = LANES // 4
-    row = tree_sum(own_ref, a_ref, b_ref, c_ref)
-    sums = [
-        jnp.sum(jnp.where((lane >= i * width) & (lane < (i + 1) * width), row, 0.0), axis=1, keepdims=True)
-        for i in range(4)
-    ]
-    m1, m2, m3 = (value / sums[0] for value in sums[1:])
-    alpha = 1.0 / (1.0 + m1)
+    total = tree_sum(own_ref, a_ref, b_ref, c_ref)
+    total = jnp.broadcast_to(jnp.sum(total, axis=1, keepdims=True), total.shape)
+    mu = [total[i : i + 1, :] for i in range(4)]
+    alpha = mu[0] / (mu[0] + mu[1])
+    scale = 1.0 / mu[0]
+    m1, m2, m3 = (value * scale for value in mu[1:])
     spread = jnp.maximum(m2 - m1 * m1, 0.0)
     bend = jnp.maximum(m3 - 2.0 * m1 * m2 + m1 * m1 * m1, 0.0)
     beta = alpha * alpha * spread
@@ -347,6 +337,8 @@
     later = jnp.where(usable, jnp.minimum(spread / jnp.where(usable, below, 1.0), 1.0), 0.0)
     on_start = alpha + later * (alpha * m1 + beta)
     on_image = -later * alpha
+    on_start = jnp.broadcast_to(widen(on_start, first_ref), first_ref.shape)
+    on_image = jnp.broadcast_to(widen(on_image, first_ref), first_ref.shape)
     increment_ref[...] = on_start * first_ref[...] + on_image * second_ref[...]
     for m in range(start_ref.shape[0]):
         control_ref[m] = on_start * start_ref[m] + on_image * image_ref[m]
@@ -409,7 +401,7 @@
     level = shape_of(levels, size)
     members_f32 = shape_of(count, levels, size)
     edge_tiles = shape_of(tiles, levels, LANES)
-    edge_row = shape_of(1, LANES)
+    moment_rows = shape_of(8, LANES)
     edge_level = shape_of(levels, LANES)
     message = shape_of(-(-tiles * HALO // SLOT), levels, LANES)
     column = shape_of(levels, levels, LANES)
@@ -465,7 +457,7 @@
     others = from_partners(part, "member")
     image = adjoint("image_vector", weighted, edge_weighted)
     second, moments = call(
-        moments_kernel, "moments", [level, edge_row],
+        moments_kernel, "moments", [level, moment_rows],
         (source, weight, first, weighted, part, *others, image), (), {8: elsewhere},
     )
     moments = domain_terms(moments, "domain")

time: 32.1 us -> 31.9 us (level)
  Pallas kernels: 7.12 us -> 6.78 us
    pallas_call x8, Pallas kernels: 7.12 us -> 6.78 us  [call(): pl.pallas_call(kernel, name=name, out_shape=list(outs), in_specs=[specs.g...]
where the time goes in v6:
time: 31.9 us; the launch traced here: 31.7 us
  starting transfers between devices  15.9 us (50%)
  waiting for transfers between devices  7.6 us (24%)
  Pallas kernels  6.78 us (21%)
  between operations  0.77 us (2%)
  local copies, waits for them, and re-layouts  0.7 us (2%)
    ppermute x6, starting transfers between devices, from_partners(): lax.ppermute(value, axis, [(i, i ^ step) for i in range(size)])  9.37 us
    pallas_call x8, Pallas kernels, call(): pl.pallas_call(kernel, name=name, out_shape=list(outs), in_specs=[specs.g...  6.78 us
    ppermute x6, waiting for transfers between devices, from_partners(): lax.ppermute(value, axis, [(i, i ^ step) for i in range(size)])  4.4 us
    ppermute x4, waiting for transfers between devices, partner(): lax.ppermute(value, axis, [(i, i ^ step) for i in range(lax.axis_size(axi...  3.2 us
    ppermute x4, starting transfers between devices, partner(): lax.ppermute(value, axis, [(i, i ^ step) for i in range(lax.axis_size(axi...  3.05 us
    ppermute x1, starting transfers between devices, local(): after = lax.ppermute(high_message, 'domain', down)  2.96 us
    unnamed x16, local copies, waits for them, and re-layouts  0.7 us
  transfers between devices with their start and end apart: 12, of which 9 were waited for; matrix products, arithmetic and copies ran while one was open for 0% of the time, Pallas kernels for 8%

profile of v6, /device:TPU:0, one launch (start us, length us, event | category | flops | bytes accessed | tf_op | source)
XLA Modules:
  0.0 31.7 jit_solution(7356145562015712408)
XLA Ops:
  0.6 0.0 copy-start
  0.6 0.0 copy-start.1
  0.7 0.0 copy-start.2
  0.7 0.0 copy-start.5
  0.7 1.8 %pack_edges.1 = (f32[7,16,128]{2,1,0:T(8,128)}, f32[7,16,128]{2,1,0:T(8,128)}, f32[2,16,128]{2,1,0:T(8,128)}, f32[2,16,128]{2,1,0:T(8,128)}) custom-call(bf16[25,16,256]{2,1,0:T(8,128)(2,1)} %members_hbm.1, f32[16,256]{1,0:T(8,128)} %innovations_hbm.1, f32[16,256]{1,0:T(8,128)} %precision_hbm.1, s32[1,256]{1,0:T(1,128)} %bitcast.2), custom_call_target="tpu_custom_call" | custom-call | flops 286720 | bytes 386048 | tf_op jit(solution)/shard_map/pack_edges/pallas_call | solution.py:358
  2.5 0.5 %collective-permute-start = (f32[2,16,128]{2,1,0:T(8,128)}, f32[2,16,128]{2,1,0:T(8,128)S(1)}, u32[]{:S(2)}, u32[]{:S(2)}) collective-permute-start(f32[2,16,128]{2,1,0:T(8,128)} %get-tuple-element.29), channel_id=1, source_target_pairs={{0,1},{1,2},{2,3},{3,4},{4,5},{5,6},{6,7},{7,0},{8,9},{9,10},{10,1... | collective-permute-start | bytes 49160 | tf_op jit(solution)/shard_map/ppermute | solution.py:422
  3.0 0.0 copy-start.7
  3.0 3.0 %collective-permute-start.1 = (f32[2,16,128]{2,1,0:T(8,128)}, f32[2,16,128]{2,1,0:T(8,128)S(1)}, u32[]{:S(2)}, u32[]{:S(2)}) collective-permute-start(f32[2,16,128]{2,1,0:T(8,128)} %get-tuple-element.30), channel_id=1, source_target_pairs={{1,0},{2,1},{3,2},{4,3},{5,4},{6,5},{7,6},{0,7},{9,8},{10,9},{11,1... | collective-permute-start | bytes 49160 | tf_op jit(solution)/shard_map/ppermute | solution.py:423
  6.0 0.0 copy-done
  6.0 0.0 copy-done.1
  6.0 0.0 copy-done.2
  6.0 0.0 copy-done.5
  6.0 0.0 copy-done.7
  6.0 0.0 copy-start.6
  6.0 0.7 %copy-done.6 = s32[256]{0:T(256)S(1)} copy-done((s32[256]{0:T(256)S(1)}, s32[256]{0:T(256)}, u32[]{:S(2)}) %copy-start.6) | copy-done | bytes 1048
  6.7 0.0 copy-start.3
  6.7 0.0 copy-start.4
  6.7 1.1 %first_inner.1 = (f32[3,16,128]{2,1,0:T(8,128)S(1)}, f32[16,16,128]{2,1,0:T(8,128)S(1)}, f32[16,16,128]{2,1,0:T(8,128)S(1)}, bf16[80,240]{1,0:T(8,128)(2,1)S(1)}...) custom-call(f32[1,16]{1,0:T(1,128)S(1)} %bitcast.4, ...), custom_call_target="tpu_custom_call" | custom-call | flops 5120000 | bytes 1637952 | tf_op jit(solution)/shard_map/first_inner/pallas_call | solution.py:358
  7.8 0.0 collective-permute-done.before_ref
  7.8 0.0 collective-permute-done.1.after_ref
  7.8 0.0 copy-done.3
  7.8 0.0 copy-done.4
  7.8 0.5 %first_edges.1 = (f32[7,16,128]{2,1,0:T(8,128)S(1)}, f32[16,128]{1,0:T(8,128)S(1)}, f32[16,128]{1,0:T(8,128)S(1)}, f32[16,384]{1,0:T(8,128)S(1)}) custom-call(f32[7,16,128]{2,1,0:T(8,128)S(1)} %copy-done.3, f32[7,16,128]{2,1,0:T(8,128)S(1)} %copy-done.4, f32[2,16,128]{2,1,0:T(8,128)S(1)} %collective-permute-done.before_ref, ...), custom_call_target="tpu_custom_call" | custom-call | flops 716800 | bytes 417792 | tf_op jit(solution)/shard_map/first_edges/pallas_call | solution.py:358
  8.4 4.3 %collective-permute-start.4 = (f32[16,384]{1,0:T(8,128)S(1)}, f32[16,384]{1,0:T(8,128)S(1)}, u32[]{:S(2)}, u32[]{:S(2)}) collective-permute-start(f32[16,384]{1,0:T(8,128)S(1)} %get-tuple-element.37.own_ref), channel_id=1, source_target_pairs={{0,24},{8,16},{16,8},{24,0},{1,25},{9,17},{17,9},{25,1},{2,26},{10... | collective-permute-start | bytes 73736 | tf_op jit(solution)/shard_map/ppermute | solution.py:376
  12.7 0.0 collective-permute-start.3
  12.7 0.6 %collective-permute-start.2 = (f32[16,384]{1,0:T(8,128)S(1)}, f32[16,384]{1,0:T(8,128)S(1)}, u32[]{:S(2)}, u32[]{:S(2)}) collective-permute-start(f32[16,384]{1,0:T(8,128)S(1)} %get-tuple-element.37.own_ref), channel_id=1, source_target_pairs={{0,8},{8,0},{16,24},{24,16},{1,9},{9,1},{17,25},{25,17},{2,10},{10... | collective-permute-start | bytes 73736 | tf_op jit(solution)/shard_map/ppermute | solution.py:376
  13.3 0.8 %start_vector.1._.start_ref = f32[25,16,256]{2,1,0:T(8,128)S(1)} custom-call(bf16[5,25,16,256]{3,2,1,0:T(8,128)(2,1)S(1)} %get-tuple-element.26.shifted_ref, f32[7,16,128]{2,1,0:T(8,128)S(1)} %get-tuple-element.34.edge_members_ref, f32[16,256]{1,0:T(8,128)S(1)} %get-tuple-element.24.field_ref.source_ref, f32[16,128]{1,0:T(8,128)S(1)} %get-tuple-element.38.edge_field_ref, ...), custom_call_target="tpu_custom_call" | custom-call | flops 5120000 | bytes 1671168 | tf_op jit(solution)/shard_map/start_vector/pallas_call | solution.py:358
  14.1 0.4 %collective-permute-done.4.c_ref = f32[16,384]{1,0:T(8,128)S(1)} collective-permute-done((f32[16,384]{1,0:T(8,128)S(1)}, f32[16,384]{1,0:T(8,128)S(1)}, u32[]{:S(2)}, u32[]{:S(2)}) %collective-permute-start.4) | collective-permute-done | bytes 24608 | tf_op jit(solution)/shard_map/ppermute | solution.py:376
  14.5 2.9 %collective-permute-done.3.b_ref = f32[16,384]{1,0:T(8,128)S(1)} collective-permute-done((f32[16,384]{1,0:T(8,128)S(1)}, f32[16,384]{1,0:T(8,128)S(1)}, u32[]{:S(2)}, u32[]{:S(2)}) %collective-permute-start.3) | collective-permute-done | bytes 24608 | tf_op jit(solution)/shard_map/ppermute | solution.py:376
  17.4 0.0 collective-permute-done.2.a_ref
  17.4 0.8 %second_apply.1 = (f32[16,256]{1,0:T(8,128)S(1)}, f32[16,256]{1,0:T(8,128)S(1)}, f32[16,128]{1,0:T(8,128)S(1)}, f32[16,256]{1,0:T(8,128)S(1)}) custom-call(bf16[5,25,16,256]{3,2,1,0:T(8,128)(2,1)S(1)} %get-tuple-element.26.shifted_ref, f32[7,16,128]{2,1,0:T(8,128)S(1)} %get-tuple-element.34.edge_members_ref, f32[16,256]{1,0:T(8,128)S(1)} %get-tuple-element.25.weight_ref, ...), custom_call_target="tpu_custom_call" | custom-call | flops 5836800 | bytes 1865216 | tf_op jit(solution)/shard_map/second_apply/pallas_call | solution.py:358
  18.2 1.5 %collective-permute-start.7 = (f32[16,256]{1,0:T(8,128)S(1)}, f32[16,256]{1,0:T(8,128)S(1)}, u32[]{:S(2)}, u32[]{:S(2)}) collective-permute-start(f32[16,256]{1,0:T(8,128)S(1)} %get-tuple-element.42.own_ref), channel_id=1, source_target_pairs={{0,24},{8,16},{16,8},{24,0},{1,25},{9,17},{17,9},{25,1},{2,26},{10... | collective-permute-start | bytes 49160 | tf_op jit(solution)/shard_map/ppermute | solution.py:376
  19.7 0.6 %collective-permute-start.6 = (f32[16,256]{1,0:T(8,128)S(1)}, f32[16,256]{1,0:T(8,128)S(1)}, u32[]{:S(2)}, u32[]{:S(2)}) collective-permute-start(f32[16,256]{1,0:T(8,128)S(1)} %get-tuple-element.42.own_ref), channel_id=1, source_target_pairs={{0,16},{8,24},{16,0},{24,8},{1,17},{9,25},{17,1},{25,9},{2,18},{10... | collective-permute-start | bytes 49160 | tf_op jit(solution)/shard_map/ppermute | solution.py:376
  20.3 2.3 %collective-permute-start.5 = (f32[16,256]{1,0:T(8,128)S(1)}, f32[16,256]{1,0:T(8,128)S(1)}, u32[]{:S(2)}, u32[]{:S(2)}) collective-permute-start(f32[16,256]{1,0:T(8,128)S(1)} %get-tuple-element.42.own_ref), channel_id=1, source_target_pairs={{0,8},{8,0},{16,24},{24,16},{1,9},{9,1},{17,25},{25,17},{2,10},{10... | collective-permute-start | bytes 49160 | tf_op jit(solution)/shard_map/ppermute | solution.py:376
  22.6 0.8 %image_vector.1._.image_ref = f32[25,16,256]{2,1,0:T(8,128)S(1)} custom-call(bf16[5,25,16,256]{3,2,1,0:T(8,128)(2,1)S(1)} %get-tuple-element.26.shifted_ref, f32[7,16,128]{2,1,0:T(8,128)S(1)} %get-tuple-element.34.edge_members_ref, f32[16,256]{1,0:T(8,128)S(1)} %get-tuple-element.41.field_ref.weighted_ref, f32[16,128]{1,0:T(8,128)S(1)} %get-tuple-element.43.edge_field_ref, ...), custom_call_target="tpu_custom_call" | custom-call | flops 5120000 | bytes 1671168 | tf_op jit(solution)/shard_map/image_vector/pallas_call | solution.py:358
  23.4 0.4 %collective-permute-done.7.c_ref = f32[16,256]{1,0:T(8,128)S(1)} collective-permute-done((f32[16,256]{1,0:T(8,128)S(1)}, f32[16,256]{1,0:T(8,128)S(1)}, u32[]{:S(2)}, u32[]{:S(2)}) %collective-permute-start.7) | collective-permute-done | bytes 16416 | tf_op jit(solution)/shard_map/ppermute | solution.py:376
  23.8 0.5 %collective-permute-done.6.b_ref = f32[16,256]{1,0:T(8,128)S(1)} collective-permute-done((f32[16,256]{1,0:T(8,128)S(1)}, f32[16,256]{1,0:T(8,128)S(1)}, u32[]{:S(2)}, u32[]{:S(2)}) %collective-permute-start.6) | collective-permute-done | bytes 16416 | tf_op jit(solution)/shard_map/ppermute | solution.py:376
  24.4 0.2 collective-permute-done.5.a_ref
  24.5 0.1 collective-permute-start.8
  24.6 1.2 %collective-permute-done.8 = f32[8,128]{1,0:T(8,128)S(1)} collective-permute-done((f32[8,128]{1,0:T(8,128)S(1)}, f32[8,128]{1,0:T(8,128)S(1)}, u32[]{:S(2)}, u32[]{:S(2)}) %collective-permute-start.8) | collective-permute-done | bytes 4128 | tf_op jit(solution)/shard_map/ppermute | solution.py:380
  25.8 1.6 %collective-permute-start.11 = (f32[8,128]{1,0:T(8,128)S(1)}, f32[8,128]{1,0:T(8,128)S(1)}, u32[]{:S(2)}, u32[]{:S(2)}) collective-permute-start(f32[8,128]{1,0:T(8,128)S(1)} %add.3.own_ref), channel_id=1, source_target_pairs={{0,7},{1,6},{2,5},{3,4},{4,3},{5,2},{6,1},{7,0},{8,15},{9,14},{10,... | collective-permute-start | bytes 12296 | tf_op jit(solution)/shard_map/ppermute | solution.py:380
  27.4 0.4 %collective-permute-start.10 = (f32[8,128]{1,0:T(8,128)S(1)}, f32[8,128]{1,0:T(8,128)S(1)}, u32[]{:S(2)}, u32[]{:S(2)}) collective-permute-start(f32[8,128]{1,0:T(8,128)S(1)} %add.3.own_ref), channel_id=1, source_target_pairs={{0,5},{1,4},{2,7},{3,6},{4,1},{5,0},{6,3},{7,2},{8,13},{9,12},{10,... | collective-permute-start | bytes 12296 | tf_op jit(solution)/shard_map/ppermute | solution.py:380
  27.8 1.0 %collective-permute-start.9 = (f32[8,128]{1,0:T(8,128)S(1)}, f32[8,128]{1,0:T(8,128)S(1)}, u32[]{:S(2)}, u32[]{:S(2)}) collective-permute-start(f32[8,128]{1,0:T(8,128)S(1)} %add.3.own_ref), channel_id=1, source_target_pairs={{0,3},{1,2},{2,1},{3,0},{4,7},{5,6},{6,5},{7,4},{8,11},{9,10},{10,... | collective-permute-start | bytes 12296 | tf_op jit(solution)/shard_map/ppermute | solution.py:380
  28.8 0.9 %collective-permute-done.11.c_ref = f32[8,128]{1,0:T(8,128)S(1)} collective-permute-done((f32[8,128]{1,0:T(8,128)S(1)}, f32[8,128]{1,0:T(8,128)S(1)}, u32[]{:S(2)}, u32[]{:S(2)}) %collective-permute-start.11) | collective-permute-done | bytes 4128 | tf_op jit(solution)/shard_map/ppermute | solution.py:380
  29.7 0.7 %collective-permute-done.10.b_ref = f32[8,128]{1,0:T(8,128)S(1)} collective-permute-done((f32[8,128]{1,0:T(8,128)S(1)}, f32[8,128]{1,0:T(8,128)S(1)}, u32[]{:S(2)}, u32[]{:S(2)}) %collective-permute-start.10) | collective-permute-done | bytes 4128 | tf_op jit(solution)/shard_map/ppermute | solution.py:380
  30.4 0.4 %collective-permute-done.9.a_ref = f32[8,128]{1,0:T(8,128)S(1)} collective-permute-done((f32[8,128]{1,0:T(8,128)S(1)}, f32[8,128]{1,0:T(8,128)S(1)}, u32[]{:S(2)}, u32[]{:S(2)}) %collective-permute-start.9) | collective-permute-done | bytes 4128 | tf_op jit(solution)/shard_map/ppermute | solution.py:380
  30.8 0.9 %combine.1 = (f32[25,16,256]{2,1,0:T(8,128)}, f32[16,256]{1,0:T(8,128)}) custom-call(f32[8,128]{1,0:T(8,128)S(1)} %add.3.own_ref, f32[8,128]{1,0:T(8,128)S(1)} %collective-permute-done.9.a_ref, f32[8,128]{1,0:T(8,128)S(1)} %collective-permute-done.10.b_ref, f32[8,128]{1,0:T(8,128)S(1)} %collective-permute-done.11.c_ref, ...), custom_call_target="tpu_custom_call" | custom-call | bytes 1294336 | tf_op jit(solution)/shard_map/combine/pallas_call | solution.py:358
  (2 shorter events, 0.0 us)
Async XLA Ops:
  0.6 5.3 %copy-start = (bf16[25,16,256]{2,1,0:T(8,128)(2,1)S(1)}, bf16[25,16,256]{2,1,0:T(8,128)(2,1)}, u32[]{:S(2)}) copy-start(bf16[25,16,256]{2,1,0:T(8,128)(2,1)} %members_hbm.1) | copy-start | bytes 614404
  0.6 5.3 %copy-start.1 = (f32[16,256]{1,0:T(8,128)S(1)}, f32[16,256]{1,0:T(8,128)}, u32[]{:S(2)}) copy-start(f32[16,256]{1,0:T(8,128)} %innovations_hbm.1) | copy-start | bytes 49156
  0.7 5.3 %copy-start.2 = (f32[16,256]{1,0:T(8,128)S(1)}, f32[16,256]{1,0:T(8,128)}, u32[]{:S(2)}) copy-start(f32[16,256]{1,0:T(8,128)} %precision_hbm.1) | copy-start | bytes 49156
  0.7 5.3 %copy-start.5 = (f32[16,16]{1,0:T(8,128)S(1)}, f32[16,16]{1,0:T(8,128)}, u32[]{:S(2)}) copy-start(f32[16,16]{1,0:T(8,128)} %map_ref.1) | copy-start | bytes 3076
  2.5 5.3 %collective-permute-start = (f32[2,16,128]{2,1,0:T(8,128)}, f32[2,16,128]{2,1,0:T(8,128)S(1)}, u32[]{:S(2)}, u32[]{:S(2)}) collective-permute-start(f32[2,16,128]{2,1,0:T(8,128)} %get-tuple-element.29), channel_id=1, source_target_pairs={{0,1},{1,2},{2,3},{3,4},{4,5},{5,6},{6,7},{7,0},{8,9},{9,10},{10,1... | collective-permute-start | bytes 49160 | tf_op jit(solution)/shard_map/ppermute | solution.py:422
  3.0 3.0 %copy-start.7 = (f32[16]{0:T(128)S(1)}, f32[16]{0:T(128)}, u32[]{:S(2)}) copy-start(f32[16]{0:T(128)} %param.11) | copy-start | bytes 196
  3.0 4.8 %collective-permute-start.1 = (f32[2,16,128]{2,1,0:T(8,128)}, f32[2,16,128]{2,1,0:T(8,128)S(1)}, u32[]{:S(2)}, u32[]{:S(2)}) collective-permute-start(f32[2,16,128]{2,1,0:T(8,128)} %get-tuple-element.30), channel_id=1, source_target_pairs={{1,0},{2,1},{3,2},{4,3},{5,4},{6,5},{7,6},{0,7},{9,8},{10,9},{11,1... | collective-permute-start | bytes 49160 | tf_op jit(solution)/shard_map/ppermute | solution.py:423
  6.0 0.7 %copy-start.6 = (s32[256]{0:T(256)S(1)}, s32[256]{0:T(256)}, u32[]{:S(2)}) copy-start(s32[256]{0:T(256)} %param.9) | copy-start | bytes 3076
  6.7 1.1 %copy-start.3 = (f32[7,16,128]{2,1,0:T(8,128)S(1)}, f32[7,16,128]{2,1,0:T(8,128)}, u32[]{:S(2)}) copy-start(f32[7,16,128]{2,1,0:T(8,128)} %get-tuple-element.27.low_ref) | copy-start | bytes 172036
  6.7 1.1 %copy-start.4 = (f32[7,16,128]{2,1,0:T(8,128)S(1)}, f32[7,16,128]{2,1,0:T(8,128)}, u32[]{:S(2)}) copy-start(f32[7,16,128]{2,1,0:T(8,128)} %get-tuple-element.28.high_ref) | copy-start | bytes 172036
  8.4 6.2 %collective-permute-start.4 = (f32[16,384]{1,0:T(8,128)S(1)}, f32[16,384]{1,0:T(8,128)S(1)}, u32[]{:S(2)}, u32[]{:S(2)}) collective-permute-start(f32[16,384]{1,0:T(8,128)S(1)} %get-tuple-element.37.own_ref), channel_id=1, source_target_pairs={{0,24},{8,16},{16,8},{24,0},{1,25},{9,17},{17,9},{25,1},{2,26},{10... | collective-permute-start | bytes 73736 | tf_op jit(solution)/shard_map/ppermute | solution.py:376
  12.7 4.7 %collective-permute-start.3 = (f32[16,384]{1,0:T(8,128)S(1)}, f32[16,384]{1,0:T(8,128)S(1)}, u32[]{:S(2)}, u32[]{:S(2)}) collective-permute-start(f32[16,384]{1,0:T(8,128)S(1)} %get-tuple-element.37.own_ref), channel_id=1, source_target_pairs={{0,16},{8,24},{16,0},{24,8},{1,17},{9,25},{17,1},{25,9},{2,18},{10... | collective-permute-start | bytes 73736 | tf_op jit(solution)/shard_map/ppermute | solution.py:376
  12.7 4.7 %collective-permute-start.2 = (f32[16,384]{1,0:T(8,128)S(1)}, f32[16,384]{1,0:T(8,128)S(1)}, u32[]{:S(2)}, u32[]{:S(2)}) collective-permute-start(f32[16,384]{1,0:T(8,128)S(1)} %get-tuple-element.37.own_ref), channel_id=1, source_target_pairs={{0,8},{8,0},{16,24},{24,16},{1,9},{9,1},{17,25},{25,17},{2,10},{10... | collective-permute-start | bytes 73736 | tf_op jit(solution)/shard_map/ppermute | solution.py:376
  18.2 5.6 %collective-permute-start.7 = (f32[16,256]{1,0:T(8,128)S(1)}, f32[16,256]{1,0:T(8,128)S(1)}, u32[]{:S(2)}, u32[]{:S(2)}) collective-permute-start(f32[16,256]{1,0:T(8,128)S(1)} %get-tuple-element.42.own_ref), channel_id=1, source_target_pairs={{0,24},{8,16},{16,8},{24,0},{1,25},{9,17},{17,9},{25,1},{2,26},{10... | collective-permute-start | bytes 49160 | tf_op jit(solution)/shard_map/ppermute | solution.py:376
  19.7 4.7 %collective-permute-start.6 = (f32[16,256]{1,0:T(8,128)S(1)}, f32[16,256]{1,0:T(8,128)S(1)}, u32[]{:S(2)}, u32[]{:S(2)}) collective-permute-start(f32[16,256]{1,0:T(8,128)S(1)} %get-tuple-element.42.own_ref), channel_id=1, source_target_pairs={{0,16},{8,24},{16,0},{24,8},{1,17},{9,25},{17,1},{25,9},{2,18},{10... | collective-permute-start | bytes 49160 | tf_op jit(solution)/shard_map/ppermute | solution.py:376
  20.3 4.2 %collective-permute-start.5 = (f32[16,256]{1,0:T(8,128)S(1)}, f32[16,256]{1,0:T(8,128)S(1)}, u32[]{:S(2)}, u32[]{:S(2)}) collective-permute-start(f32[16,256]{1,0:T(8,128)S(1)} %get-tuple-element.42.own_ref), channel_id=1, source_target_pairs={{0,8},{8,0},{16,24},{24,16},{1,9},{9,1},{17,25},{25,17},{2,10},{10... | collective-permute-start | bytes 49160 | tf_op jit(solution)/shard_map/ppermute | solution.py:376
  24.5 1.2 %collective-permute-start.8 = (f32[8,128]{1,0:T(8,128)S(1)}, f32[8,128]{1,0:T(8,128)S(1)}, u32[]{:S(2)}, u32[]{:S(2)}) collective-permute-start(f32[8,128]{1,0:T(8,128)S(1)} %get-tuple-element.44), channel_id=1, source_target_pairs={{0,1},{1,0},{2,3},{3,2},{4,5},{5,4},{6,7},{7,6},{8,9},{9,8},{10,11... | collective-permute-start | bytes 12296 | tf_op jit(solution)/shard_map/ppermute | solution.py:380
  25.8 3.9 %collective-permute-start.11 = (f32[8,128]{1,0:T(8,128)S(1)}, f32[8,128]{1,0:T(8,128)S(1)}, u32[]{:S(2)}, u32[]{:S(2)}) collective-permute-start(f32[8,128]{1,0:T(8,128)S(1)} %add.3.own_ref), channel_id=1, source_target_pairs={{0,7},{1,6},{2,5},{3,4},{4,3},{5,2},{6,1},{7,0},{8,15},{9,14},{10,... | collective-permute-start | bytes 12296 | tf_op jit(solution)/shard_map/ppermute | solution.py:380
  27.4 3.0 %collective-permute-start.10 = (f32[8,128]{1,0:T(8,128)S(1)}, f32[8,128]{1,0:T(8,128)S(1)}, u32[]{:S(2)}, u32[]{:S(2)}) collective-permute-start(f32[8,128]{1,0:T(8,128)S(1)} %add.3.own_ref), channel_id=1, source_target_pairs={{0,5},{1,4},{2,7},{3,6},{4,1},{5,0},{6,3},{7,2},{8,13},{9,12},{10,... | collective-permute-start | bytes 12296 | tf_op jit(solution)/shard_map/ppermute | solution.py:380
  27.8 3.0 %collective-permute-start.9 = (f32[8,128]{1,0:T(8,128)S(1)}, f32[8,128]{1,0:T(8,128)S(1)}, u32[]{:S(2)}, u32[]{:S(2)}) collective-permute-start(f32[8,128]{1,0:T(8,128)S(1)} %add.3.own_ref), channel_id=1, source_target_pairs={{0,3},{1,2},{2,1},{3,0},{4,7},{5,6},{6,5},{7,4},{8,11},{9,10},{10,... | collective-permute-start | bytes 12296 | tf_op jit(solution)/shard_map/ppermute | solution.py:380

commit v7 on v6

--- a/solution.py
+++ b/solution.py
@@ -190,16 +190,10 @@
 
 
 def main_kernel(
-    diffusivity_hbm, map_ref, members_ref, innovations_ref, precision_ref, counts_hbm,
+    diffusivity_ref, map_ref, members_ref, innovations_ref, precision_ref, counts_ref,
     taps_ref, square_ref, adjoint_ref, blocks_ref, shifted_ref, source_ref, weight_ref, out_ref,
-    split_ref, y_ref, diffusivity_ref, counts_ref, sems,
-):
-    copies = [
-        pltpu.make_async_copy(diffusivity_hbm, diffusivity_ref, sems.at[0]),
-        pltpu.make_async_copy(counts_hbm, counts_ref, sems.at[1]),
-    ]
-    for copy in copies:
-        copy.start()
+    split_ref, y_ref,
+):
     levels = members_ref.shape[1]
     matrix = map_ref[...]
     dims = (((1,), (1,)), ((), ()))
@@ -221,8 +215,6 @@
         value = members_ref[m].astype(F32)
         for i, s in enumerate(SHIFTS):
             shifted_ref[i, m] = shifted_by(value, s).astype(shifted_ref.dtype)
-    for copy in copies:
-        copy.wait()
     coef = level_column(diffusivity_ref[...])
     keep = 1.0 - 2.0 * coef
     taps_ref[0] = keep * keep + 2.0 * coef * coef
@@ -431,8 +423,7 @@
             level, level, level,
         ],
         (diffusivity.reshape(1, levels), vertical_map, perturbations, innovations, precision_field, counts),
-        [split, scratch[0], pltpu.VMEM((1, levels), F32), pltpu.VMEM((1, size), jnp.int32), pltpu.SemaphoreType.DMA((2,))],
-        {0: elsewhere, 5: elsewhere}, work,
+        [split, scratch[0]], flops=work,
     )
     edge_members, edge_source, edge_weight, part = call(
         functools.partial(edge_kernel, count), "first_edges",

time: 31.9 us -> 31.8 us (level)
  no operation moved by 1% of the time
where the time goes in v7:
time: 31.8 us; the launch traced here: 31.6 us
  starting transfers between devices  15.9 us (50%)
  waiting for transfers between devices  7.64 us (24%)
  Pallas kernels  6.64 us (21%)
  between operations  0.77 us (2%)
  local copies, waits for them, and re-layouts  0.7 us (2%)
    ppermute x6, starting transfers between devices, from_partners(): lax.ppermute(value, axis, [(i, i ^ step) for i in range(size)])  9.37 us
    pallas_call x8, Pallas kernels, call(): pl.pallas_call(kernel, name=name, out_shape=list(outs), in_specs=[specs.g...  6.64 us
    ppermute x6, waiting for transfers between devices, from_partners(): lax.ppermute(value, axis, [(i, i ^ step) for i in range(size)])  4.4 us
    ppermute x4, waiting for transfers between devices, partner(): lax.ppermute(value, axis, [(i, i ^ step) for i in range(lax.axis_size(axi...  3.24 us
    ppermute x4, starting transfers between devices, partner(): lax.ppermute(value, axis, [(i, i ^ step) for i in range(lax.axis_size(axi...  3.05 us
    ppermute x1, starting transfers between devices, local(): after = lax.ppermute(high_message, 'domain', down)  2.96 us
    unnamed x16, local copies, waits for them, and re-layouts  0.7 us
  transfers between devices with their start and end apart: 12, of which 9 were waited for; matrix products, arithmetic and copies ran while one was open for 0% of the time, Pallas kernels for 8%

profile of v7, /device:TPU:0, one launch (start us, length us, event | category | flops | bytes accessed | tf_op | source)
XLA Modules:
  0.0 31.6 jit_solution(3966308373279993247)
XLA Ops:
  0.6 0.0 copy-start
  0.6 0.0 copy-start.1
  0.7 0.0 copy-start.2
  0.7 0.0 copy-start.5
  0.7 1.8 %pack_edges.1 = (f32[7,16,128]{2,1,0:T(8,128)}, f32[7,16,128]{2,1,0:T(8,128)}, f32[2,16,128]{2,1,0:T(8,128)}, f32[2,16,128]{2,1,0:T(8,128)}) custom-call(bf16[25,16,256]{2,1,0:T(8,128)(2,1)} %members_hbm.1, f32[16,256]{1,0:T(8,128)} %innovations_hbm.1, f32[16,256]{1,0:T(8,128)} %precision_hbm.1, s32[1,256]{1,0:T(1,128)} %bitcast.2), custom_call_target="tpu_custom_call" | custom-call | flops 286720 | bytes 386048 | tf_op jit(solution)/shard_map/pack_edges/pallas_call | solution.py:350
  2.5 0.5 %collective-permute-start = (f32[2,16,128]{2,1,0:T(8,128)}, f32[2,16,128]{2,1,0:T(8,128)S(1)}, u32[]{:S(2)}, u32[]{:S(2)}) collective-permute-start(f32[2,16,128]{2,1,0:T(8,128)} %get-tuple-element.29), channel_id=1, source_target_pairs={{0,1},{1,2},{2,3},{3,4},{4,5},{5,6},{6,7},{7,0},{8,9},{9,10},{10,1... | collective-permute-start | bytes 49160 | tf_op jit(solution)/shard_map/ppermute | solution.py:414
  3.0 0.0 copy-start.7
  3.0 3.0 %collective-permute-start.1 = (f32[2,16,128]{2,1,0:T(8,128)}, f32[2,16,128]{2,1,0:T(8,128)S(1)}, u32[]{:S(2)}, u32[]{:S(2)}) collective-permute-start(f32[2,16,128]{2,1,0:T(8,128)} %get-tuple-element.30), channel_id=1, source_target_pairs={{1,0},{2,1},{3,2},{4,3},{5,4},{6,5},{7,6},{0,7},{9,8},{10,9},{11,1... | collective-permute-start | bytes 49160 | tf_op jit(solution)/shard_map/ppermute | solution.py:415
  6.0 0.0 copy-done
  6.0 0.0 copy-done.1
  6.0 0.0 copy-done.2
  6.0 0.0 copy-done.5
  6.0 0.0 copy-done.7
  6.0 0.0 copy-start.6
  6.0 0.7 %copy-done.6 = s32[256]{0:T(256)S(1)} copy-done((s32[256]{0:T(256)S(1)}, s32[256]{0:T(256)}, u32[]{:S(2)}) %copy-start.6) | copy-done | bytes 1048
  6.7 0.0 copy-start.3
  6.7 0.0 copy-start.4
  6.7 1.0 %first_inner.1 = (f32[3,16,128]{2,1,0:T(8,128)S(1)}, f32[16,16,128]{2,1,0:T(8,128)S(1)}, f32[16,16,128]{2,1,0:T(8,128)S(1)}, bf16[80,240]{1,0:T(8,128)(2,1)S(1)}...) custom-call(f32[1,16]{1,0:T(1,128)S(1)} %bitcast.4, ...), custom_call_target="tpu_custom_call" | custom-call | flops 5120000 | bytes 1637952 | tf_op jit(solution)/shard_map/first_inner/pallas_call | solution.py:350
  7.6 0.0 collective-permute-done.before_ref
  7.7 0.0 collective-permute-done.1.after_ref
  7.7 0.0 copy-done.3
  7.7 0.0 copy-done.4
  7.7 0.5 %first_edges.1 = (f32[7,16,128]{2,1,0:T(8,128)S(1)}, f32[16,128]{1,0:T(8,128)S(1)}, f32[16,128]{1,0:T(8,128)S(1)}, f32[16,384]{1,0:T(8,128)S(1)}) custom-call(f32[7,16,128]{2,1,0:T(8,128)S(1)} %copy-done.3, f32[7,16,128]{2,1,0:T(8,128)S(1)} %copy-done.4, f32[2,16,128]{2,1,0:T(8,128)S(1)} %collective-permute-done.before_ref, ...), custom_call_target="tpu_custom_call" | custom-call | flops 716800 | bytes 417792 | tf_op jit(solution)/shard_map/first_edges/pallas_call | solution.py:350
  8.2 4.3 %collective-permute-start.4 = (f32[16,384]{1,0:T(8,128)S(1)}, f32[16,384]{1,0:T(8,128)S(1)}, u32[]{:S(2)}, u32[]{:S(2)}) collective-permute-start(f32[16,384]{1,0:T(8,128)S(1)} %get-tuple-element.37.own_ref), channel_id=1, source_target_pairs={{0,24},{8,16},{16,8},{24,0},{1,25},{9,17},{17,9},{25,1},{2,26},{10... | collective-permute-start | bytes 73736 | tf_op jit(solution)/shard_map/ppermute | solution.py:368
  12.5 0.0 collective-permute-start.3
  12.5 0.6 %collective-permute-start.2 = (f32[16,384]{1,0:T(8,128)S(1)}, f32[16,384]{1,0:T(8,128)S(1)}, u32[]{:S(2)}, u32[]{:S(2)}) collective-permute-start(f32[16,384]{1,0:T(8,128)S(1)} %get-tuple-element.37.own_ref), channel_id=1, source_target_pairs={{0,8},{8,0},{16,24},{24,16},{1,9},{9,1},{17,25},{25,17},{2,10},{10... | collective-permute-start | bytes 73736 | tf_op jit(solution)/shard_map/ppermute | solution.py:368
  13.2 0.8 %start_vector.1._.start_ref = f32[25,16,256]{2,1,0:T(8,128)S(1)} custom-call(bf16[5,25,16,256]{3,2,1,0:T(8,128)(2,1)S(1)} %get-tuple-element.26.shifted_ref, f32[7,16,128]{2,1,0:T(8,128)S(1)} %get-tuple-element.34.edge_members_ref, f32[16,256]{1,0:T(8,128)S(1)} %get-tuple-element.24.field_ref.source_ref, f32[16,128]{1,0:T(8,128)S(1)} %get-tuple-element.38.edge_field_ref, ...), custom_call_target="tpu_custom_call" | custom-call | flops 5120000 | bytes 1671168 | tf_op jit(solution)/shard_map/start_vector/pallas_call | solution.py:350
  14.0 0.6 %collective-permute-done.4.c_ref = f32[16,384]{1,0:T(8,128)S(1)} collective-permute-done((f32[16,384]{1,0:T(8,128)S(1)}, f32[16,384]{1,0:T(8,128)S(1)}, u32[]{:S(2)}, u32[]{:S(2)}) %collective-permute-start.4) | collective-permute-done | bytes 24608 | tf_op jit(solution)/shard_map/ppermute | solution.py:368
  14.5 2.7 %collective-permute-done.3.b_ref = f32[16,384]{1,0:T(8,128)S(1)} collective-permute-done((f32[16,384]{1,0:T(8,128)S(1)}, f32[16,384]{1,0:T(8,128)S(1)}, u32[]{:S(2)}, u32[]{:S(2)}) %collective-permute-start.3) | collective-permute-done | bytes 24608 | tf_op jit(solution)/shard_map/ppermute | solution.py:368
  17.3 0.0 collective-permute-done.2.a_ref
  17.3 0.8 %second_apply.1 = (f32[16,256]{1,0:T(8,128)S(1)}, f32[16,256]{1,0:T(8,128)S(1)}, f32[16,128]{1,0:T(8,128)S(1)}, f32[16,256]{1,0:T(8,128)S(1)}) custom-call(bf16[5,25,16,256]{3,2,1,0:T(8,128)(2,1)S(1)} %get-tuple-element.26.shifted_ref, f32[7,16,128]{2,1,0:T(8,128)S(1)} %get-tuple-element.34.edge_members_ref, f32[16,256]{1,0:T(8,128)S(1)} %get-tuple-element.25.weight_ref, ...), custom_call_target="tpu_custom_call" | custom-call | flops 5836800 | bytes 1865216 | tf_op jit(solution)/shard_map/second_apply/pallas_call | solution.py:350
  18.1 1.5 %collective-permute-start.7 = (f32[16,256]{1,0:T(8,128)S(1)}, f32[16,256]{1,0:T(8,128)S(1)}, u32[]{:S(2)}, u32[]{:S(2)}) collective-permute-start(f32[16,256]{1,0:T(8,128)S(1)} %get-tuple-element.42.own_ref), channel_id=1, source_target_pairs={{0,24},{8,16},{16,8},{24,0},{1,25},{9,17},{17,9},{25,1},{2,26},{10... | collective-permute-start | bytes 49160 | tf_op jit(solution)/shard_map/ppermute | solution.py:368
  19.6 0.6 %collective-permute-start.6 = (f32[16,256]{1,0:T(8,128)S(1)}, f32[16,256]{1,0:T(8,128)S(1)}, u32[]{:S(2)}, u32[]{:S(2)}) collective-permute-start(f32[16,256]{1,0:T(8,128)S(1)} %get-tuple-element.42.own_ref), channel_id=1, source_target_pairs={{0,16},{8,24},{16,0},{24,8},{1,17},{9,25},{17,1},{25,9},{2,18},{10... | collective-permute-start | bytes 49160 | tf_op jit(solution)/shard_map/ppermute | solution.py:368
  20.2 2.3 %collective-permute-start.5 = (f32[16,256]{1,0:T(8,128)S(1)}, f32[16,256]{1,0:T(8,128)S(1)}, u32[]{:S(2)}, u32[]{:S(2)}) collective-permute-start(f32[16,256]{1,0:T(8,128)S(1)} %get-tuple-element.42.own_ref), channel_id=1, source_target_pairs={{0,8},{8,0},{16,24},{24,16},{1,9},{9,1},{17,25},{25,17},{2,10},{10... | collective-permute-start | bytes 49160 | tf_op jit(solution)/shard_map/ppermute | solution.py:368
  22.5 0.8 %image_vector.1._.image_ref = f32[25,16,256]{2,1,0:T(8,128)S(1)} custom-call(bf16[5,25,16,256]{3,2,1,0:T(8,128)(2,1)S(1)} %get-tuple-element.26.shifted_ref, f32[7,16,128]{2,1,0:T(8,128)S(1)} %get-tuple-element.34.edge_members_ref, f32[16,256]{1,0:T(8,128)S(1)} %get-tuple-element.41.field_ref.weighted_ref, f32[16,128]{1,0:T(8,128)S(1)} %get-tuple-element.43.edge_field_ref, ...), custom_call_target="tpu_custom_call" | custom-call | flops 5120000 | bytes 1671168 | tf_op jit(solution)/shard_map/image_vector/pallas_call | solution.py:350
  23.3 0.4 %collective-permute-done.7.c_ref = f32[16,256]{1,0:T(8,128)S(1)} collective-permute-done((f32[16,256]{1,0:T(8,128)S(1)}, f32[16,256]{1,0:T(8,128)S(1)}, u32[]{:S(2)}, u32[]{:S(2)}) %collective-permute-start.7) | collective-permute-done | bytes 16416 | tf_op jit(solution)/shard_map/ppermute | solution.py:368
  23.6 0.6 %collective-permute-done.6.b_ref = f32[16,256]{1,0:T(8,128)S(1)} collective-permute-done((f32[16,256]{1,0:T(8,128)S(1)}, f32[16,256]{1,0:T(8,128)S(1)}, u32[]{:S(2)}, u32[]{:S(2)}) %collective-permute-start.6) | collective-permute-done | bytes 16416 | tf_op jit(solution)/shard_map/ppermute | solution.py:368
  24.2 0.2 collective-permute-done.5.a_ref
  24.4 0.1 collective-permute-start.8
  24.5 1.2 %collective-permute-done.8 = f32[8,128]{1,0:T(8,128)S(1)} collective-permute-done((f32[8,128]{1,0:T(8,128)S(1)}, f32[8,128]{1,0:T(8,128)S(1)}, u32[]{:S(2)}, u32[]{:S(2)}) %collective-permute-start.8) | collective-permute-done | bytes 4128 | tf_op jit(solution)/shard_map/ppermute | solution.py:372
  25.6 1.5 %collective-permute-start.11 = (f32[8,128]{1,0:T(8,128)S(1)}, f32[8,128]{1,0:T(8,128)S(1)}, u32[]{:S(2)}, u32[]{:S(2)}) collective-permute-start(f32[8,128]{1,0:T(8,128)S(1)} %add.3.own_ref), channel_id=1, source_target_pairs={{0,7},{1,6},{2,5},{3,4},{4,3},{5,2},{6,1},{7,0},{8,15},{9,14},{10,... | collective-permute-start | bytes 12296 | tf_op jit(solution)/shard_map/ppermute | solution.py:372
  27.1 0.6 %collective-permute-start.10 = (f32[8,128]{1,0:T(8,128)S(1)}, f32[8,128]{1,0:T(8,128)S(1)}, u32[]{:S(2)}, u32[]{:S(2)}) collective-permute-start(f32[8,128]{1,0:T(8,128)S(1)} %add.3.own_ref), channel_id=1, source_target_pairs={{0,5},{1,4},{2,7},{3,6},{4,1},{5,0},{6,3},{7,2},{8,13},{9,12},{10,... | collective-permute-start | bytes 12296 | tf_op jit(solution)/shard_map/ppermute | solution.py:372
  27.7 0.9 %collective-permute-start.9 = (f32[8,128]{1,0:T(8,128)S(1)}, f32[8,128]{1,0:T(8,128)S(1)}, u32[]{:S(2)}, u32[]{:S(2)}) collective-permute-start(f32[8,128]{1,0:T(8,128)S(1)} %add.3.own_ref), channel_id=1, source_target_pairs={{0,3},{1,2},{2,1},{3,0},{4,7},{5,6},{6,5},{7,4},{8,11},{9,10},{10,... | collective-permute-start | bytes 12296 | tf_op jit(solution)/shard_map/ppermute | solution.py:372
  28.6 0.9 %collective-permute-done.11.c_ref = f32[8,128]{1,0:T(8,128)S(1)} collective-permute-done((f32[8,128]{1,0:T(8,128)S(1)}, f32[8,128]{1,0:T(8,128)S(1)}, u32[]{:S(2)}, u32[]{:S(2)}) %collective-permute-start.11) | collective-permute-done | bytes 4128 | tf_op jit(solution)/shard_map/ppermute | solution.py:372
  29.6 0.6 %collective-permute-done.10.b_ref = f32[8,128]{1,0:T(8,128)S(1)} collective-permute-done((f32[8,128]{1,0:T(8,128)S(1)}, f32[8,128]{1,0:T(8,128)S(1)}, u32[]{:S(2)}, u32[]{:S(2)}) %collective-permute-start.10) | collective-permute-done | bytes 4128 | tf_op jit(solution)/shard_map/ppermute | solution.py:372
  30.2 0.6 %collective-permute-done.9.a_ref = f32[8,128]{1,0:T(8,128)S(1)} collective-permute-done((f32[8,128]{1,0:T(8,128)S(1)}, f32[8,128]{1,0:T(8,128)S(1)}, u32[]{:S(2)}, u32[]{:S(2)}) %collective-permute-start.9) | collective-permute-done | bytes 4128 | tf_op jit(solution)/shard_map/ppermute | solution.py:372
  30.7 0.9 %combine.1 = (f32[25,16,256]{2,1,0:T(8,128)}, f32[16,256]{1,0:T(8,128)}) custom-call(f32[8,128]{1,0:T(8,128)S(1)} %add.3.own_ref, f32[8,128]{1,0:T(8,128)S(1)} %collective-permute-done.9.a_ref, f32[8,128]{1,0:T(8,128)S(1)} %collective-permute-done.10.b_ref, f32[8,128]{1,0:T(8,128)S(1)} %collective-permute-done.11.c_ref, ...), custom_call_target="tpu_custom_call" | custom-call | bytes 1294336 | tf_op jit(solution)/shard_map/combine/pallas_call | solution.py:350
  (2 shorter events, 0.0 us)
Async XLA Ops:
  0.6 5.3 %copy-start = (bf16[25,16,256]{2,1,0:T(8,128)(2,1)S(1)}, bf16[25,16,256]{2,1,0:T(8,128)(2,1)}, u32[]{:S(2)}) copy-start(bf16[25,16,256]{2,1,0:T(8,128)(2,1)} %members_hbm.1) | copy-start | bytes 614404
  0.6 5.3 %copy-start.1 = (f32[16,256]{1,0:T(8,128)S(1)}, f32[16,256]{1,0:T(8,128)}, u32[]{:S(2)}) copy-start(f32[16,256]{1,0:T(8,128)} %innovations_hbm.1) | copy-start | bytes 49156
  0.7 5.3 %copy-start.2 = (f32[16,256]{1,0:T(8,128)S(1)}, f32[16,256]{1,0:T(8,128)}, u32[]{:S(2)}) copy-start(f32[16,256]{1,0:T(8,128)} %precision_hbm.1) | copy-start | bytes 49156
  0.7 5.3 %copy-start.5 = (f32[16,16]{1,0:T(8,128)S(1)}, f32[16,16]{1,0:T(8,128)}, u32[]{:S(2)}) copy-start(f32[16,16]{1,0:T(8,128)} %map_ref.1) | copy-start | bytes 3076
  2.5 5.1 %collective-permute-start = (f32[2,16,128]{2,1,0:T(8,128)}, f32[2,16,128]{2,1,0:T(8,128)S(1)}, u32[]{:S(2)}, u32[]{:S(2)}) collective-permute-start(f32[2,16,128]{2,1,0:T(8,128)} %get-tuple-element.29), channel_id=1, source_target_pairs={{0,1},{1,2},{2,3},{3,4},{4,5},{5,6},{6,7},{7,0},{8,9},{9,10},{10,1... | collective-permute-start | bytes 49160 | tf_op jit(solution)/shard_map/ppermute | solution.py:414
  3.0 3.0 %copy-start.7 = (f32[16]{0:T(128)S(1)}, f32[16]{0:T(128)}, u32[]{:S(2)}) copy-start(f32[16]{0:T(128)} %param.11) | copy-start | bytes 196
  3.0 4.6 %collective-permute-start.1 = (f32[2,16,128]{2,1,0:T(8,128)}, f32[2,16,128]{2,1,0:T(8,128)S(1)}, u32[]{:S(2)}, u32[]{:S(2)}) collective-permute-start(f32[2,16,128]{2,1,0:T(8,128)} %get-tuple-element.30), channel_id=1, source_target_pairs={{1,0},{2,1},{3,2},{4,3},{5,4},{6,5},{7,6},{0,7},{9,8},{10,9},{11,1... | collective-permute-start | bytes 49160 | tf_op jit(solution)/shard_map/ppermute | solution.py:415
  6.0 0.7 %copy-start.6 = (s32[256]{0:T(256)S(1)}, s32[256]{0:T(256)}, u32[]{:S(2)}) copy-start(s32[256]{0:T(256)} %param.9) | copy-start | bytes 3076
  6.7 1.0 %copy-start.3 = (f32[7,16,128]{2,1,0:T(8,128)S(1)}, f32[7,16,128]{2,1,0:T(8,128)}, u32[]{:S(2)}) copy-start(f32[7,16,128]{2,1,0:T(8,128)} %get-tuple-element.27.low_ref) | copy-start | bytes 172036
  6.7 1.0 %copy-start.4 = (f32[7,16,128]{2,1,0:T(8,128)S(1)}, f32[7,16,128]{2,1,0:T(8,128)}, u32[]{:S(2)}) copy-start(f32[7,16,128]{2,1,0:T(8,128)} %get-tuple-element.28.high_ref) | copy-start | bytes 172036
  8.2 6.3 %collective-permute-start.4 = (f32[16,384]{1,0:T(8,128)S(1)}, f32[16,384]{1,0:T(8,128)S(1)}, u32[]{:S(2)}, u32[]{:S(2)}) collective-permute-start(f32[16,384]{1,0:T(8,128)S(1)} %get-tuple-element.37.own_ref), channel_id=1, source_target_pairs={{0,24},{8,16},{16,8},{24,0},{1,25},{9,17},{17,9},{25,1},{2,26},{10... | collective-permute-start | bytes 73736 | tf_op jit(solution)/shard_map/ppermute | solution.py:368
  12.5 4.7 %collective-permute-start.3 = (f32[16,384]{1,0:T(8,128)S(1)}, f32[16,384]{1,0:T(8,128)S(1)}, u32[]{:S(2)}, u32[]{:S(2)}) collective-permute-start(f32[16,384]{1,0:T(8,128)S(1)} %get-tuple-element.37.own_ref), channel_id=1, source_target_pairs={{0,16},{8,24},{16,0},{24,8},{1,17},{9,25},{17,1},{25,9},{2,18},{10... | collective-permute-start | bytes 73736 | tf_op jit(solution)/shard_map/ppermute | solution.py:368
  12.5 4.7 %collective-permute-start.2 = (f32[16,384]{1,0:T(8,128)S(1)}, f32[16,384]{1,0:T(8,128)S(1)}, u32[]{:S(2)}, u32[]{:S(2)}) collective-permute-start(f32[16,384]{1,0:T(8,128)S(1)} %get-tuple-element.37.own_ref), channel_id=1, source_target_pairs={{0,8},{8,0},{16,24},{24,16},{1,9},{9,1},{17,25},{25,17},{2,10},{10... | collective-permute-start | bytes 73736 | tf_op jit(solution)/shard_map/ppermute | solution.py:368
  18.1 5.6 %collective-permute-start.7 = (f32[16,256]{1,0:T(8,128)S(1)}, f32[16,256]{1,0:T(8,128)S(1)}, u32[]{:S(2)}, u32[]{:S(2)}) collective-permute-start(f32[16,256]{1,0:T(8,128)S(1)} %get-tuple-element.42.own_ref), channel_id=1, source_target_pairs={{0,24},{8,16},{16,8},{24,0},{1,25},{9,17},{17,9},{25,1},{2,26},{10... | collective-permute-start | bytes 49160 | tf_op jit(solution)/shard_map/ppermute | solution.py:368
  19.6 4.7 %collective-permute-start.6 = (f32[16,256]{1,0:T(8,128)S(1)}, f32[16,256]{1,0:T(8,128)S(1)}, u32[]{:S(2)}, u32[]{:S(2)}) collective-permute-start(f32[16,256]{1,0:T(8,128)S(1)} %get-tuple-element.42.own_ref), channel_id=1, source_target_pairs={{0,16},{8,24},{16,0},{24,8},{1,17},{9,25},{17,1},{25,9},{2,18},{10... | collective-permute-start | bytes 49160 | tf_op jit(solution)/shard_map/ppermute | solution.py:368
  20.2 4.2 %collective-permute-start.5 = (f32[16,256]{1,0:T(8,128)S(1)}, f32[16,256]{1,0:T(8,128)S(1)}, u32[]{:S(2)}, u32[]{:S(2)}) collective-permute-start(f32[16,256]{1,0:T(8,128)S(1)} %get-tuple-element.42.own_ref), channel_id=1, source_target_pairs={{0,8},{8,0},{16,24},{24,16},{1,9},{9,1},{17,25},{25,17},{2,10},{10... | collective-permute-start | bytes 49160 | tf_op jit(solution)/shard_map/ppermute | solution.py:368
  24.4 1.2 %collective-permute-start.8 = (f32[8,128]{1,0:T(8,128)S(1)}, f32[8,128]{1,0:T(8,128)S(1)}, u32[]{:S(2)}, u32[]{:S(2)}) collective-permute-start(f32[8,128]{1,0:T(8,128)S(1)} %get-tuple-element.44), channel_id=1, source_target_pairs={{0,1},{1,0},{2,3},{3,2},{4,5},{5,4},{6,7},{7,6},{8,9},{9,8},{10,11... | collective-permute-start | bytes 12296 | tf_op jit(solution)/shard_map/ppermute | solution.py:372
  25.6 3.9 %collective-permute-start.11 = (f32[8,128]{1,0:T(8,128)S(1)}, f32[8,128]{1,0:T(8,128)S(1)}, u32[]{:S(2)}, u32[]{:S(2)}) collective-permute-start(f32[8,128]{1,0:T(8,128)S(1)} %add.3.own_ref), channel_id=1, source_target_pairs={{0,7},{1,6},{2,5},{3,4},{4,3},{5,2},{6,1},{7,0},{8,15},{9,14},{10,... | collective-permute-start | bytes 12296 | tf_op jit(solution)/shard_map/ppermute | solution.py:372
  27.1 3.0 %collective-permute-start.10 = (f32[8,128]{1,0:T(8,128)S(1)}, f32[8,128]{1,0:T(8,128)S(1)}, u32[]{:S(2)}, u32[]{:S(2)}) collective-permute-start(f32[8,128]{1,0:T(8,128)S(1)} %add.3.own_ref), channel_id=1, source_target_pairs={{0,5},{1,4},{2,7},{3,6},{4,1},{5,0},{6,3},{7,2},{8,13},{9,12},{10,... | collective-permute-start | bytes 12296 | tf_op jit(solution)/shard_map/ppermute | solution.py:372
  27.7 3.0 %collective-permute-start.9 = (f32[8,128]{1,0:T(8,128)S(1)}, f32[8,128]{1,0:T(8,128)S(1)}, u32[]{:S(2)}, u32[]{:S(2)}) collective-permute-start(f32[8,128]{1,0:T(8,128)S(1)} %add.3.own_ref), channel_id=1, source_target_pairs={{0,3},{1,2},{2,1},{3,0},{4,7},{5,6},{6,5},{7,4},{8,11},{9,10},{10,... | collective-permute-start | bytes 12296 | tf_op jit(solution)/shard_map/ppermute | solution.py:372

commit v8 on v7

--- a/solution.py
+++ b/solution.py
@@ -166,7 +166,7 @@
     at = lane % SLOT
     low_message, high_message = [None] * low_message_ref.shape[0], [None] * low_message_ref.shape[0]
     for tile in range(low_ref.shape[0]):
-        low = high = None
+        low = None
         for slot in range(SLOTS):
             m = tile * SLOTS + slot
             if m < count:
@@ -177,13 +177,12 @@
                 continue
             ends = ends_of(first, last, lane)
             low = added(low, lane_roll(ends, slot * SLOT + HALO))
-            high = added(high, lane_roll(ends, slot * SLOT + 3 * HALO))
         low_ref[tile] = low
-        high_ref[tile] = high
+        high_ref[tile] = lane_roll(low, 2 * HALO)
         place, shift = divmod(tile, SLOT // HALO)
         low_message[place] = added(low_message[place], lane_roll(jnp.where(at < HALO, low, 0.0), shift * HALO))
-        high = lane_roll(jnp.where(at >= 3 * HALO, high, 0.0), shift * HALO - 3 * HALO)
-        high_message[place] = added(high_message[place], high)
+        first = jnp.where((at >= HALO) & (at < 2 * HALO), low, 0.0)
+        high_message[place] = added(high_message[place], lane_roll(first, shift * HALO - HALO))
     for place in range(low_message_ref.shape[0]):
         low_message_ref[place] = low_message[place]
         high_message_ref[place] = high_message[place]

time: 31.8 us -> 31.9 us (level)
  no operation moved by 1% of the time
where the time goes in v8:
time: 31.9 us; the launch traced here: 31.7 us
  starting transfers between devices  15.9 us (50%)
  waiting for transfers between devices  7.64 us (24%)
  Pallas kernels  6.68 us (21%)
  between operations  0.77 us (2%)
  local copies, waits for them, and re-layouts  0.7 us (2%)
    ppermute x6, starting transfers between devices, from_partners(): lax.ppermute(value, axis, [(i, i ^ step) for i in range(size)])  9.37 us
    pallas_call x8, Pallas kernels, call(): pl.pallas_call(kernel, name=name, out_shape=list(outs), in_specs=[specs.g...  6.68 us
    ppermute x6, waiting for transfers between devices, from_partners(): lax.ppermute(value, axis, [(i, i ^ step) for i in range(size)])  4.4 us
    ppermute x4, waiting for transfers between devices, partner(): lax.ppermute(value, axis, [(i, i ^ step) for i in range(lax.axis_size(axi...  3.24 us
    ppermute x4, starting transfers between devices, partner(): lax.ppermute(value, axis, [(i, i ^ step) for i in range(lax.axis_size(axi...  3.05 us
    ppermute x1, starting transfers between devices, local(): after = lax.ppermute(high_message, 'domain', down)  2.96 us
    unnamed x16, local copies, waits for them, and re-layouts  0.7 us
  transfers between devices with their start and end apart: 12, of which 9 were waited for; matrix products, arithmetic and copies ran while one was open for 0% of the time, Pallas kernels for 8%

profile of v8, /device:TPU:0, one launch (start us, length us, event | category | flops | bytes accessed | tf_op | source)
XLA Modules:
  0.0 31.7 jit_solution(15391138526863677557)
XLA Ops:
  0.6 0.0 copy-start
  0.6 0.0 copy-start.1
  0.7 0.0 copy-start.2
  0.7 0.0 copy-start.5
  0.7 1.9 %pack_edges.1 = (f32[7,16,128]{2,1,0:T(8,128)}, f32[7,16,128]{2,1,0:T(8,128)}, f32[2,16,128]{2,1,0:T(8,128)}, f32[2,16,128]{2,1,0:T(8,128)}) custom-call(bf16[25,16,256]{2,1,0:T(8,128)(2,1)} %members_hbm.1, f32[16,256]{1,0:T(8,128)} %innovations_hbm.1, f32[16,256]{1,0:T(8,128)} %precision_hbm.1, s32[1,256]{1,0:T(1,128)} %bitcast.2), custom_call_target="tpu_custom_call" | custom-call | flops 286720 | bytes 386048 | tf_op jit(solution)/shard_map/pack_edges/pallas_call | solution.py:349
  2.5 0.5 %collective-permute-start = (f32[2,16,128]{2,1,0:T(8,128)}, f32[2,16,128]{2,1,0:T(8,128)S(1)}, u32[]{:S(2)}, u32[]{:S(2)}) collective-permute-start(f32[2,16,128]{2,1,0:T(8,128)} %get-tuple-element.29), channel_id=1, source_target_pairs={{0,1},{1,2},{2,3},{3,4},{4,5},{5,6},{6,7},{7,0},{8,9},{9,10},{10,1... | collective-permute-start | bytes 49160 | tf_op jit(solution)/shard_map/ppermute | solution.py:413
  3.0 0.0 copy-start.7
  3.1 3.0 %collective-permute-start.1 = (f32[2,16,128]{2,1,0:T(8,128)}, f32[2,16,128]{2,1,0:T(8,128)S(1)}, u32[]{:S(2)}, u32[]{:S(2)}) collective-permute-start(f32[2,16,128]{2,1,0:T(8,128)} %get-tuple-element.30), channel_id=1, source_target_pairs={{1,0},{2,1},{3,2},{4,3},{5,4},{6,5},{7,6},{0,7},{9,8},{10,9},{11,1... | collective-permute-start | bytes 49160 | tf_op jit(solution)/shard_map/ppermute | solution.py:414
  6.0 0.0 copy-done
  6.0 0.0 copy-done.1
  6.0 0.0 copy-done.2
  6.0 0.0 copy-done.5
  6.0 0.0 copy-done.7
  6.0 0.0 copy-start.6
  6.0 0.7 %copy-done.6 = s32[256]{0:T(256)S(1)} copy-done((s32[256]{0:T(256)S(1)}, s32[256]{0:T(256)}, u32[]{:S(2)}) %copy-start.6) | copy-done | bytes 1048
  6.7 0.0 copy-start.3
  6.7 0.0 copy-start.4
  6.7 1.0 %first_inner.1 = (f32[3,16,128]{2,1,0:T(8,128)S(1)}, f32[16,16,128]{2,1,0:T(8,128)S(1)}, f32[16,16,128]{2,1,0:T(8,128)S(1)}, bf16[80,240]{1,0:T(8,128)(2,1)S(1)}...) custom-call(f32[1,16]{1,0:T(1,128)S(1)} %bitcast.4, ...), custom_call_target="tpu_custom_call" | custom-call | flops 5120000 | bytes 1637952 | tf_op jit(solution)/shard_map/first_inner/pallas_call | solution.py:349
  7.7 0.0 collective-permute-done.before_ref
  7.7 0.0 collective-permute-done.1.after_ref
  7.7 0.0 copy-done.3
  7.7 0.0 copy-done.4
  7.7 0.5 %first_edges.1 = (f32[7,16,128]{2,1,0:T(8,128)S(1)}, f32[16,128]{1,0:T(8,128)S(1)}, f32[16,128]{1,0:T(8,128)S(1)}, f32[16,384]{1,0:T(8,128)S(1)}) custom-call(f32[7,16,128]{2,1,0:T(8,128)S(1)} %copy-done.3, f32[7,16,128]{2,1,0:T(8,128)S(1)} %copy-done.4, f32[2,16,128]{2,1,0:T(8,128)S(1)} %collective-permute-done.before_ref, ...), custom_call_target="tpu_custom_call" | custom-call | flops 716800 | bytes 417792 | tf_op jit(solution)/shard_map/first_edges/pallas_call | solution.py:349
  8.3 4.3 %collective-permute-start.4 = (f32[16,384]{1,0:T(8,128)S(1)}, f32[16,384]{1,0:T(8,128)S(1)}, u32[]{:S(2)}, u32[]{:S(2)}) collective-permute-start(f32[16,384]{1,0:T(8,128)S(1)} %get-tuple-element.37.own_ref), channel_id=1, source_target_pairs={{0,24},{8,16},{16,8},{24,0},{1,25},{9,17},{17,9},{25,1},{2,26},{10... | collective-permute-start | bytes 73736 | tf_op jit(solution)/shard_map/ppermute | solution.py:367
  12.6 0.0 collective-permute-start.3
  12.6 0.6 %collective-permute-start.2 = (f32[16,384]{1,0:T(8,128)S(1)}, f32[16,384]{1,0:T(8,128)S(1)}, u32[]{:S(2)}, u32[]{:S(2)}) collective-permute-start(f32[16,384]{1,0:T(8,128)S(1)} %get-tuple-element.37.own_ref), channel_id=1, source_target_pairs={{0,8},{8,0},{16,24},{24,16},{1,9},{9,1},{17,25},{25,17},{2,10},{10... | collective-permute-start | bytes 73736 | tf_op jit(solution)/shard_map/ppermute | solution.py:367
  13.2 0.8 %start_vector.1._.start_ref = f32[25,16,256]{2,1,0:T(8,128)S(1)} custom-call(bf16[5,25,16,256]{3,2,1,0:T(8,128)(2,1)S(1)} %get-tuple-element.26.shifted_ref, f32[7,16,128]{2,1,0:T(8,128)S(1)} %get-tuple-element.34.edge_members_ref, f32[16,256]{1,0:T(8,128)S(1)} %get-tuple-element.24.field_ref.source_ref, f32[16,128]{1,0:T(8,128)S(1)} %get-tuple-element.38.edge_field_ref, ...), custom_call_target="tpu_custom_call" | custom-call | flops 5120000 | bytes 1671168 | tf_op jit(solution)/shard_map/start_vector/pallas_call | solution.py:349
  14.0 0.6 %collective-permute-done.4.c_ref = f32[16,384]{1,0:T(8,128)S(1)} collective-permute-done((f32[16,384]{1,0:T(8,128)S(1)}, f32[16,384]{1,0:T(8,128)S(1)}, u32[]{:S(2)}, u32[]{:S(2)}) %collective-permute-start.4) | collective-permute-done | bytes 24608 | tf_op jit(solution)/shard_map/ppermute | solution.py:367
  14.6 2.7 %collective-permute-done.3.b_ref = f32[16,384]{1,0:T(8,128)S(1)} collective-permute-done((f32[16,384]{1,0:T(8,128)S(1)}, f32[16,384]{1,0:T(8,128)S(1)}, u32[]{:S(2)}, u32[]{:S(2)}) %collective-permute-start.3) | collective-permute-done | bytes 24608 | tf_op jit(solution)/shard_map/ppermute | solution.py:367
  17.3 0.0 collective-permute-done.2.a_ref
  17.3 0.8 %second_apply.1 = (f32[16,256]{1,0:T(8,128)S(1)}, f32[16,256]{1,0:T(8,128)S(1)}, f32[16,128]{1,0:T(8,128)S(1)}, f32[16,256]{1,0:T(8,128)S(1)}) custom-call(bf16[5,25,16,256]{3,2,1,0:T(8,128)(2,1)S(1)} %get-tuple-element.26.shifted_ref, f32[7,16,128]{2,1,0:T(8,128)S(1)} %get-tuple-element.34.edge_members_ref, f32[16,256]{1,0:T(8,128)S(1)} %get-tuple-element.25.weight_ref, ...), custom_call_target="tpu_custom_call" | custom-call | flops 5836800 | bytes 1865216 | tf_op jit(solution)/shard_map/second_apply/pallas_call | solution.py:349
  18.1 1.5 %collective-permute-start.7 = (f32[16,256]{1,0:T(8,128)S(1)}, f32[16,256]{1,0:T(8,128)S(1)}, u32[]{:S(2)}, u32[]{:S(2)}) collective-permute-start(f32[16,256]{1,0:T(8,128)S(1)} %get-tuple-element.42.own_ref), channel_id=1, source_target_pairs={{0,24},{8,16},{16,8},{24,0},{1,25},{9,17},{17,9},{25,1},{2,26},{10... | collective-permute-start | bytes 49160 | tf_op jit(solution)/shard_map/ppermute | solution.py:367
  19.6 0.6 %collective-permute-start.6 = (f32[16,256]{1,0:T(8,128)S(1)}, f32[16,256]{1,0:T(8,128)S(1)}, u32[]{:S(2)}, u32[]{:S(2)}) collective-permute-start(f32[16,256]{1,0:T(8,128)S(1)} %get-tuple-element.42.own_ref), channel_id=1, source_target_pairs={{0,16},{8,24},{16,0},{24,8},{1,17},{9,25},{17,1},{25,9},{2,18},{10... | collective-permute-start | bytes 49160 | tf_op jit(solution)/shard_map/ppermute | solution.py:367
  20.2 2.3 %collective-permute-start.5 = (f32[16,256]{1,0:T(8,128)S(1)}, f32[16,256]{1,0:T(8,128)S(1)}, u32[]{:S(2)}, u32[]{:S(2)}) collective-permute-start(f32[16,256]{1,0:T(8,128)S(1)} %get-tuple-element.42.own_ref), channel_id=1, source_target_pairs={{0,8},{8,0},{16,24},{24,16},{1,9},{9,1},{17,25},{25,17},{2,10},{10... | collective-permute-start | bytes 49160 | tf_op jit(solution)/shard_map/ppermute | solution.py:367
  22.5 0.8 %image_vector.1._.image_ref = f32[25,16,256]{2,1,0:T(8,128)S(1)} custom-call(bf16[5,25,16,256]{3,2,1,0:T(8,128)(2,1)S(1)} %get-tuple-element.26.shifted_ref, f32[7,16,128]{2,1,0:T(8,128)S(1)} %get-tuple-element.34.edge_members_ref, f32[16,256]{1,0:T(8,128)S(1)} %get-tuple-element.41.field_ref.weighted_ref, f32[16,128]{1,0:T(8,128)S(1)} %get-tuple-element.43.edge_field_ref, ...), custom_call_target="tpu_custom_call" | custom-call | flops 5120000 | bytes 1671168 | tf_op jit(solution)/shard_map/image_vector/pallas_call | solution.py:349
  23.3 0.4 %collective-permute-done.7.c_ref = f32[16,256]{1,0:T(8,128)S(1)} collective-permute-done((f32[16,256]{1,0:T(8,128)S(1)}, f32[16,256]{1,0:T(8,128)S(1)}, u32[]{:S(2)}, u32[]{:S(2)}) %collective-permute-start.7) | collective-permute-done | bytes 16416 | tf_op jit(solution)/shard_map/ppermute | solution.py:367
  23.7 0.6 %collective-permute-done.6.b_ref = f32[16,256]{1,0:T(8,128)S(1)} collective-permute-done((f32[16,256]{1,0:T(8,128)S(1)}, f32[16,256]{1,0:T(8,128)S(1)}, u32[]{:S(2)}, u32[]{:S(2)}) %collective-permute-start.6) | collective-permute-done | bytes 16416 | tf_op jit(solution)/shard_map/ppermute | solution.py:367
  24.3 0.2 collective-permute-done.5.a_ref
  24.4 0.1 collective-permute-start.8
  24.5 1.2 %collective-permute-done.8 = f32[8,128]{1,0:T(8,128)S(1)} collective-permute-done((f32[8,128]{1,0:T(8,128)S(1)}, f32[8,128]{1,0:T(8,128)S(1)}, u32[]{:S(2)}, u32[]{:S(2)}) %collective-permute-start.8) | collective-permute-done | bytes 4128 | tf_op jit(solution)/shard_map/ppermute | solution.py:371
  25.7 1.5 %collective-permute-start.11 = (f32[8,128]{1,0:T(8,128)S(1)}, f32[8,128]{1,0:T(8,128)S(1)}, u32[]{:S(2)}, u32[]{:S(2)}) collective-permute-start(f32[8,128]{1,0:T(8,128)S(1)} %add.3.own_ref), channel_id=1, source_target_pairs={{0,7},{1,6},{2,5},{3,4},{4,3},{5,2},{6,1},{7,0},{8,15},{9,14},{10,... | collective-permute-start | bytes 12296 | tf_op jit(solution)/shard_map/ppermute | solution.py:371
  27.2 0.6 %collective-permute-start.10 = (f32[8,128]{1,0:T(8,128)S(1)}, f32[8,128]{1,0:T(8,128)S(1)}, u32[]{:S(2)}, u32[]{:S(2)}) collective-permute-start(f32[8,128]{1,0:T(8,128)S(1)} %add.3.own_ref), channel_id=1, source_target_pairs={{0,5},{1,4},{2,7},{3,6},{4,1},{5,0},{6,3},{7,2},{8,13},{9,12},{10,... | collective-permute-start | bytes 12296 | tf_op jit(solution)/shard_map/ppermute | solution.py:371
  27.7 0.9 %collective-permute-start.9 = (f32[8,128]{1,0:T(8,128)S(1)}, f32[8,128]{1,0:T(8,128)S(1)}, u32[]{:S(2)}, u32[]{:S(2)}) collective-permute-start(f32[8,128]{1,0:T(8,128)S(1)} %add.3.own_ref), channel_id=1, source_target_pairs={{0,3},{1,2},{2,1},{3,0},{4,7},{5,6},{6,5},{7,4},{8,11},{9,10},{10,... | collective-permute-start | bytes 12296 | tf_op jit(solution)/shard_map/ppermute | solution.py:371
  28.7 0.9 %collective-permute-done.11.c_ref = f32[8,128]{1,0:T(8,128)S(1)} collective-permute-done((f32[8,128]{1,0:T(8,128)S(1)}, f32[8,128]{1,0:T(8,128)S(1)}, u32[]{:S(2)}, u32[]{:S(2)}) %collective-permute-start.11) | collective-permute-done | bytes 4128 | tf_op jit(solution)/shard_map/ppermute | solution.py:371
  29.6 0.6 %collective-permute-done.10.b_ref = f32[8,128]{1,0:T(8,128)S(1)} collective-permute-done((f32[8,128]{1,0:T(8,128)S(1)}, f32[8,128]{1,0:T(8,128)S(1)}, u32[]{:S(2)}, u32[]{:S(2)}) %collective-permute-start.10) | collective-permute-done | bytes 4128 | tf_op jit(solution)/shard_map/ppermute | solution.py:371
  30.2 0.6 %collective-permute-done.9.a_ref = f32[8,128]{1,0:T(8,128)S(1)} collective-permute-done((f32[8,128]{1,0:T(8,128)S(1)}, f32[8,128]{1,0:T(8,128)S(1)}, u32[]{:S(2)}, u32[]{:S(2)}) %collective-permute-start.9) | collective-permute-done | bytes 4128 | tf_op jit(solution)/shard_map/ppermute | solution.py:371
  30.8 0.9 %combine.1 = (f32[25,16,256]{2,1,0:T(8,128)}, f32[16,256]{1,0:T(8,128)}) custom-call(f32[8,128]{1,0:T(8,128)S(1)} %add.3.own_ref, f32[8,128]{1,0:T(8,128)S(1)} %collective-permute-done.9.a_ref, f32[8,128]{1,0:T(8,128)S(1)} %collective-permute-done.10.b_ref, f32[8,128]{1,0:T(8,128)S(1)} %collective-permute-done.11.c_ref, ...), custom_call_target="tpu_custom_call" | custom-call | bytes 1294336 | tf_op jit(solution)/shard_map/combine/pallas_call | solution.py:349
  (2 shorter events, 0.0 us)
Async XLA Ops:
  0.6 5.4 %copy-start = (bf16[25,16,256]{2,1,0:T(8,128)(2,1)S(1)}, bf16[25,16,256]{2,1,0:T(8,128)(2,1)}, u32[]{:S(2)}) copy-start(bf16[25,16,256]{2,1,0:T(8,128)(2,1)} %members_hbm.1) | copy-start | bytes 614404
  0.6 5.4 %copy-start.1 = (f32[16,256]{1,0:T(8,128)S(1)}, f32[16,256]{1,0:T(8,128)}, u32[]{:S(2)}) copy-start(f32[16,256]{1,0:T(8,128)} %innovations_hbm.1) | copy-start | bytes 49156
  0.7 5.4 %copy-start.2 = (f32[16,256]{1,0:T(8,128)S(1)}, f32[16,256]{1,0:T(8,128)}, u32[]{:S(2)}) copy-start(f32[16,256]{1,0:T(8,128)} %precision_hbm.1) | copy-start | bytes 49156
  0.7 5.4 %copy-start.5 = (f32[16,16]{1,0:T(8,128)S(1)}, f32[16,16]{1,0:T(8,128)}, u32[]{:S(2)}) copy-start(f32[16,16]{1,0:T(8,128)} %map_ref.1) | copy-start | bytes 3076
  2.5 5.1 %collective-permute-start = (f32[2,16,128]{2,1,0:T(8,128)}, f32[2,16,128]{2,1,0:T(8,128)S(1)}, u32[]{:S(2)}, u32[]{:S(2)}) collective-permute-start(f32[2,16,128]{2,1,0:T(8,128)} %get-tuple-element.29), channel_id=1, source_target_pairs={{0,1},{1,2},{2,3},{3,4},{4,5},{5,6},{6,7},{7,0},{8,9},{9,10},{10,1... | collective-permute-start | bytes 49160 | tf_op jit(solution)/shard_map/ppermute | solution.py:413
  3.0 3.0 %copy-start.7 = (f32[16]{0:T(128)S(1)}, f32[16]{0:T(128)}, u32[]{:S(2)}) copy-start(f32[16]{0:T(128)} %param.11) | copy-start | bytes 196
  3.1 4.6 %collective-permute-start.1 = (f32[2,16,128]{2,1,0:T(8,128)}, f32[2,16,128]{2,1,0:T(8,128)S(1)}, u32[]{:S(2)}, u32[]{:S(2)}) collective-permute-start(f32[2,16,128]{2,1,0:T(8,128)} %get-tuple-element.30), channel_id=1, source_target_pairs={{1,0},{2,1},{3,2},{4,3},{5,4},{6,5},{7,6},{0,7},{9,8},{10,9},{11,1... | collective-permute-start | bytes 49160 | tf_op jit(solution)/shard_map/ppermute | solution.py:414
  6.0 0.7 %copy-start.6 = (s32[256]{0:T(256)S(1)}, s32[256]{0:T(256)}, u32[]{:S(2)}) copy-start(s32[256]{0:T(256)} %param.9) | copy-start | bytes 3076
  6.7 1.0 %copy-start.3 = (f32[7,16,128]{2,1,0:T(8,128)S(1)}, f32[7,16,128]{2,1,0:T(8,128)}, u32[]{:S(2)}) copy-start(f32[7,16,128]{2,1,0:T(8,128)} %get-tuple-element.27.low_ref) | copy-start | bytes 172036
  6.7 1.0 %copy-start.4 = (f32[7,16,128]{2,1,0:T(8,128)S(1)}, f32[7,16,128]{2,1,0:T(8,128)}, u32[]{:S(2)}) copy-start(f32[7,16,128]{2,1,0:T(8,128)} %get-tuple-element.28.high_ref) | copy-start | bytes 172036
  8.3 6.3 %collective-permute-start.4 = (f32[16,384]{1,0:T(8,128)S(1)}, f32[16,384]{1,0:T(8,128)S(1)}, u32[]{:S(2)}, u32[]{:S(2)}) collective-permute-start(f32[16,384]{1,0:T(8,128)S(1)} %get-tuple-element.37.own_ref), channel_id=1, source_target_pairs={{0,24},{8,16},{16,8},{24,0},{1,25},{9,17},{17,9},{25,1},{2,26},{10... | collective-permute-start | bytes 73736 | tf_op jit(solution)/shard_map/ppermute | solution.py:367
  12.6 4.7 %collective-permute-start.3 = (f32[16,384]{1,0:T(8,128)S(1)}, f32[16,384]{1,0:T(8,128)S(1)}, u32[]{:S(2)}, u32[]{:S(2)}) collective-permute-start(f32[16,384]{1,0:T(8,128)S(1)} %get-tuple-element.37.own_ref), channel_id=1, source_target_pairs={{0,16},{8,24},{16,0},{24,8},{1,17},{9,25},{17,1},{25,9},{2,18},{10... | collective-permute-start | bytes 73736 | tf_op jit(solution)/shard_map/ppermute | solution.py:367
  12.6 4.7 %collective-permute-start.2 = (f32[16,384]{1,0:T(8,128)S(1)}, f32[16,384]{1,0:T(8,128)S(1)}, u32[]{:S(2)}, u32[]{:S(2)}) collective-permute-start(f32[16,384]{1,0:T(8,128)S(1)} %get-tuple-element.37.own_ref), channel_id=1, source_target_pairs={{0,8},{8,0},{16,24},{24,16},{1,9},{9,1},{17,25},{25,17},{2,10},{10... | collective-permute-start | bytes 73736 | tf_op jit(solution)/shard_map/ppermute | solution.py:367
  18.1 5.6 %collective-permute-start.7 = (f32[16,256]{1,0:T(8,128)S(1)}, f32[16,256]{1,0:T(8,128)S(1)}, u32[]{:S(2)}, u32[]{:S(2)}) collective-permute-start(f32[16,256]{1,0:T(8,128)S(1)} %get-tuple-element.42.own_ref), channel_id=1, source_target_pairs={{0,24},{8,16},{16,8},{24,0},{1,25},{9,17},{17,9},{25,1},{2,26},{10... | collective-permute-start | bytes 49160 | tf_op jit(solution)/shard_map/ppermute | solution.py:367
  19.6 4.7 %collective-permute-start.6 = (f32[16,256]{1,0:T(8,128)S(1)}, f32[16,256]{1,0:T(8,128)S(1)}, u32[]{:S(2)}, u32[]{:S(2)}) collective-permute-start(f32[16,256]{1,0:T(8,128)S(1)} %get-tuple-element.42.own_ref), channel_id=1, source_target_pairs={{0,16},{8,24},{16,0},{24,8},{1,17},{9,25},{17,1},{25,9},{2,18},{10... | collective-permute-start | bytes 49160 | tf_op jit(solution)/shard_map/ppermute | solution.py:367
  20.2 4.2 %collective-permute-start.5 = (f32[16,256]{1,0:T(8,128)S(1)}, f32[16,256]{1,0:T(8,128)S(1)}, u32[]{:S(2)}, u32[]{:S(2)}) collective-permute-start(f32[16,256]{1,0:T(8,128)S(1)} %get-tuple-element.42.own_ref), channel_id=1, source_target_pairs={{0,8},{8,0},{16,24},{24,16},{1,9},{9,1},{17,25},{25,17},{2,10},{10... | collective-permute-start | bytes 49160 | tf_op jit(solution)/shard_map/ppermute | solution.py:367
  24.4 1.2 %collective-permute-start.8 = (f32[8,128]{1,0:T(8,128)S(1)}, f32[8,128]{1,0:T(8,128)S(1)}, u32[]{:S(2)}, u32[]{:S(2)}) collective-permute-start(f32[8,128]{1,0:T(8,128)S(1)} %get-tuple-element.44), channel_id=1, source_target_pairs={{0,1},{1,0},{2,3},{3,2},{4,5},{5,4},{6,7},{7,6},{8,9},{9,8},{10,11... | collective-permute-start | bytes 12296 | tf_op jit(solution)/shard_map/ppermute | solution.py:371
  25.7 3.9 %collective-permute-start.11 = (f32[8,128]{1,0:T(8,128)S(1)}, f32[8,128]{1,0:T(8,128)S(1)}, u32[]{:S(2)}, u32[]{:S(2)}) collective-permute-start(f32[8,128]{1,0:T(8,128)S(1)} %add.3.own_ref), channel_id=1, source_target_pairs={{0,7},{1,6},{2,5},{3,4},{4,3},{5,2},{6,1},{7,0},{8,15},{9,14},{10,... | collective-permute-start | bytes 12296 | tf_op jit(solution)/shard_map/ppermute | solution.py:371
  27.2 3.0 %collective-permute-start.10 = (f32[8,128]{1,0:T(8,128)S(1)}, f32[8,128]{1,0:T(8,128)S(1)}, u32[]{:S(2)}, u32[]{:S(2)}) collective-permute-start(f32[8,128]{1,0:T(8,128)S(1)} %add.3.own_ref), channel_id=1, source_target_pairs={{0,5},{1,4},{2,7},{3,6},{4,1},{5,0},{6,3},{7,2},{8,13},{9,12},{10,... | collective-permute-start | bytes 12296 | tf_op jit(solution)/shard_map/ppermute | solution.py:371
  27.7 3.0 %collective-permute-start.9 = (f32[8,128]{1,0:T(8,128)S(1)}, f32[8,128]{1,0:T(8,128)S(1)}, u32[]{:S(2)}, u32[]{:S(2)}) collective-permute-start(f32[8,128]{1,0:T(8,128)S(1)} %add.3.own_ref), channel_id=1, source_target_pairs={{0,3},{1,2},{2,1},{3,0},{4,7},{5,6},{6,5},{7,4},{8,11},{9,10},{10,... | collective-permute-start | bytes 12296 | tf_op jit(solution)/shard_map/ppermute | solution.py:371
